TPU v7x, 512 devices: a whole 4x8x8 slice. The times are simulated.
512 devices in a mesh: src: 32 (over y_hi, z, core), cand: 16 (over x, y_lo).
Axes of the slice: x: 4, y: 8 (y_hi: 2, y_lo: 4; y = y_hi * 4 + y_lo), z: 8, core: 2. Of those that a mesh axis runs over, the one named last changes fastest.
Arguments:
- layer_input: bfloat16 [512, 128, 1024], P(('src', 'cand')), parts along dimension 0, may hold values from -16 to 16
- token_ids: int32 [512, 128], P(('src', 'cand')), parts along dimension 0, may hold values from 0 to 50264
- lengths: int32 [512], P(('src', 'cand')), parts along dimension 0, may hold values from 32 to 128
- idf_table: float32 [1608480], P('src'), parts along dimension 0, may hold values from 1 to 12
- query_weight: bfloat16 [1024, 1024], P('cand'), may hold values from -0.1875 to 0.1875
- key_weight: bfloat16 [1024, 1024], P('cand'), may hold values from -0.1875 to 0.1875
- value_weight: bfloat16 [1024, 1024], P('cand'), may hold values from -0.1875 to 0.1875
- output_weight: bfloat16 [1024, 1024], P('cand'), may hold values from -0.1875 to 0.1875
Outputs:
- embedded: bfloat16 [512, 128, 1024], P(('src', 'cand')), parts along dimension 0
- pair_utility: float32 [512, 16], P(('src', 'cand')), parts along dimension 0
- expected_utility: float32 [512], P(('src', 'cand')), parts along dimension 0
There are 32 independent parts, one for each index of `src`. A program takes and returns all parts, laid end to end along the dimension named above; an argument that names none is the same for every part. Nothing has to cross between parts.
All inputs are finite; a program needn't handle non-finite values.
Results may differ from a plain program's by a relative error of at most 0.0086.
Values may be sent and summed in bfloat16 or wider, within the bound.
No kernel may reach another device: no remote copies, remote signals or barrier semaphores. Data moves between devices by JAX's collectives and lax.ppermute only.
A program may use at most 64 MiB of HBM per device.

v0:
```python
import math

import jax
import jax.numpy as jnp
from jax import lax
from jax.sharding import PartitionSpec as P

HEAD = 64


def side_by_side(arrays, axis, dim, along):
    ends, at = ([], 0)
    for a in arrays[:-1]:
        at += a.shape[along]
        ends.append(at)
    both = jnp.concatenate(arrays, axis=along)
    return tuple(jnp.split(lax.all_gather(both, axis, axis=dim, tiled=True), ends, axis=along))


def joined_along(tiles, dim):
    lengths = list(tiles.shape[1:])
    lengths[dim] *= tiles.shape[0]
    return jnp.moveaxis(tiles, 0, dim).reshape(lengths)


def sent_to_all(x, axis):
    copies = jnp.broadcast_to(x, (lax.axis_size(axis), *x.shape))
    return lax.all_to_all(copies, axis, split_axis=0, concat_axis=0, tiled=True)


def collect(x, axis, dim):
    return joined_along(sent_to_all(x, axis), dim)


def block_utility(own_vectors, own_weight, far_vectors, far_weight):
    own_count, length, width = own_vectors.shape
    far_count = far_vectors.shape[0]
    similar = lax.dot_general(
        own_vectors.reshape(own_count * length, width),
        far_vectors.reshape(far_count * length, width),
        (((1,), (1,)), ((), ())),
        preferred_element_type=jnp.float32,
    )
    similar = similar.reshape(own_count, length, far_count, length)
    own_usable = own_weight > 0
    far_usable = far_weight > 0
    best_far = jnp.max(jnp.where(far_usable[None, None, :, :], similar, -4.0), axis=3)
    best_own = jnp.max(jnp.where(own_usable[:, :, None, None], similar, -4.0), axis=1)
    own_float = own_weight.astype(jnp.float32)
    far_float = far_weight.astype(jnp.float32)
    forward = jnp.einsum("il,ilj->ij", own_float, best_far, precision=lax.Precision.HIGHEST)
    forward = forward / jnp.sum(own_float, axis=1)[:, None]
    backward = jnp.einsum("jm,ijm->ij", far_float, best_own, precision=lax.Precision.HIGHEST)
    backward = backward / jnp.sum(far_float, axis=1)[None, :]
    return 0.5 * (forward + backward)


def shards(
    layer_input,
    token_ids,
    lengths,
    idf_table,
    query_weight,
    key_weight,
    value_weight,
    output_weight,
):
    local_cands, length, width = layer_input.shape
    cycle_size = lax.axis_size("cand")
    all_cands = local_cands * cycle_size
    head_size = HEAD
    head_count = width // head_size
    flat = layer_input.reshape(local_cands * length, width)
    pieces = side_by_side((query_weight, key_weight, value_weight), "cand", 0, 1)
    columns = flat
    queries, key_rows, value_rows = tuple(
        (jnp.dot(columns, piece, preferred_element_type=jnp.float32) for piece in pieces)
    )
    queries = queries.astype(jnp.bfloat16).reshape(local_cands, length, head_count, head_size)
    key_rows = key_rows.astype(jnp.bfloat16).reshape(local_cands, length, head_count, head_size)
    value_rows = value_rows.astype(jnp.bfloat16).reshape(local_cands, length, head_count, head_size)
    positions = jnp.arange(length, dtype=jnp.int32)
    valid = positions[None, :] < lengths[:, None]
    scale = 1.0 / math.sqrt(head_size)
    scores = (
        jnp.einsum("clhe,cmhe->chlm", queries, key_rows, preferred_element_type=jnp.float32) * scale
    )
    scores = jnp.where(valid[:, None, None, :], scores, -1000000000.0)
    highest = jnp.max(scores, axis=-1, keepdims=True)
    expo = jnp.exp(scores - highest)
    probs = (expo / jnp.sum(expo, axis=-1, keepdims=True)).astype(jnp.bfloat16)
    context = jnp.einsum("chlm,cmhe->clhe", probs, value_rows, preferred_element_type=jnp.float32)
    context = context.astype(jnp.bfloat16).reshape(local_cands * length, width)
    columns = context
    mixed = jnp.dot(
        columns, collect(output_weight, "cand", 0), preferred_element_type=jnp.float32
    ) + flat.astype(jnp.float32)
    centred = mixed - jnp.mean(mixed, axis=-1, keepdims=True)
    squares = jnp.sum(centred * centred, axis=-1, keepdims=True)
    embedded = (
        (centred / jnp.sqrt(squares + 0.001))
        .astype(jnp.bfloat16)
        .reshape(local_cands, length, width)
    )
    token_weight = (jnp.take(idf_table, token_ids, axis=0) * valid.astype(jnp.float32)).astype(
        jnp.bfloat16
    )
    myself = lax.axis_index("cand")
    piece = (
        lax.all_gather(embedded, "cand", axis=0, tiled=True),
        lax.all_gather(token_weight, "cand", axis=0, tiled=True),
    )
    utility = block_utility(embedded, token_weight, piece[0], piece[1])
    blocks = utility.reshape(local_cands, cycle_size, local_cands)
    own_part = lax.dynamic_slice(blocks, (0, myself, 0), (local_cands, 1, local_cands))[:, 0, :]
    diagonal = jnp.diagonal(own_part)
    expected_utility = (jnp.sum(utility, axis=1) - diagonal) / (all_cands - 1)
    return (embedded, utility, expected_utility)


def solution(mesh):
    in_specs = (
        P(("src", "cand"), None, None),
        P(("src", "cand"), None),
        P(("src", "cand")),
        P("src"),
        P("cand", None),
        P("cand", None),
        P("cand", None),
        P("cand", None),
    )
    out_specs = (P(("src", "cand"), None, None), P(("src", "cand"), None), P(("src", "cand")))
    return jax.shard_map(shards, mesh=mesh, in_specs=in_specs, out_specs=out_specs, check_vma=False)
```

profile of v0, /device:TPU:448, one launch (start us, length us, event | category | flops | bytes accessed | tf_op | source)
XLA Modules:
  0.0 324.0 jit_solution(17611935127552149624)
XLA Ops:
  7.2 1.9 pad_maximum_fusion
  9.2 2.5 broadcast_in_dim.62
  11.7 7.4 %all-to-all-start = ((bf16[16,64,1024]{2,1,0:T(8,128)(2,1)}), bf16[16,64,1024]{2,1,0:T(8,128)(2,1)S(1)}, u32[]{:S(2)}, u32[]{:S(2)}) async-start(bf16[16,64,1024]{2,1,0:T(8,128)(2,1)} %broadcast_in_dim.62), calls=%async_computation | async-start | bytes 4194304 | tf_op jit(solution)/shard_map/all_to_all | solution.py:28
  19.8 173.5 %all-gather.5.cloned.1.call-done = bf16[1024,3072]{1,0:T(8,128)(2,1)} async-done(((bf16[64,3072]{1,0:T(8,128)(2,1)}), bf16[1024,3072]{1,0:T(8,128)(2,1)}) %all-gather.5.cloned.1.call-update) | async-done | bytes 6291472 | tf_op jit(solution)/shard_map/all_gather | solution.py:17
  193.3 2.4 fusion.13
  195.7 2.4 fusion.16
  198.0 0.5 fusion.34
  198.6 1.4 fusion.9
  200.0 2.4 fusion.10
  202.4 2.1 convolution_convert_fusion
  204.5 0.5 fusion.35
  205.1 0.2 multiply_reduce_fusion
  205.3 0.8 divide_convert_fusion.1
  206.2 1.1 gather_fusion
  207.4 0.6 convert_reduce_fusion.1
  208.0 39.7 %all-gather.1 = bf16[16,1,128]{2,1,0:T(2,128)(2,1)S(1)} all-gather(bf16[1,1,128]{2,1,0:T(2,128)(2,1)S(1)} %bitcast.84), channel_id=1, replica_groups=mesh['src'=32,'cand'=16] {'cand'}, dimensions={0}, use_global_device_ids=true | all-gather | bytes 4352 | tf_op jit(solution)/shard_map/all_gather | solution.py:111
  247.7 0.8 fusion.48
  248.5 59.6 %all-gather.7.cloned.1.call-done = bf16[2048,1024]{1,0:T(8,128)(2,1)} async-done(((bf16[128,1024]{1,0:T(8,128)(2,1)}), bf16[2048,1024]{1,0:T(8,128)(2,1)}) %all-gather.7.cloned.1.call-update) | async-done | bytes 4194320 | tf_op jit(solution)/shard_map/all_gather | solution.py:110
  308.1 3.8 %select_reduce_fusion = (f32[2048]{0:T(1024)S(1)}, f32[128,2048]{1,0:T(8,128)S(1)}) fusion(pred[128]{0:T(512)(128)(4,1)S(1)} %compare_bitcast_fusion, bf16[128,1024]{1,0:T(8,128)(2,1)} %divide_convert_fusion.1, bf16[2048,1024]{1,0:T(8,128)(2,1)} %all-gather.7.cloned.1.call-done), kind=kOutput, calls=%fused_computation.23 | convolution fusion | flops 537393152 | bytes 5513344 | tf_op jit(solution)/shard_map/dot_general | solution.py:38
  311.9 0.1 convert_reduce_fusion
  312.0 0.2 copy.20
  312.2 0.3 fusion.22
  312.6 1.4 fusion.36
  314.0 0.7 gather.9
  (20 shorter events, 0.2 us)
Async XLA Ops:
  7.2 199.0 %copy-start = (f32[50265]{0:T(1024)S(1)}, f32[50265]{0:T(1024)}, u32[]{:S(2)}) copy-start(f32[50265]{0:T(1024)} %param.11) | copy-start | bytes 603184
  7.2 186.1 %copy-start.1 = (bf16[1,128,1024]{2,1,0:T(8,128)(2,1)S(1)}, bf16[1,128,1024]{2,1,0:T(8,128)(2,1)}, u32[]{:S(2)}) copy-start(bf16[1,128,1024]{2,1,0:T(8,128)(2,1)} %param.8) | copy-start | bytes 786436
  7.2 186.1 %all-gather.5.cloned.1.call-start = ((), (), s32[]{:S(2)}) async-start(), calls=%async_computation.1 | async-start | bytes 6684672 | tf_op jit(solution)/shard_map/all_gather | solution.py:17
  11.7 192.8 %all-to-all-start = ((bf16[16,64,1024]{2,1,0:T(8,128)(2,1)}), bf16[16,64,1024]{2,1,0:T(8,128)(2,1)S(1)}, u32[]{:S(2)}, u32[]{:S(2)}) async-start(bf16[16,64,1024]{2,1,0:T(8,128)(2,1)} %broadcast_in_dim.62), calls=%async_computation | async-start | bytes 4194304 | tf_op jit(solution)/shard_map/all_to_all | solution.py:28
  19.1 289.0 %all-gather.7.cloned.1.call-start = ((), (), s32[]{:S(2)}) async-start(), calls=%async_computation.2 | async-start | bytes 4456448 | tf_op jit(solution)/shard_map/all_gather | solution.py:110
  202.4 3.8 %copy-start.3 = (s32[1,128]{1,0:T(1,128)S(1)}, s32[1,128]{1,0:T(1,128)}, u32[]{:S(2)}) copy-start(s32[1,128]{1,0:T(1,128)} %param.9) | copy-start | bytes 1540
  314.0 2.0 copy-start.2
Sparse Core Ops, SparseCore 0:
  10.1 183.1 all-gather.4
  206.3 101.8 all-gather.6
where the time goes:
time: 330 us; the launch traced here: 324 us
  waiting for transfers between devices  233 us (71%)
  blocking collectives  39.7 us (12%)
  between operations  17.3 us (5%)
  matrix products  16.9 us (5%)
  starting transfers between devices  7.52 us (2%)
  other arithmetic  4.88 us (1%)
  local copies, waits for them, and re-layouts  4.53 us (1%)
    all_gather x1, waiting for transfers between devices, side_by_side(): lax.all_gather(both, axis, axis=dim, tiled=True)  173 us
    all_gather x1, waiting for transfers between devices, shards(): lax.all_gather(embedded, 'cand', axis=0, tiled=True)  59.6 us
    all_gather x1, blocking collectives, shards(): lax.all_gather(token_weight, 'cand', axis=0, tiled=True)  39.7 us
    all_to_all x1, starting transfers between devices, sent_to_all(): return lax.all_to_all(copies, axis, split_axis=0, concat_axis=0, tiled=True)  7.44 us
    dot_general x3, matrix products, shards(): jnp.dot(columns, piece, preferred_element_type=jnp.float32)  7.08 us
  transfers between devices with their start and end apart: 3, of which 2 were waited for; matrix products, arithmetic and copies ran while one was open for 5% of the time, Pallas kernels for 0%

commit v1 on v0

v1 whole, which is shorter than its diff:
```python
import functools

import jax
import jax.numpy as jnp
import numpy as np
from jax import lax
from jax.experimental import pallas as pl
from jax.experimental.pallas import tpu as pltpu
from jax.sharding import Mesh, PartitionSpec as P

HEAD = 64
LANES = 128
PAD = 16
VMEM = pl.BlockSpec(memory_space=pltpu.VMEM)
SMEM = pl.BlockSpec(memory_space=pltpu.SMEM)


def params():
    return pltpu.CompilerParams(vmem_limit_bytes=40 * 1024 * 1024)


def prepare_kernel(lengths_ref, x_ref, q_ref, k_ref, v_ref, chunk_ref, ext_ref):
    core = lax.axis_index("core")
    rows = x_ref.shape[1]
    for block in range(4):
        at = pl.multiple_of(block * 2 * LANES + core * LANES, LANES)
        for n, ref in enumerate((q_ref, k_ref, v_ref)):
            piece = ref[:, pl.ds(at, LANES)]
            for y in range(4):
                chunk_ref[block * 4 + y, :, n * LANES : (n + 1) * LANES] = piece
    ext_ref[:rows, :] = x_ref[0]
    length = lengths_ref[0].astype(jnp.float32)
    ext_ref[rows:, :] = jnp.full((PAD, ext_ref.shape[1]), length, jnp.float32).astype(jnp.bfloat16)


def attend_kernel(x0, x1, x2, x3, wa_ref, wb_ref, o0, o1, o2, o3, part_ref, wo_ref):
    core = lax.axis_index("core")
    x = lax.axis_index("x")
    y = lax.axis_index("y")
    length = LANES
    for k, ref in enumerate((o0, o1, o2, o3)):
        at = pl.multiple_of(lax.rem(y + k, 4) * HEAD, HEAD)
        wo_ref[pl.ds(at, HEAD), :] = ref[...]
    xs = (x0, x1, x2, x3)
    tokens = jnp.concatenate([r[:length, :] for r in xs], axis=0)
    lane = lax.broadcasted_iota(jnp.int32, (length, LANES), 1)
    first = lane < HEAD
    lane2 = lax.broadcasted_iota(jnp.int32, (2 * length, length), 1).astype(jnp.float32)
    contexts = []
    for w_ref in (wa_ref, wb_ref):
        qkv = jnp.dot(tokens, w_ref[...], preferred_element_type=jnp.float32).astype(jnp.bfloat16)
        own = []
        for c in range(4):
            rows = slice(c * length, (c + 1) * length)
            q = qkv[rows, :LANES]
            key = qkv[rows, LANES : 2 * LANES]
            v = qkv[rows, 2 * LANES :]
            zero = jnp.zeros_like(q)
            both = jnp.concatenate([jnp.where(first, q, zero), jnp.where(first, zero, q)], axis=0)
            scores = lax.dot_general(
                both, key, (((1,), (1,)), ((), ())), preferred_element_type=jnp.float32
            ) * (HEAD ** -0.5)
            used = xs[c][length : length + 1, :length].astype(jnp.float32)
            scores = jnp.where(lane2 < used, scores, -1e9)
            expo = jnp.exp(scores - jnp.max(scores, axis=1, keepdims=True))
            probs = (expo / jnp.sum(expo, axis=1, keepdims=True)).astype(jnp.bfloat16)
            ctx = jnp.dot(probs, v, preferred_element_type=jnp.float32)
            own.append(jnp.where(first, ctx[:length], ctx[length:]).astype(jnp.bfloat16))
        contexts.append(jnp.concatenate(own, axis=0))
    wo_a = wo_ref[pl.ds(pl.multiple_of(core * LANES, LANES), LANES), :]
    wo_b = wo_ref[pl.ds(pl.multiple_of((1 - core) * LANES, LANES), LANES), :]
    part = jnp.dot(contexts[0], wo_a, preferred_element_type=jnp.float32)
    part = part + jnp.dot(contexts[1], wo_b, preferred_element_type=jnp.float32)
    for c in range(4):
        part_ref[lax.rem(x + c, 4)] = part[c * length : (c + 1) * length].astype(jnp.bfloat16)


def embed_kernel(weight_ref, parts_ref, x_ref, out_ref, ext_ref, row_ref):
    rows, width = x_ref.shape[1:]
    mixed = x_ref[0].astype(jnp.float32)
    for n in range(4):
        mixed = mixed + parts_ref[n].astype(jnp.float32)
    centred = mixed - jnp.mean(mixed, axis=1, keepdims=True)
    squares = jnp.sum(centred * centred, axis=1, keepdims=True)
    embedded = (centred / jnp.sqrt(squares + 0.001)).astype(jnp.bfloat16)
    out_ref[0] = embedded
    tail = jnp.concatenate(
        [jnp.broadcast_to(weight_ref[...].astype(jnp.float32), (PAD, LANES)), jnp.zeros((PAD, width - LANES), jnp.float32)],
        axis=1,
    ).astype(jnp.bfloat16)
    ext_ref[:rows, :] = embedded
    ext_ref[rows:, :] = tail
    for n in range(4):
        row_ref[n, :rows, :] = embedded
        row_ref[n, rows:, :] = tail


def pairs_kernel(row_ref, near_ref, far_ref, own_ref, out_ref):
    x = lax.axis_index("x")
    y = lax.axis_index("y")
    n = LANES
    me = x * 4 + y
    near = x * 4 + lax.rem(y + 1, 4)
    far = x * 4 + lax.rem(y + 2, 4)
    has_far = jnp.logical_or(y == 0, y == 3)
    rows = jnp.concatenate([row_ref[c, :n, :] for c in range(4)], axis=0)
    cols = jnp.concatenate([near_ref[:n, :], far_ref[:n, :], own_ref[:n, :]], axis=0)
    similar = lax.dot_general(rows, cols, (((1,), (1,)), ((), ())), preferred_element_type=jnp.float32)
    col_weight = [r[n : n + 1, :n].astype(jnp.float32) for r in (near_ref, far_ref, own_ref)]
    row_weight = [row_ref[c, n : n + 1, :n].astype(jnp.float32) for c in range(4)]
    down = [jnp.transpose(jnp.broadcast_to(w, (n, n))) for w in row_weight]
    row_sum = [jnp.sum(w, axis=1, keepdims=True) for w in row_weight]
    col_sum = [jnp.sum(w, axis=1, keepdims=True) for w in col_weight]
    col_sum[1] = jnp.where(has_far, col_sum[1], 1.0)
    dest = lax.broadcasted_iota(jnp.int32, (16, LANES), 0)
    lane = lax.broadcasted_iota(jnp.int32, (16, LANES), 1)
    total = jnp.zeros((16, LANES), jnp.float32)
    for j, other in enumerate((near, far, me)):
        w_col = col_weight[j]
        for c in range(4):
            block = similar[c * n : (c + 1) * n, j * n : (j + 1) * n]
            best_col = jnp.max(jnp.where(w_col > 0, block, -4.0), axis=1, keepdims=True)
            best_row = jnp.max(jnp.where(down[c] > 0, block, -4.0), axis=0, keepdims=True)
            forward = jnp.sum(best_col * down[c][:, :1], axis=0, keepdims=True) / row_sum[c]
            backward = jnp.sum(best_row * w_col, axis=1, keepdims=True) / col_sum[j]
            utility = 0.5 * (forward + backward)
            mate = c * 4 + y
            here = jnp.logical_and(dest == other, lane == mate)
            if j < 2:
                here = jnp.logical_or(here, jnp.logical_and(dest == mate, lane == other))
            if j == 1:
                here = jnp.logical_and(here, has_far)
            total = total + jnp.where(here, jnp.broadcast_to(utility, total.shape), 0.0)
    for p in range(16):
        out_ref[p] = jnp.broadcast_to(total[p : p + 1], (8, LANES))


def finish_kernel(got_ref, pair_ref, mean_ref):
    me = lax.axis_index("x") * 4 + lax.axis_index("y")
    total = got_ref[0]
    for p in range(1, 16):
        total = total + got_ref[p]
    lane = lax.broadcasted_iota(jnp.int32, total.shape, 1)
    pair_ref[...] = total[:1, :16]
    rest = jnp.where(jnp.logical_and(lane < 16, lane != me), total, 0.0)
    mean_ref[...] = (jnp.sum(rest, axis=1, keepdims=True) / 15)[:1]


def call(kernel, ins, outs, *args, scratch=()):
    return pl.pallas_call(
        kernel,
        in_specs=ins,
        out_specs=tuple(VMEM for _ in outs) if len(outs) > 1 else VMEM,
        out_shape=outs if len(outs) > 1 else outs[0],
        scratch_shapes=list(scratch),
        compiler_params=params(),
    )(*args)


def shift(size, by):
    return [((i + by) % size, i) for i in range(size)]


def shards(layer_input, token_ids, lengths, idf_table, query_weight, key_weight, value_weight, output_weight):
    _, length, width = layer_input.shape
    depth = query_weight.shape[0]
    bf16, f32 = jnp.bfloat16, jnp.float32
    chunks, extended = call(
        prepare_kernel,
        [SMEM] + [VMEM] * 4,
        (
            jax.ShapeDtypeStruct((16, depth, 3 * LANES), bf16),
            jax.ShapeDtypeStruct((length + PAD, width), bf16),
        ),
        lengths, layer_input, query_weight, key_weight, value_weight,
    )
    near_half = lax.all_to_all(chunks, ("x", "y"), split_axis=0, concat_axis=0, tiled=True)
    others = [lax.ppermute(extended, "x", shift(4, k)) for k in (1, 2, 3)]
    blocks = [lax.ppermute(output_weight, ("yh", "y"), shift(8, k)) for k in (1, 2, 7)]
    far_half = lax.ppermute(near_half, "core", [(0, 1), (1, 0)])
    parts = call(
        attend_kernel,
        [VMEM] * 10,
        (jax.ShapeDtypeStruct((4, length, width), bf16),),
        extended, *others,
        near_half.reshape(width, 3 * LANES), far_half.reshape(width, 3 * LANES),
        output_weight, *blocks,
        scratch=(pltpu.VMEM((4 * HEAD, width), bf16),),
    )
    parts = lax.all_to_all(parts, "x", split_axis=0, concat_axis=0, tiled=True)
    positions = jnp.arange(length, dtype=jnp.int32)
    valid = positions[None, :] < lengths[:, None]
    token_weight = (jnp.take(idf_table, token_ids, axis=0) * valid.astype(f32)).astype(bf16)
    embedded, own, row = call(
        embed_kernel,
        [VMEM] * 3,
        (
            jax.ShapeDtypeStruct((1, length, width), bf16),
            jax.ShapeDtypeStruct((length + PAD, width), bf16),
            jax.ShapeDtypeStruct((4, length + PAD, width), bf16),
        ),
        token_weight, parts, layer_input,
    )
    near = lax.ppermute(own, "y", shift(4, 1))
    far = lax.ppermute(own, "y", [(2, 0), (1, 3)])
    row = lax.all_to_all(row, "x", split_axis=0, concat_axis=0, tiled=True)
    known = call(
        pairs_kernel, [VMEM] * 4, (jax.ShapeDtypeStruct((16, 8, LANES), f32),), row, near, far, own
    )
    known = lax.all_to_all(known, ("x", "y"), split_axis=0, concat_axis=0, tiled=True)
    pair, mean = call(
        finish_kernel,
        [VMEM],
        (jax.ShapeDtypeStruct((1, 16), f32), jax.ShapeDtypeStruct((1, 1), f32)),
        known,
    )
    return embedded, pair, mean.reshape(1)


def solution(mesh):
    fine = Mesh(np.asarray(mesh.devices).reshape(2, 8, 2, 4, 4), ("yh", "z", "core", "x", "y"))
    src = ("yh", "z", "core")
    cand = ("x", "y")
    in_specs = (
        P(src + cand, None, None),
        P(src + cand, None),
        P(src + cand),
        P(src),
        P(cand, None),
        P(cand, None),
        P(cand, None),
        P(cand, None),
    )
    out_specs = (P(src + cand, None, None), P(src + cand, None), P(src + cand))
    return jax.shard_map(shards, mesh=fine, in_specs=in_specs, out_specs=out_specs, check_vma=False)
```

time: 330 us -> 119 us (0.36); the launches traced: 324 us -> 118 us
  waiting for transfers between devices: 233 us -> 30 us
  starting transfers between devices: 7.52 us -> 32.7 us
  matrix products: 16.9 us -> 0 us
  between operations: 17.3 us -> 1.52 us
  Pallas kernels: 0 us -> 6.69 us
  other arithmetic: 4.88 us -> 0.02 us
    all_gather x2 -> x0, waiting for transfers between devices: 233 us -> none  [the longest x1 173 us: side_by_side(): lax.all_gather(both, axis, axis=dim, tiled=True)]
    all_to_all x0 -> x2, blocking collectives: none -> 42.7 us  [the longest x1 29.4 us: shards(): lax.all_to_all(chunks, ('x', 'y'), split_axis=0, concat_axis=0, tiled=True)]
    all_gather x1 -> x0, blocking collectives: 39.7 us -> none  [shards(): lax.all_gather(token_weight, 'cand', axis=0, tiled=True)]
    ppermute x0 -> x9, starting transfers between devices: none -> 25.5 us  [the longest x3 9.7 us: shards(): others = [lax.ppermute(extended, 'x', shift(4, k)) for k in (1, 2, 3)]]
    ppermute x0 -> x9, waiting for transfers between devices: none -> 18.3 us  [the longest x3 8.79 us: shards(): lax.ppermute(output_weight, ('yh', 'y'), shift(8, k))]
    dot_general x8 -> x0, matrix products: 16.4 us -> none  [the longest x3 7.08 us: shards(): jnp.dot(columns, piece, preferred_element_type=jnp.float32)]
    all_to_all x1 -> x2, waiting for transfers between devices: 0.01 us -> 11.7 us  [the longest x1 11.7 us: shards(): parts = lax.all_to_all(parts, 'x', split_axis=0, concat_axis=0, tiled=True)]
    pallas_call x0 -> x5, Pallas kernels: none -> 6.69 us  [call(): pl.pallas_call(kernel, in_specs=ins, out_specs=tuple((VMEM for _ in outs)...]
  transfers between devices with their start and end apart: 3 -> 11, of which waited for: 2 -> 5; matrix products, arithmetic and copies ran while one was open for 5% -> 1% of each run, Pallas kernels for 0% -> 0%
where the time goes in v1:
time: 119 us; the launch traced here: 118 us
  blocking collectives  42.7 us (36%)
  starting transfers between devices  32.7 us (27%)
  waiting for transfers between devices  30 us (25%)
  Pallas kernels  6.69 us (6%)
  local copies, waits for them, and re-layouts  4.83 us (4%)
  between operations  1.52 us (1%)
    all_to_all x1, blocking collectives, shards(): lax.all_to_all(chunks, ('x', 'y'), split_axis=0, concat_axis=0, tiled=True)  29.4 us
    all_to_all x1, blocking collectives, shards(): lax.all_to_all(known, ('x', 'y'), split_axis=0, concat_axis=0, tiled=True)  13.4 us
    all_to_all x1, waiting for transfers between devices, shards(): parts = lax.all_to_all(parts, 'x', split_axis=0, concat_axis=0, tiled=True)  11.7 us
    ppermute x3, starting transfers between devices, shards(): others = [lax.ppermute(extended, 'x', shift(4, k)) for k in (1, 2, 3)]  9.7 us
    ppermute x3, starting transfers between devices, shards(): lax.ppermute(output_weight, ('yh', 'y'), shift(8, k))  9.3 us
    ppermute x3, waiting for transfers between devices, shards(): lax.ppermute(output_weight, ('yh', 'y'), shift(8, k))  8.79 us
    pallas_call x5, Pallas kernels, call(): pl.pallas_call(kernel, in_specs=ins, out_specs=tuple((VMEM for _ in outs)...  6.69 us
    ppermute x1, waiting for transfers between devices, shards(): far = lax.ppermute(own, 'y', [(2, 0), (1, 3)])  6.53 us
  transfers between devices with their start and end apart: 11, of which 5 were waited for; matrix products, arithmetic and copies ran while one was open for 1% of the time, Pallas kernels for 0%

profile of v1, /device:TPU:448, one launch (start us, length us, event | category | flops | bytes accessed | tf_op | source)
XLA Modules:
  0.0 118.5 jit_solution(16779617843151860250)
XLA Ops:
  1.3 0.9 copy-done.1
  2.3 0.9 copy-done.4
  5.1 29.4 %all_to_all.20 = bf16[16,64,384]{2,1,0:T(8,128)(2,1)S(1)} all-to-all(bf16[16,64,384]{2,1,0:T(8,128)(2,1)S(1)} %get-tuple-element.11), channel_id=1, replica_groups=mesh['yh'=2,'z'=8,'core'=2,'x'=4,'y'=4] {'x','y'}, dimensions={0} | all-to-all | bytes 1572864 | tf_op jit(solution)/shard_map/all_to_all | solution.py:177
  34.5 1.9 %collective-permute-start.3 = (bf16[16,64,384]{2,1,0:T(8,128)(2,1)S(1)}, bf16[16,64,384]{2,1,0:T(8,128)(2,1)S(1)}, u32[]{:S(2)}, u32[]{:S(2)}) collective-permute-start(bf16[16,64,384]{2,1,0:T(8,128)(2,1)S(1)} %all_to_all.20), channel_id=1, source_target_pairs={{0,16},{16,0},{1,17},{17,1},{2,18},{18,2},{3,19},{19,3},{4,20},{20... | collective-permute-start | bytes 2359304 | tf_op jit(solution)/shard_map/ppermute | solution.py:180
  36.4 3.2 %collective-permute-start.5 = (bf16[64,1024]{1,0:T(8,128)(2,1)S(1)}, bf16[64,1024]{1,0:T(8,128)(2,1)S(1)}, u32[]{:S(2)}, u32[]{:S(2)}) collective-permute-start(bf16[64,1024]{1,0:T(8,128)(2,1)S(1)} %copy-done.3), channel_id=1, source_target_pairs={{2,0},{3,1},{256,2},{257,3},{258,256},{259,257},{0,258},{1,259},{6... | collective-permute-start | bytes 393224 | tf_op jit(solution)/shard_map/ppermute | solution.py:179
  39.6 2.5 %collective-permute-start.2 = (bf16[144,1024]{1,0:T(8,128)(2,1)S(1)}, bf16[144,1024]{1,0:T(8,128)(2,1)S(1)}, u32[]{:S(2)}, u32[]{:S(2)}) collective-permute-start(bf16[144,1024]{1,0:T(8,128)(2,1)S(1)} %get-tuple-element.10.x0), channel_id=1, source_target_pairs={{12,0},{0,4},{4,8},{8,12},{13,1},{1,5},{5,9},{9,13},{14,2},{2,6},{... | collective-permute-start | bytes 884744 | tf_op jit(solution)/shard_map/ppermute | solution.py:178
  42.1 4.0 %collective-permute-start.1 = (bf16[144,1024]{1,0:T(8,128)(2,1)S(1)}, bf16[144,1024]{1,0:T(8,128)(2,1)S(1)}, u32[]{:S(2)}, u32[]{:S(2)}) collective-permute-start(bf16[144,1024]{1,0:T(8,128)(2,1)S(1)} %get-tuple-element.10.x0), channel_id=1, source_target_pairs={{8,0},{12,4},{0,8},{4,12},{9,1},{13,5},{1,9},{5,13},{10,2},{14,6},... | collective-permute-start | bytes 884744 | tf_op jit(solution)/shard_map/ppermute | solution.py:178
  46.1 3.3 %collective-permute-start = (bf16[144,1024]{1,0:T(8,128)(2,1)S(1)}, bf16[144,1024]{1,0:T(8,128)(2,1)S(1)}, u32[]{:S(2)}, u32[]{:S(2)}) collective-permute-start(bf16[144,1024]{1,0:T(8,128)(2,1)S(1)} %get-tuple-element.10.x0), channel_id=1, source_target_pairs={{4,0},{8,4},{12,8},{0,12},{5,1},{9,5},{13,9},{1,13},{6,2},{10,6},{... | collective-permute-start | bytes 884744 | tf_op jit(solution)/shard_map/ppermute | solution.py:178
  49.3 3.2 %collective-permute-start.4 = (bf16[64,1024]{1,0:T(8,128)(2,1)S(1)}, bf16[64,1024]{1,0:T(8,128)(2,1)S(1)}, u32[]{:S(2)}, u32[]{:S(2)}) collective-permute-start(bf16[64,1024]{1,0:T(8,128)(2,1)S(1)} %copy-done.3), channel_id=1, source_target_pairs={{1,0},{2,1},{3,2},{256,3},{257,256},{258,257},{259,258},{0,259},{5... | collective-permute-start | bytes 393224 | tf_op jit(solution)/shard_map/ppermute | solution.py:179
  52.5 3.7 %collective-permute-done.4.o1 = bf16[64,1024]{1,0:T(8,128)(2,1)S(1)} collective-permute-done((bf16[64,1024]{1,0:T(8,128)(2,1)S(1)}, bf16[64,1024]{1,0:T(8,128)(2,1)S(1)}, u32[]{:S(2)}, u32[]{:S(2)}) %collective-permute-start.4) | collective-permute-done | bytes 131104 | tf_op jit(solution)/shard_map/ppermute | solution.py:179
  56.2 2.9 %collective-permute-start.6 = (bf16[64,1024]{1,0:T(8,128)(2,1)S(1)}, bf16[64,1024]{1,0:T(8,128)(2,1)S(1)}, u32[]{:S(2)}, u32[]{:S(2)}) collective-permute-start(bf16[64,1024]{1,0:T(8,128)(2,1)S(1)} %copy-done.3), channel_id=1, source_target_pairs={{259,0},{0,1},{1,2},{2,3},{3,256},{256,257},{257,258},{258,259},{2... | collective-permute-start | bytes 393224 | tf_op jit(solution)/shard_map/ppermute | solution.py:179
  59.1 5.1 %collective-permute-done.6.o3 = bf16[64,1024]{1,0:T(8,128)(2,1)S(1)} collective-permute-done((bf16[64,1024]{1,0:T(8,128)(2,1)S(1)}, bf16[64,1024]{1,0:T(8,128)(2,1)S(1)}, u32[]{:S(2)}, u32[]{:S(2)}) %collective-permute-start.6) | collective-permute-done | bytes 131104 | tf_op jit(solution)/shard_map/ppermute | solution.py:179
  64.3 3.5 %shard_map.104 = bf16[4,128,1024]{2,1,0:T(8,128)(2,1)} custom-call(bf16[144,1024]{1,0:T(8,128)(2,1)S(1)} %get-tuple-element.10.x0, bf16[144,1024]{1,0:T(8,128)(2,1)S(1)} %collective-permute-done.x1, bf16[144,1024]{1,0:T(8,128)(2,1)S(1)} %collective-permute-done.1.x2, bf16[144,1024]{1,0:T(8,128)(2,1)S(1)} %collective-permute-done.2.x3, ...), custom_call_target="tpu_custom_call" | custom-call | tf_op jit(solution)/shard_map/pallas_call | solution.py:150
  67.8 3.6 %all-to-all-start.1 = ((bf16[4,128,1024]{2,1,0:T(8,128)(2,1)}), bf16[4,128,1024]{2,1,0:T(8,128)(2,1)S(1)}, u32[]{:S(2)}, u32[]{:S(2)}) async-start(bf16[4,128,1024]{2,1,0:T(8,128)(2,1)} %shard_map.104), calls=%async_computation.1 | async-start | bytes 2097152 | tf_op jit(solution)/shard_map/all_to_all | solution.py:190
  71.5 1.1 gather_fusion
  72.7 11.7 %all-to-all-done.1.parts_ref = bf16[4,128,1024]{2,1,0:T(8,128)(2,1)S(1)} async-done(((bf16[4,128,1024]{2,1,0:T(8,128)(2,1)}), bf16[4,128,1024]{2,1,0:T(8,128)(2,1)S(1)}, u32[]{:S(2)}, u32[]{:S(2)}) %all-to-all-start.1) | async-done | bytes 1048608 | tf_op jit(solution)/shard_map/all_to_all | solution.py:190
  84.3 1.5 %shard_map.105 = (bf16[1,128,1024]{2,1,0:T(8,128)(2,1)}, bf16[144,1024]{1,0:T(8,128)(2,1)S(1)}, bf16[4,144,1024]{2,1,0:T(8,128)(2,1)}) custom-call(bf16[1,128]{1,0:T(2,128)(2,1)S(1)} %fusion.weight_ref, bf16[4,128,1024]{2,1,0:T(8,128)(2,1)S(1)} %all-to-all-done.1.parts_ref, bf16[1,128,1024]{2,1,0:T(8,128)(2,1)S(1)} %copy-done.2), custom_call_target="tpu_custom_call" | custom-call | tf_op jit(solution)/shard_map/pallas_call | solution.py:150
  85.8 3.5 %all-to-all-start.2 = ((bf16[4,144,1024]{2,1,0:T(8,128)(2,1)}), bf16[4,144,1024]{2,1,0:T(8,128)(2,1)S(1)}, u32[]{:S(2)}, u32[]{:S(2)}) async-start(bf16[4,144,1024]{2,1,0:T(8,128)(2,1)} %get-tuple-element.13), calls=%async_computation.2 | async-start | bytes 2359296 | tf_op jit(solution)/shard_map/all_to_all | solution.py:206
  89.4 1.3 %collective-permute-start.8 = (bf16[144,1024]{1,0:T(8,128)(2,1)S(1)}, bf16[144,1024]{1,0:T(8,128)(2,1)S(1)}, u32[]{:S(2)}, u32[]{:S(2)}) collective-permute-start(bf16[144,1024]{1,0:T(8,128)(2,1)S(1)} %get-tuple-element.14.own_ref), channel_id=1, source_target_pairs={{2,0},{1,3},{6,4},{5,7},{10,8},{9,11},{14,12},{13,15},{18,16},{17,... | collective-permute-start | bytes 884744 | tf_op jit(solution)/shard_map/ppermute | solution.py:205
  90.7 3.3 %collective-permute-start.7 = (bf16[144,1024]{1,0:T(8,128)(2,1)S(1)}, bf16[144,1024]{1,0:T(8,128)(2,1)S(1)}, u32[]{:S(2)}, u32[]{:S(2)}) collective-permute-start(bf16[144,1024]{1,0:T(8,128)(2,1)S(1)} %get-tuple-element.14.own_ref), channel_id=1, source_target_pairs={{1,0},{2,1},{3,2},{0,3},{5,4},{6,5},{7,6},{4,7},{9,8},{10,9},{11,1... | collective-permute-start | bytes 884744 | tf_op jit(solution)/shard_map/ppermute | solution.py:204
  94.0 6.5 %collective-permute-done.8.far_ref = bf16[144,1024]{1,0:T(8,128)(2,1)S(1)} collective-permute-done((bf16[144,1024]{1,0:T(8,128)(2,1)S(1)}, bf16[144,1024]{1,0:T(8,128)(2,1)S(1)}, u32[]{:S(2)}, u32[]{:S(2)}) %collective-permute-start.8) | collective-permute-done | bytes 294944 | tf_op jit(solution)/shard_map/ppermute | solution.py:205
  100.5 3.0 %collective-permute-done.7.near_ref = bf16[144,1024]{1,0:T(8,128)(2,1)S(1)} collective-permute-done((bf16[144,1024]{1,0:T(8,128)(2,1)S(1)}, bf16[144,1024]{1,0:T(8,128)(2,1)S(1)}, u32[]{:S(2)}, u32[]{:S(2)}) %collective-permute-start.7) | collective-permute-done | bytes 294944 | tf_op jit(solution)/shard_map/ppermute | solution.py:204
  103.6 1.0 shard_map.106
  104.5 13.4 %all_to_all.21.got_ref = f32[16,8,128]{2,1,0:T(8,128)S(1)} all-to-all(f32[16,8,128]{2,1,0:T(8,128)S(1)} %shard_map.106), channel_id=1, replica_groups=mesh['yh'=2,'z'=8,'core'=2,'x'=4,'y'=4] {'x','y'}, dimensions={0} | all-to-all | bytes 131072 | tf_op jit(solution)/shard_map/all_to_all | solution.py:210
  (25 shorter events, 2.6 us)
Async XLA Ops:
  0.6 70.9 %copy-start = (f32[50265]{0:T(1024)S(1)}, f32[50265]{0:T(1024)}, u32[]{:S(2)}) copy-start(f32[50265]{0:T(1024)} %param.11) | copy-start | bytes 603184
  1.3 1.0 copy-start.1
  2.3 0.9 copy-start.4
  3.2 0.9 copy-start.5
  4.1 0.9 copy-start.6
  5.0 31.4 %copy-start.3 = (bf16[64,1024]{1,0:T(8,128)(2,1)S(1)}, bf16[64,1024]{1,0:T(8,128)(2,1)}, u32[]{:S(2)}) copy-start(bf16[64,1024]{1,0:T(8,128)(2,1)} %o0.1) | copy-start | bytes 393220
  34.5 29.8 %collective-permute-start.3 = (bf16[16,64,384]{2,1,0:T(8,128)(2,1)S(1)}, bf16[16,64,384]{2,1,0:T(8,128)(2,1)S(1)}, u32[]{:S(2)}, u32[]{:S(2)}) collective-permute-start(bf16[16,64,384]{2,1,0:T(8,128)(2,1)S(1)} %all_to_all.20), channel_id=1, source_target_pairs={{0,16},{16,0},{1,17},{17,1},{2,18},{18,2},{3,19},{19,3},{4,20},{20... | collective-permute-start | bytes 2359304 | tf_op jit(solution)/shard_map/ppermute | solution.py:180
  36.4 12.9 %collective-permute-start.5 = (bf16[64,1024]{1,0:T(8,128)(2,1)S(1)}, bf16[64,1024]{1,0:T(8,128)(2,1)S(1)}, u32[]{:S(2)}, u32[]{:S(2)}) collective-permute-start(bf16[64,1024]{1,0:T(8,128)(2,1)S(1)} %copy-done.3), channel_id=1, source_target_pairs={{2,0},{3,1},{256,2},{257,3},{258,256},{259,257},{0,258},{1,259},{6... | collective-permute-start | bytes 393224 | tf_op jit(solution)/shard_map/ppermute | solution.py:179
  39.6 24.7 %collective-permute-start.2 = (bf16[144,1024]{1,0:T(8,128)(2,1)S(1)}, bf16[144,1024]{1,0:T(8,128)(2,1)S(1)}, u32[]{:S(2)}, u32[]{:S(2)}) collective-permute-start(bf16[144,1024]{1,0:T(8,128)(2,1)S(1)} %get-tuple-element.10.x0), channel_id=1, source_target_pairs={{12,0},{0,4},{4,8},{8,12},{13,1},{1,5},{5,9},{9,13},{14,2},{2,6},{... | collective-permute-start | bytes 884744 | tf_op jit(solution)/shard_map/ppermute | solution.py:178
  42.1 22.2 %collective-permute-start.1 = (bf16[144,1024]{1,0:T(8,128)(2,1)S(1)}, bf16[144,1024]{1,0:T(8,128)(2,1)S(1)}, u32[]{:S(2)}, u32[]{:S(2)}) collective-permute-start(bf16[144,1024]{1,0:T(8,128)(2,1)S(1)} %get-tuple-element.10.x0), channel_id=1, source_target_pairs={{8,0},{12,4},{0,8},{4,12},{9,1},{13,5},{1,9},{5,13},{10,2},{14,6},... | collective-permute-start | bytes 884744 | tf_op jit(solution)/shard_map/ppermute | solution.py:178
  46.1 18.2 %collective-permute-start = (bf16[144,1024]{1,0:T(8,128)(2,1)S(1)}, bf16[144,1024]{1,0:T(8,128)(2,1)S(1)}, u32[]{:S(2)}, u32[]{:S(2)}) collective-permute-start(bf16[144,1024]{1,0:T(8,128)(2,1)S(1)} %get-tuple-element.10.x0), channel_id=1, source_target_pairs={{4,0},{8,4},{12,8},{0,12},{5,1},{9,5},{13,9},{1,13},{6,2},{10,6},{... | collective-permute-start | bytes 884744 | tf_op jit(solution)/shard_map/ppermute | solution.py:178
  49.3 6.9 %collective-permute-start.4 = (bf16[64,1024]{1,0:T(8,128)(2,1)S(1)}, bf16[64,1024]{1,0:T(8,128)(2,1)S(1)}, u32[]{:S(2)}, u32[]{:S(2)}) collective-permute-start(bf16[64,1024]{1,0:T(8,128)(2,1)S(1)} %copy-done.3), channel_id=1, source_target_pairs={{1,0},{2,1},{3,2},{256,3},{257,256},{258,257},{259,258},{0,259},{5... | collective-permute-start | bytes 393224 | tf_op jit(solution)/shard_map/ppermute | solution.py:179
  56.2 8.1 %collective-permute-start.6 = (bf16[64,1024]{1,0:T(8,128)(2,1)S(1)}, bf16[64,1024]{1,0:T(8,128)(2,1)S(1)}, u32[]{:S(2)}, u32[]{:S(2)}) collective-permute-start(bf16[64,1024]{1,0:T(8,128)(2,1)S(1)} %copy-done.3), channel_id=1, source_target_pairs={{259,0},{0,1},{1,2},{2,3},{3,256},{256,257},{257,258},{258,259},{2... | collective-permute-start | bytes 393224 | tf_op jit(solution)/shard_map/ppermute | solution.py:179
  67.8 3.7 %copy-start.7 = (s32[1,128]{1,0:T(1,128)S(1)}, s32[1,128]{1,0:T(1,128)}, u32[]{:S(2)}) copy-start(s32[1,128]{1,0:T(1,128)} %param.9) | copy-start | bytes 1540
  67.8 16.5 %copy-start.2 = (bf16[1,128,1024]{2,1,0:T(8,128)(2,1)S(1)}, bf16[1,128,1024]{2,1,0:T(8,128)(2,1)}, u32[]{:S(2)}) copy-start(bf16[1,128,1024]{2,1,0:T(8,128)(2,1)} %x_ref.3) | copy-start | bytes 786436
  67.8 16.5 %all-to-all-start.1 = ((bf16[4,128,1024]{2,1,0:T(8,128)(2,1)}), bf16[4,128,1024]{2,1,0:T(8,128)(2,1)S(1)}, u32[]{:S(2)}, u32[]{:S(2)}) async-start(bf16[4,128,1024]{2,1,0:T(8,128)(2,1)} %shard_map.104), calls=%async_computation.1 | async-start | bytes 2097152 | tf_op jit(solution)/shard_map/all_to_all | solution.py:190
  85.8 17.7 %all-to-all-start.2 = ((bf16[4,144,1024]{2,1,0:T(8,128)(2,1)}), bf16[4,144,1024]{2,1,0:T(8,128)(2,1)S(1)}, u32[]{:S(2)}, u32[]{:S(2)}) async-start(bf16[4,144,1024]{2,1,0:T(8,128)(2,1)} %get-tuple-element.13), calls=%async_computation.2 | async-start | bytes 2359296 | tf_op jit(solution)/shard_map/all_to_all | solution.py:206
  89.4 11.2 %collective-permute-start.8 = (bf16[144,1024]{1,0:T(8,128)(2,1)S(1)}, bf16[144,1024]{1,0:T(8,128)(2,1)S(1)}, u32[]{:S(2)}, u32[]{:S(2)}) collective-permute-start(bf16[144,1024]{1,0:T(8,128)(2,1)S(1)} %get-tuple-element.14.own_ref), channel_id=1, source_target_pairs={{2,0},{1,3},{6,4},{5,7},{10,8},{9,11},{14,12},{13,15},{18,16},{17,... | collective-permute-start | bytes 884744 | tf_op jit(solution)/shard_map/ppermute | solution.py:205
  90.7 12.9 %collective-permute-start.7 = (bf16[144,1024]{1,0:T(8,128)(2,1)S(1)}, bf16[144,1024]{1,0:T(8,128)(2,1)S(1)}, u32[]{:S(2)}, u32[]{:S(2)}) collective-permute-start(bf16[144,1024]{1,0:T(8,128)(2,1)S(1)} %get-tuple-element.14.own_ref), channel_id=1, source_target_pairs={{1,0},{2,1},{3,2},{0,3},{5,4},{6,5},{7,6},{4,7},{9,8},{10,9},{11,1... | collective-permute-start | bytes 884744 | tf_op jit(solution)/shard_map/ppermute | solution.py:204

commit v2 on v1

--- a/solution.py
+++ b/solution.py
@@ -15,22 +15,28 @@
 SMEM = pl.BlockSpec(memory_space=pltpu.SMEM)
 
 
-def params():
-    return pltpu.CompilerParams(vmem_limit_bytes=40 * 1024 * 1024)
-
-
-def prepare_kernel(lengths_ref, x_ref, q_ref, k_ref, v_ref, chunk_ref, ext_ref):
+def params(mebibytes):
+    return pltpu.CompilerParams(vmem_limit_bytes=mebibytes * 1024 * 1024)
+
+
+def prepare_kernel(lengths_ref, x_hbm, q_hbm, k_hbm, v_hbm, chunk_ref, ext_ref, q_ref, k_ref, v_ref, sems):
     core = lax.axis_index("core")
-    rows = x_ref.shape[1]
-    for block in range(4):
-        at = pl.multiple_of(block * 2 * LANES + core * LANES, LANES)
-        for n, ref in enumerate((q_ref, k_ref, v_ref)):
+    rows = x_hbm.shape[1]
+    copies = [pltpu.make_async_copy(x_hbm.at[0], ext_ref.at[pl.ds(0, rows)], sems.at[3])]
+    for n, (far, near) in enumerate(((q_hbm, q_ref), (k_hbm, k_ref), (v_hbm, v_ref))):
+        copies.append(pltpu.make_async_copy(far, near, sems.at[n]))
+    for copy in copies:
+        copy.start()
+    length = lengths_ref[0].astype(jnp.float32)
+    ext_ref[rows:, :] = jnp.full((PAD, ext_ref.shape[1]), length, jnp.float32).astype(jnp.bfloat16)
+    for n, ref in enumerate((q_ref, k_ref, v_ref)):
+        copies[n + 1].wait()
+        for block in range(4):
+            at = pl.multiple_of(block * 2 * LANES + core * LANES, LANES)
             piece = ref[:, pl.ds(at, LANES)]
             for y in range(4):
                 chunk_ref[block * 4 + y, :, n * LANES : (n + 1) * LANES] = piece
-    ext_ref[:rows, :] = x_ref[0]
-    length = lengths_ref[0].astype(jnp.float32)
-    ext_ref[rows:, :] = jnp.full((PAD, ext_ref.shape[1]), length, jnp.float32).astype(jnp.bfloat16)
+    copies[0].wait()
 
 
 def attend_kernel(x0, x1, x2, x3, wa_ref, wb_ref, o0, o1, o2, o3, part_ref, wo_ref):
@@ -146,14 +152,14 @@
     mean_ref[...] = (jnp.sum(rest, axis=1, keepdims=True) / 15)[:1]
 
 
-def call(kernel, ins, outs, *args, scratch=()):
+def call(kernel, ins, outs, *args, scratch=(), mebibytes=40):
     return pl.pallas_call(
         kernel,
         in_specs=ins,
         out_specs=tuple(VMEM for _ in outs) if len(outs) > 1 else VMEM,
         out_shape=outs if len(outs) > 1 else outs[0],
         scratch_shapes=list(scratch),
-        compiler_params=params(),
+        compiler_params=params(mebibytes),
     )(*args)
 
 
@@ -167,16 +173,19 @@
     bf16, f32 = jnp.bfloat16, jnp.float32
     chunks, extended = call(
         prepare_kernel,
-        [SMEM] + [VMEM] * 4,
+        [SMEM] + [pl.BlockSpec(memory_space=pltpu.HBM)] * 4,
         (
             jax.ShapeDtypeStruct((16, depth, 3 * LANES), bf16),
             jax.ShapeDtypeStruct((length + PAD, width), bf16),
         ),
         lengths, layer_input, query_weight, key_weight, value_weight,
+        scratch=[pltpu.VMEM((depth, width), bf16)] * 3 + [pltpu.SemaphoreType.DMA((4,))],
+        mebibytes=63,
     )
     near_half = lax.all_to_all(chunks, ("x", "y"), split_axis=0, concat_axis=0, tiled=True)
     others = [lax.ppermute(extended, "x", shift(4, k)) for k in (1, 2, 3)]
     blocks = [lax.ppermute(output_weight, ("yh", "y"), shift(8, k)) for k in (1, 2, 7)]
+    near_half, others, blocks = lax.optimization_barrier((near_half, others, blocks))
     far_half = lax.ppermute(near_half, "core", [(0, 1), (1, 0)])
     parts = call(
         attend_kernel,

time: 119 us -> 110 us (0.924)
  blocking collectives: 42.7 us -> 12.6 us
  waiting for transfers between devices: 30 us -> 43.7 us
  starting transfers between devices: 32.7 us -> 41.8 us
  local copies, waits for them, and re-layouts: 4.83 us -> 1.17 us
  Pallas kernels: 6.69 us -> 8.77 us
    all_to_all x1 -> x0, blocking collectives: 29.4 us -> none  [shards(): lax.all_to_all(chunks, ('x', 'y'), split_axis=0, concat_axis=0, tiled=True)]
    all_to_all x0 -> x1, starting transfers between devices: none -> 7.59 us  [shards(): lax.all_to_all(chunks, ('x', 'y'), split_axis=0, concat_axis=0, tiled=True)]
    ppermute x3, waiting for transfers between devices: 8.79 us -> 13.5 us  [shards(): lax.ppermute(output_weight, ('yh', 'y'), shift(8, k))]
    unnamed x16 -> x10, local copies, waits for them, and re-layouts: 3.68 us -> 0.03 us
    ppermute x1, waiting for transfers between devices: 6.53 us -> 9.52 us  [shards(): far = lax.ppermute(own, 'y', [(2, 0), (1, 3)])]
    all_to_all x1, waiting for transfers between devices: 11.7 us -> 14.2 us  [shards(): parts = lax.all_to_all(parts, 'x', split_axis=0, concat_axis=0, tiled=True)]
    ppermute x1, waiting for transfers between devices: 0.01 us -> 2.25 us  [shards(): far_half = lax.ppermute(near_half, 'core', [(0, 1), (1, 0)])]
    ppermute x3, starting transfers between devices: 9.7 us -> 11.8 us  [shards(): others = [lax.ppermute(extended, 'x', shift(4, k)) for k in (1, 2, 3)]]
  transfers between devices with their start and end apart: 11 -> 12, of which waited for: 5 -> 6; matrix products, arithmetic and copies ran while one was open for 1% -> 1% of each run, Pallas kernels for 0% -> 0%
where the time goes in v2:
time: 110 us
  waiting for transfers between devices  43.7 us (40%)
  starting transfers between devices  41.8 us (38%)
  blocking collectives  12.6 us (11%)
  Pallas kernels  8.77 us (8%)
  between operations  1.53 us (1%)
  local copies, waits for them, and re-layouts  1.17 us (1%)
    all_to_all x1, waiting for transfers between devices, shards(): parts = lax.all_to_all(parts, 'x', split_axis=0, concat_axis=0, tiled=True)  14.2 us
    ppermute x3, waiting for transfers between devices, shards(): lax.ppermute(output_weight, ('yh', 'y'), shift(8, k))  13.5 us
    all_to_all x1, blocking collectives, shards(): lax.all_to_all(known, ('x', 'y'), split_axis=0, concat_axis=0, tiled=True)  12.6 us
    ppermute x3, starting transfers between devices, shards(): others = [lax.ppermute(extended, 'x', shift(4, k)) for k in (1, 2, 3)]  11.8 us
    ppermute x1, waiting for transfers between devices, shards(): far = lax.ppermute(own, 'y', [(2, 0), (1, 3)])  9.52 us
    ppermute x3, starting transfers between devices, shards(): lax.ppermute(output_weight, ('yh', 'y'), shift(8, k))  9.42 us
    pallas_call x5, Pallas kernels, call(): pl.pallas_call(kernel, in_specs=ins, out_specs=tuple((VMEM for _ in outs)...  8.77 us
    all_to_all x1, starting transfers between devices, shards(): lax.all_to_all(chunks, ('x', 'y'), split_axis=0, concat_axis=0, tiled=True)  7.59 us
  transfers between devices with their start and end apart: 12, of which 6 were waited for; matrix products, arithmetic and copies ran while one was open for 1% of the time, Pallas kernels for 0%

profile of v2, /device:TPU:448, one launch (start us, length us, event | category | flops | bytes accessed | tf_op | source)
XLA Modules:
  0.0 109.6 jit_solution(11558565770919108604)
XLA Ops:
  1.3 2.2 %shard_map.103 = (bf16[16,64,384]{2,1,0:T(8,128)(2,1)}, bf16[144,1024]{1,0:T(8,128)(2,1)}) custom-call(s32[1]{0:T(128)} %copy.11.lengths_ref, bf16[1,128,1024]{2,1,0:T(8,128)(2,1)} %x_ref.1, bf16[64,1024]{1,0:T(8,128)(2,1)} %q_hbm.1, bf16[64,1024]{1,0:T(8,128)(2,1)} %k_hbm.1, bf16[64,1024]{1,0:T(8,128)(2,1)} %v_hbm.1), custom_call_target="tpu_custom_call" | custom-call | tf_op jit(solution)/shard_map/pallas_call | solution.py:156
  3.5 7.6 %all-to-all-start = ((bf16[16,64,384]{2,1,0:T(8,128)(2,1)}), bf16[16,64,384]{2,1,0:T(8,128)(2,1)S(1)}, u32[]{:S(2)}, u32[]{:S(2)}) async-start(bf16[16,64,384]{2,1,0:T(8,128)(2,1)} %get-tuple-element.18), calls=%async_computation | async-start | bytes 1572864 | tf_op jit(solution)/shard_map/all_to_all | solution.py:185
  11.2 3.8 %collective-permute-start.2 = (bf16[144,1024]{1,0:T(8,128)(2,1)S(1)}, bf16[144,1024]{1,0:T(8,128)(2,1)S(1)}, u32[]{:S(2)}, u32[]{:S(2)}) collective-permute-start(bf16[144,1024]{1,0:T(8,128)(2,1)S(1)} %copy-done.2), channel_id=1, source_target_pairs={{12,0},{0,4},{4,8},{8,12},{13,1},{1,5},{5,9},{9,13},{14,2},{2,6},{... | collective-permute-start | bytes 884744 | tf_op jit(solution)/shard_map/ppermute | solution.py:186
  15.0 4.6 %collective-permute-start.1 = (bf16[144,1024]{1,0:T(8,128)(2,1)S(1)}, bf16[144,1024]{1,0:T(8,128)(2,1)S(1)}, u32[]{:S(2)}, u32[]{:S(2)}) collective-permute-start(bf16[144,1024]{1,0:T(8,128)(2,1)S(1)} %copy-done.2), channel_id=1, source_target_pairs={{8,0},{12,4},{0,8},{4,12},{9,1},{13,5},{1,9},{5,13},{10,2},{14,6},... | collective-permute-start | bytes 884744 | tf_op jit(solution)/shard_map/ppermute | solution.py:186
  19.6 3.4 %collective-permute-start = (bf16[144,1024]{1,0:T(8,128)(2,1)S(1)}, bf16[144,1024]{1,0:T(8,128)(2,1)S(1)}, u32[]{:S(2)}, u32[]{:S(2)}) collective-permute-start(bf16[144,1024]{1,0:T(8,128)(2,1)S(1)} %copy-done.2), channel_id=1, source_target_pairs={{4,0},{8,4},{12,8},{0,12},{5,1},{9,5},{13,9},{1,13},{6,2},{10,6},{... | collective-permute-start | bytes 884744 | tf_op jit(solution)/shard_map/ppermute | solution.py:186
  23.0 5.0 %collective-permute-start.4 = (bf16[64,1024]{1,0:T(8,128)(2,1)S(1)}, bf16[64,1024]{1,0:T(8,128)(2,1)S(1)}, u32[]{:S(2)}, u32[]{:S(2)}) collective-permute-start(bf16[64,1024]{1,0:T(8,128)(2,1)S(1)} %copy-done.3), channel_id=1, source_target_pairs={{2,0},{3,1},{256,2},{257,3},{258,256},{259,257},{0,258},{1,259},{6... | collective-permute-start | bytes 393224 | tf_op jit(solution)/shard_map/ppermute | solution.py:187
  28.0 2.5 %collective-permute-start.3 = (bf16[64,1024]{1,0:T(8,128)(2,1)S(1)}, bf16[64,1024]{1,0:T(8,128)(2,1)S(1)}, u32[]{:S(2)}, u32[]{:S(2)}) collective-permute-start(bf16[64,1024]{1,0:T(8,128)(2,1)S(1)} %copy-done.3), channel_id=1, source_target_pairs={{1,0},{2,1},{3,2},{256,3},{257,256},{258,257},{259,258},{0,259},{5... | collective-permute-start | bytes 393224 | tf_op jit(solution)/shard_map/ppermute | solution.py:187
  30.5 7.4 %collective-permute-done.4.o2 = bf16[64,1024]{1,0:T(8,128)(2,1)S(1)} collective-permute-done((bf16[64,1024]{1,0:T(8,128)(2,1)S(1)}, bf16[64,1024]{1,0:T(8,128)(2,1)S(1)}, u32[]{:S(2)}, u32[]{:S(2)}) %collective-permute-start.4) | collective-permute-done | bytes 131104 | tf_op jit(solution)/shard_map/ppermute | solution.py:187
  37.9 1.9 %collective-permute-start.5 = (bf16[64,1024]{1,0:T(8,128)(2,1)S(1)}, bf16[64,1024]{1,0:T(8,128)(2,1)S(1)}, u32[]{:S(2)}, u32[]{:S(2)}) collective-permute-start(bf16[64,1024]{1,0:T(8,128)(2,1)S(1)} %copy-done.3), channel_id=1, source_target_pairs={{259,0},{0,1},{1,2},{2,3},{3,256},{256,257},{257,258},{258,259},{2... | collective-permute-start | bytes 393224 | tf_op jit(solution)/shard_map/ppermute | solution.py:187
  39.8 6.1 %collective-permute-done.5.o3 = bf16[64,1024]{1,0:T(8,128)(2,1)S(1)} collective-permute-done((bf16[64,1024]{1,0:T(8,128)(2,1)S(1)}, bf16[64,1024]{1,0:T(8,128)(2,1)S(1)}, u32[]{:S(2)}, u32[]{:S(2)}) %collective-permute-start.5) | collective-permute-done | bytes 131104 | tf_op jit(solution)/shard_map/ppermute | solution.py:187
  45.9 1.9 %collective-permute-start.6 = (bf16[16,64,384]{2,1,0:T(8,128)(2,1)S(1)}, bf16[16,64,384]{2,1,0:T(8,128)(2,1)S(1)}, u32[]{:S(2)}, u32[]{:S(2)}) collective-permute-start(bf16[16,64,384]{2,1,0:T(8,128)(2,1)S(1)} %all-to-all-done), channel_id=1, source_target_pairs={{0,16},{16,0},{1,17},{17,1},{2,18},{18,2},{3,19},{19,3},{4,20},{20... | collective-permute-start | bytes 2359304 | tf_op jit(solution)/shard_map/ppermute | solution.py:189
  47.9 2.3 %collective-permute-done.6 = bf16[16,64,384]{2,1,0:T(8,128)(2,1)S(1)} collective-permute-done((bf16[16,64,384]{2,1,0:T(8,128)(2,1)S(1)}, bf16[16,64,384]{2,1,0:T(8,128)(2,1)S(1)}, u32[]{:S(2)}, u32[]{:S(2)}) %collective-permute-start.6) | collective-permute-done | bytes 786464 | tf_op jit(solution)/shard_map/ppermute | solution.py:189
  50.1 3.5 %shard_map.104 = bf16[4,128,1024]{2,1,0:T(8,128)(2,1)} custom-call(bf16[144,1024]{1,0:T(8,128)(2,1)S(1)} %copy-done.2, bf16[144,1024]{1,0:T(8,128)(2,1)S(1)} %collective-permute-done.x1, bf16[144,1024]{1,0:T(8,128)(2,1)S(1)} %collective-permute-done.1.x2, bf16[144,1024]{1,0:T(8,128)(2,1)S(1)} %collective-permute-done.2.x3, bf16[1024,384]{1,0:T(8,128)(2,1)S(1)} %bitcast.9, ...), custom_call_target="tpu_custom_call" | custom-call | tf_op jit(solution)/shard_map/pallas_call | solution.py:156
  53.7 4.4 %all-to-all-start.1 = ((bf16[4,128,1024]{2,1,0:T(8,128)(2,1)}), bf16[4,128,1024]{2,1,0:T(8,128)(2,1)S(1)}, u32[]{:S(2)}, u32[]{:S(2)}) async-start(bf16[4,128,1024]{2,1,0:T(8,128)(2,1)} %shard_map.104), calls=%async_computation.1 | async-start | bytes 2097152 | tf_op jit(solution)/shard_map/all_to_all | solution.py:199
  58.1 1.1 %gather_fusion = bf16[128]{0:T(256)(128)(2,1)S(1)} fusion(f32[50265]{0:T(1024)S(1)} %copy-done, s32[1024]{0:T(1024)S(1)} %pad_clamp_fusion), kind=kCustom, calls=%fused_computation | custom fusion | bytes 1024 | tf_op jit(solution)/shard_map/jit(_take)/gather | solution.py:202
  59.2 14.2 %all-to-all-done.1.parts_ref = bf16[4,128,1024]{2,1,0:T(8,128)(2,1)S(1)} async-done(((bf16[4,128,1024]{2,1,0:T(8,128)(2,1)}), bf16[4,128,1024]{2,1,0:T(8,128)(2,1)S(1)}, u32[]{:S(2)}, u32[]{:S(2)}) %all-to-all-start.1) | async-done | bytes 1048608 | tf_op jit(solution)/shard_map/all_to_all | solution.py:199
  73.4 1.5 %shard_map.105 = (bf16[1,128,1024]{2,1,0:T(8,128)(2,1)}, bf16[144,1024]{1,0:T(8,128)(2,1)S(1)}, bf16[4,144,1024]{2,1,0:T(8,128)(2,1)}) custom-call(bf16[1,128]{1,0:T(2,128)(2,1)S(1)} %fusion.weight_ref, bf16[4,128,1024]{2,1,0:T(8,128)(2,1)S(1)} %all-to-all-done.1.parts_ref, bf16[1,128,1024]{2,1,0:T(8,128)(2,1)S(1)} %copy-done.1), custom_call_target="tpu_custom_call" | custom-call | tf_op jit(solution)/shard_map/pallas_call | solution.py:156
  74.9 3.5 %all-to-all-start.2 = ((bf16[4,144,1024]{2,1,0:T(8,128)(2,1)}), bf16[4,144,1024]{2,1,0:T(8,128)(2,1)S(1)}, u32[]{:S(2)}, u32[]{:S(2)}) async-start(bf16[4,144,1024]{2,1,0:T(8,128)(2,1)} %get-tuple-element.27), calls=%async_computation.2 | async-start | bytes 2359296 | tf_op jit(solution)/shard_map/all_to_all | solution.py:215
  78.5 1.3 %collective-permute-start.8 = (bf16[144,1024]{1,0:T(8,128)(2,1)S(1)}, bf16[144,1024]{1,0:T(8,128)(2,1)S(1)}, u32[]{:S(2)}, u32[]{:S(2)}) collective-permute-start(bf16[144,1024]{1,0:T(8,128)(2,1)S(1)} %get-tuple-element.28.own_ref), channel_id=1, source_target_pairs={{2,0},{1,3},{6,4},{5,7},{10,8},{9,11},{14,12},{13,15},{18,16},{17,... | collective-permute-start | bytes 884744 | tf_op jit(solution)/shard_map/ppermute | solution.py:214
  79.8 1.9 %collective-permute-start.7 = (bf16[144,1024]{1,0:T(8,128)(2,1)S(1)}, bf16[144,1024]{1,0:T(8,128)(2,1)S(1)}, u32[]{:S(2)}, u32[]{:S(2)}) collective-permute-start(bf16[144,1024]{1,0:T(8,128)(2,1)S(1)} %get-tuple-element.28.own_ref), channel_id=1, source_target_pairs={{1,0},{2,1},{3,2},{0,3},{5,4},{6,5},{7,6},{4,7},{9,8},{10,9},{11,1... | collective-permute-start | bytes 884744 | tf_op jit(solution)/shard_map/ppermute | solution.py:213
  81.7 9.5 %collective-permute-done.8.far_ref = bf16[144,1024]{1,0:T(8,128)(2,1)S(1)} collective-permute-done((bf16[144,1024]{1,0:T(8,128)(2,1)S(1)}, bf16[144,1024]{1,0:T(8,128)(2,1)S(1)}, u32[]{:S(2)}, u32[]{:S(2)}) %collective-permute-start.8) | collective-permute-done | bytes 294944 | tf_op jit(solution)/shard_map/ppermute | solution.py:214
  91.2 4.2 %collective-permute-done.7.near_ref = bf16[144,1024]{1,0:T(8,128)(2,1)S(1)} collective-permute-done((bf16[144,1024]{1,0:T(8,128)(2,1)S(1)}, bf16[144,1024]{1,0:T(8,128)(2,1)S(1)}, u32[]{:S(2)}, u32[]{:S(2)}) %collective-permute-start.7) | collective-permute-done | bytes 294944 | tf_op jit(solution)/shard_map/ppermute | solution.py:213
  95.5 1.0 shard_map.106
  96.4 12.6 %all_to_all.20.got_ref = f32[16,8,128]{2,1,0:T(8,128)S(1)} all-to-all(f32[16,8,128]{2,1,0:T(8,128)S(1)} %shard_map.106), channel_id=1, replica_groups=mesh['yh'=2,'z'=8,'core'=2,'x'=4,'y'=4] {'x','y'}, dimensions={0} | all-to-all | bytes 131072 | tf_op jit(solution)/shard_map/all_to_all | solution.py:219
  (20 shorter events, 0.7 us)
Async XLA Ops:
  0.6 57.4 %copy-start = (f32[50265]{0:T(1024)S(1)}, f32[50265]{0:T(1024)}, u32[]{:S(2)}) copy-start(f32[50265]{0:T(1024)} %param.11) | copy-start | bytes 603184
  0.6 22.3 %copy-start.3 = (bf16[64,1024]{1,0:T(8,128)(2,1)S(1)}, bf16[64,1024]{1,0:T(8,128)(2,1)}, u32[]{:S(2)}) copy-start(bf16[64,1024]{1,0:T(8,128)(2,1)} %o0.1) | copy-start | bytes 393220
  3.5 7.6 %copy-start.2 = (bf16[144,1024]{1,0:T(8,128)(2,1)S(1)}, bf16[144,1024]{1,0:T(8,128)(2,1)}, u32[]{:S(2)}) copy-start(bf16[144,1024]{1,0:T(8,128)(2,1)} %get-tuple-element.17.x0) | copy-start | bytes 884740
  3.5 42.4 %all-to-all-start = ((bf16[16,64,384]{2,1,0:T(8,128)(2,1)}), bf16[16,64,384]{2,1,0:T(8,128)(2,1)S(1)}, u32[]{:S(2)}, u32[]{:S(2)}) async-start(bf16[16,64,384]{2,1,0:T(8,128)(2,1)} %get-tuple-element.18), calls=%async_computation | async-start | bytes 1572864 | tf_op jit(solution)/shard_map/all_to_all | solution.py:185
  11.2 34.8 %collective-permute-start.2 = (bf16[144,1024]{1,0:T(8,128)(2,1)S(1)}, bf16[144,1024]{1,0:T(8,128)(2,1)S(1)}, u32[]{:S(2)}, u32[]{:S(2)}) collective-permute-start(bf16[144,1024]{1,0:T(8,128)(2,1)S(1)} %copy-done.2), channel_id=1, source_target_pairs={{12,0},{0,4},{4,8},{8,12},{13,1},{1,5},{5,9},{9,13},{14,2},{2,6},{... | collective-permute-start | bytes 884744 | tf_op jit(solution)/shard_map/ppermute | solution.py:186
  15.0 30.9 %collective-permute-start.1 = (bf16[144,1024]{1,0:T(8,128)(2,1)S(1)}, bf16[144,1024]{1,0:T(8,128)(2,1)S(1)}, u32[]{:S(2)}, u32[]{:S(2)}) collective-permute-start(bf16[144,1024]{1,0:T(8,128)(2,1)S(1)} %copy-done.2), channel_id=1, source_target_pairs={{8,0},{12,4},{0,8},{4,12},{9,1},{13,5},{1,9},{5,13},{10,2},{14,6},... | collective-permute-start | bytes 884744 | tf_op jit(solution)/shard_map/ppermute | solution.py:186
  19.6 26.3 %collective-permute-start = (bf16[144,1024]{1,0:T(8,128)(2,1)S(1)}, bf16[144,1024]{1,0:T(8,128)(2,1)S(1)}, u32[]{:S(2)}, u32[]{:S(2)}) collective-permute-start(bf16[144,1024]{1,0:T(8,128)(2,1)S(1)} %copy-done.2), channel_id=1, source_target_pairs={{4,0},{8,4},{12,8},{0,12},{5,1},{9,5},{13,9},{1,13},{6,2},{10,6},{... | collective-permute-start | bytes 884744 | tf_op jit(solution)/shard_map/ppermute | solution.py:186
  23.0 14.9 %collective-permute-start.4 = (bf16[64,1024]{1,0:T(8,128)(2,1)S(1)}, bf16[64,1024]{1,0:T(8,128)(2,1)S(1)}, u32[]{:S(2)}, u32[]{:S(2)}) collective-permute-start(bf16[64,1024]{1,0:T(8,128)(2,1)S(1)} %copy-done.3), channel_id=1, source_target_pairs={{2,0},{3,1},{256,2},{257,3},{258,256},{259,257},{0,258},{1,259},{6... | collective-permute-start | bytes 393224 | tf_op jit(solution)/shard_map/ppermute | solution.py:187
  28.0 11.8 %collective-permute-start.3 = (bf16[64,1024]{1,0:T(8,128)(2,1)S(1)}, bf16[64,1024]{1,0:T(8,128)(2,1)S(1)}, u32[]{:S(2)}, u32[]{:S(2)}) collective-permute-start(bf16[64,1024]{1,0:T(8,128)(2,1)S(1)} %copy-done.3), channel_id=1, source_target_pairs={{1,0},{2,1},{3,2},{256,3},{257,256},{258,257},{259,258},{0,259},{5... | collective-permute-start | bytes 393224 | tf_op jit(solution)/shard_map/ppermute | solution.py:187
  37.9 8.1 %collective-permute-start.5 = (bf16[64,1024]{1,0:T(8,128)(2,1)S(1)}, bf16[64,1024]{1,0:T(8,128)(2,1)S(1)}, u32[]{:S(2)}, u32[]{:S(2)}) collective-permute-start(bf16[64,1024]{1,0:T(8,128)(2,1)S(1)} %copy-done.3), channel_id=1, source_target_pairs={{259,0},{0,1},{1,2},{2,3},{3,256},{256,257},{257,258},{258,259},{2... | collective-permute-start | bytes 393224 | tf_op jit(solution)/shard_map/ppermute | solution.py:187
  45.9 4.2 %collective-permute-start.6 = (bf16[16,64,384]{2,1,0:T(8,128)(2,1)S(1)}, bf16[16,64,384]{2,1,0:T(8,128)(2,1)S(1)}, u32[]{:S(2)}, u32[]{:S(2)}) collective-permute-start(bf16[16,64,384]{2,1,0:T(8,128)(2,1)S(1)} %all-to-all-done), channel_id=1, source_target_pairs={{0,16},{16,0},{1,17},{17,1},{2,18},{18,2},{3,19},{19,3},{4,20},{20... | collective-permute-start | bytes 2359304 | tf_op jit(solution)/shard_map/ppermute | solution.py:189
  53.7 4.4 %copy-start.4 = (s32[1,128]{1,0:T(1,128)S(1)}, s32[1,128]{1,0:T(1,128)}, u32[]{:S(2)}) copy-start(s32[1,128]{1,0:T(1,128)} %param.9) | copy-start | bytes 1540
  53.7 19.8 %copy-start.1 = (bf16[1,128,1024]{2,1,0:T(8,128)(2,1)S(1)}, bf16[1,128,1024]{2,1,0:T(8,128)(2,1)}, u32[]{:S(2)}) copy-start(bf16[1,128,1024]{2,1,0:T(8,128)(2,1)} %x_ref.1) | copy-start | bytes 786436
  53.7 19.8 %all-to-all-start.1 = ((bf16[4,128,1024]{2,1,0:T(8,128)(2,1)}), bf16[4,128,1024]{2,1,0:T(8,128)(2,1)S(1)}, u32[]{:S(2)}, u32[]{:S(2)}) async-start(bf16[4,128,1024]{2,1,0:T(8,128)(2,1)} %shard_map.104), calls=%async_computation.1 | async-start | bytes 2097152 | tf_op jit(solution)/shard_map/all_to_all | solution.py:199
  74.9 20.5 %all-to-all-start.2 = ((bf16[4,144,1024]{2,1,0:T(8,128)(2,1)}), bf16[4,144,1024]{2,1,0:T(8,128)(2,1)S(1)}, u32[]{:S(2)}, u32[]{:S(2)}) async-start(bf16[4,144,1024]{2,1,0:T(8,128)(2,1)} %get-tuple-element.27), calls=%async_computation.2 | async-start | bytes 2359296 | tf_op jit(solution)/shard_map/all_to_all | solution.py:215
  78.5 12.8 %collective-permute-start.8 = (bf16[144,1024]{1,0:T(8,128)(2,1)S(1)}, bf16[144,1024]{1,0:T(8,128)(2,1)S(1)}, u32[]{:S(2)}, u32[]{:S(2)}) collective-permute-start(bf16[144,1024]{1,0:T(8,128)(2,1)S(1)} %get-tuple-element.28.own_ref), channel_id=1, source_target_pairs={{2,0},{1,3},{6,4},{5,7},{10,8},{9,11},{14,12},{13,15},{18,16},{17,... | collective-permute-start | bytes 884744 | tf_op jit(solution)/shard_map/ppermute | solution.py:214
  79.8 15.7 %collective-permute-start.7 = (bf16[144,1024]{1,0:T(8,128)(2,1)S(1)}, bf16[144,1024]{1,0:T(8,128)(2,1)S(1)}, u32[]{:S(2)}, u32[]{:S(2)}) collective-permute-start(bf16[144,1024]{1,0:T(8,128)(2,1)S(1)} %get-tuple-element.28.own_ref), channel_id=1, source_target_pairs={{1,0},{2,1},{3,2},{0,3},{5,4},{6,5},{7,6},{4,7},{9,8},{10,9},{11,1... | collective-permute-start | bytes 884744 | tf_op jit(solution)/shard_map/ppermute | solution.py:213

commit v3 on v2

v3 whole, which is shorter than its diff:
```python
import functools

import jax
import jax.numpy as jnp
import numpy as np
from jax import lax
from jax.experimental import pallas as pl
from jax.experimental.pallas import tpu as pltpu
from jax.sharding import Mesh, PartitionSpec as P

HEAD = 64
LANES = 128
PAD = 16
VMEM = pl.BlockSpec(memory_space=pltpu.VMEM)
SMEM = pl.BlockSpec(memory_space=pltpu.SMEM)


def params(mebibytes):
    return pltpu.CompilerParams(vmem_limit_bytes=mebibytes * 1024 * 1024)


def prepare_kernel(lengths_ref, x_hbm, q_hbm, k_hbm, v_hbm, o_hbm, chunk_ref, ext_ref, q_ref, k_ref, v_ref, o_ref, sems):
    core = lax.axis_index("core")
    rows = x_hbm.shape[1]
    copies = [pltpu.make_async_copy(x_hbm.at[0], ext_ref.at[pl.ds(0, rows)], sems.at[4])]
    for n, (far, near) in enumerate(((q_hbm, q_ref), (k_hbm, k_ref), (v_hbm, v_ref), (o_hbm, o_ref))):
        copies.append(pltpu.make_async_copy(far, near, sems.at[n]))
    for copy in copies:
        copy.start()
    length = lengths_ref[0].astype(jnp.float32)
    ext_ref[rows:, :] = jnp.full((PAD, ext_ref.shape[1]), length, jnp.float32).astype(jnp.bfloat16)
    for n, ref in enumerate((q_ref, k_ref, v_ref)):
        copies[n + 1].wait()
        for block in range(4):
            at = pl.multiple_of(block * 2 * LANES + core * LANES, LANES)
            piece = ref[:, pl.ds(at, LANES)]
            for y in range(4):
                chunk_ref[block * 4 + y, :, n * LANES : (n + 1) * LANES] = piece
    copies[4].wait()
    half = o_ref.shape[1] // 2
    piece = o_ref[:, pl.ds(pl.multiple_of(core * half, half), half)]
    for p in range(16):
        chunk_ref[p, :, 3 * LANES :] = piece
    copies[0].wait()


def attend_kernel(x0, x1, x2, x3, wa_ref, wb_ref, weight_ref, out_ref):
    core = lax.axis_index("core")
    x = lax.axis_index("x")
    length = LANES
    xs = (x0, x1, x2, x3)
    tokens = jnp.concatenate([r[:length, :] for r in xs], axis=0)
    first = lax.broadcasted_iota(jnp.int32, (length, LANES), 1) < HEAD
    position = lax.broadcasted_iota(jnp.int32, (2 * length, length), 1).astype(jnp.float32)
    for half, w_ref in enumerate((wa_ref, wb_ref)):
        columns = pl.ds(pl.multiple_of((core if half == 0 else 1 - core) * LANES, LANES), LANES)
        qkv = jnp.dot(tokens, w_ref[:, : 3 * LANES], preferred_element_type=jnp.float32).astype(jnp.bfloat16)
        for c in range(4):
            rows = slice(c * length, (c + 1) * length)
            q = qkv[rows, :LANES]
            key = qkv[rows, LANES : 2 * LANES]
            v = qkv[rows, 2 * LANES :]
            zero = jnp.zeros_like(q)
            both = jnp.concatenate([jnp.where(first, q, zero), jnp.where(first, zero, q)], axis=0)
            scores = lax.dot_general(
                both, key, (((1,), (1,)), ((), ())), preferred_element_type=jnp.float32
            ) * (HEAD ** -0.5)
            used = xs[c][length : length + 1, :length].astype(jnp.float32)
            scores = jnp.where(position < used, scores, -1e9)
            expo = jnp.exp(scores - jnp.max(scores, axis=1, keepdims=True))
            probs = (expo / jnp.sum(expo, axis=1, keepdims=True)).astype(jnp.bfloat16)
            ctx = jnp.dot(probs, v, preferred_element_type=jnp.float32)
            at = pl.multiple_of(lax.rem(x + c, 4) * length, length)
            context = jnp.where(first, ctx[:length], ctx[length:]).astype(jnp.bfloat16)
            for p in range(4):
                out_ref[p, pl.ds(at, length), columns] = context
    weight = jnp.broadcast_to(weight_ref[...].astype(jnp.float32), (PAD, LANES))
    weight = jnp.concatenate([weight, weight], axis=1).astype(jnp.bfloat16)
    for p in range(4):
        out_ref[p, 4 * length :, :] = weight


def embed_kernel(ctxs_ref, x0, x1, x2, x3, wa_ref, wb_ref, out_ref, ext_ref, row_ref, weight_ref, ctx_ref, mixed_ref):
    core = lax.axis_index("core")
    x = lax.axis_index("x")
    length = LANES
    width = out_ref.shape[2]
    for c in range(4):
        at = pl.multiple_of(lax.rem(x + c, 4) * length, length)
        for g in range(4):
            columns = slice(g * 4 * HEAD, (g + 1) * 4 * HEAD)
            ctx_ref[c * length : (c + 1) * length, columns] = ctxs_ref[g, pl.ds(at, length), :]
    half = width // 2
    for side, w_ref in ((core, wa_ref), (1 - core, wb_ref)):
        columns = pl.ds(pl.multiple_of(side * half, half), half)
        mixed_ref[:, columns] = jnp.dot(ctx_ref[...], w_ref[:, 3 * LANES :], preferred_element_type=jnp.float32)
    for c, x_ref in enumerate((x0, x1, x2, x3)):
        rows = slice(c * length, (c + 1) * length)
        mixed = mixed_ref[rows, :] + x_ref[:length, :].astype(jnp.float32)
        centred = mixed - jnp.mean(mixed, axis=1, keepdims=True)
        squares = jnp.sum(centred * centred, axis=1, keepdims=True)
        embedded = (centred / jnp.sqrt(squares + 0.001)).astype(jnp.bfloat16)
        row_ref[rows, :] = embedded
        if c == 0:
            out_ref[0] = embedded
            ext_ref[:length, :] = embedded
    own = ctxs_ref[x, 4 * length :, :]
    ext_ref[length:, :] = jnp.concatenate([own] * (width // (4 * HEAD)), axis=1)
    for c in range(4):
        weight_ref[c * PAD : (c + 1) * PAD, :] = ctxs_ref[lax.rem(x + c, 4), 4 * length :, :LANES].astype(jnp.float32)


def pairs_kernel(row_ref, weight_ref, near_ref, far_ref, out_ref):
    x = lax.axis_index("x")
    y = lax.axis_index("y")
    n = LANES
    me = x * 4 + y
    near = x * 4 + lax.rem(y + 1, 4)
    far = x * 4 + lax.rem(y + 2, 4)
    has_far = jnp.logical_or(y == 0, y == 3)
    cols = jnp.concatenate([near_ref[:n, :], far_ref[:n, :], row_ref[:n, :]], axis=0)
    similar = lax.dot_general(row_ref[...], cols, (((1,), (1,)), ((), ())), preferred_element_type=jnp.float32)
    row_weight = [weight_ref[c * PAD : c * PAD + 1, :] for c in range(4)]
    col_weight = [r[n : n + 1, :n].astype(jnp.float32) for r in (near_ref, far_ref)] + [row_weight[0]]
    down = [jnp.transpose(jnp.broadcast_to(w, (n, n))) for w in row_weight]
    row_sum = [jnp.sum(w, axis=1, keepdims=True) for w in row_weight]
    col_sum = [jnp.sum(w, axis=1, keepdims=True) for w in col_weight]
    col_sum[1] = jnp.where(has_far, col_sum[1], 1.0)
    dest = lax.broadcasted_iota(jnp.int32, (16, LANES), 0)
    lane = lax.broadcasted_iota(jnp.int32, (16, LANES), 1)
    total = jnp.zeros((16, LANES), jnp.float32)
    for j, other in enumerate((near, far, me)):
        w_col = col_weight[j]
        for c in range(4):
            block = similar[c * n : (c + 1) * n, j * n : (j + 1) * n]
            best_col = jnp.max(jnp.where(w_col > 0, block, -4.0), axis=1, keepdims=True)
            best_row = jnp.max(jnp.where(down[c] > 0, block, -4.0), axis=0, keepdims=True)
            forward = jnp.sum(best_col * down[c][:, :1], axis=0, keepdims=True) / row_sum[c]
            backward = jnp.sum(best_row * w_col, axis=1, keepdims=True) / col_sum[j]
            utility = 0.5 * (forward + backward)
            mate = lax.rem(x + c, 4) * 4 + y
            here = jnp.logical_and(dest == other, lane == mate)
            if j < 2:
                here = jnp.logical_or(here, jnp.logical_and(dest == mate, lane == other))
            if j == 1:
                here = jnp.logical_and(here, has_far)
            total = total + jnp.where(here, jnp.broadcast_to(utility, total.shape), 0.0)
    for p in range(16):
        out_ref[p] = jnp.broadcast_to(total[p : p + 1], (8, LANES))


def finish_kernel(got_ref, pair_ref, mean_ref):
    me = lax.axis_index("x") * 4 + lax.axis_index("y")
    total = got_ref[0]
    for p in range(1, 16):
        total = total + got_ref[p]
    lane = lax.broadcasted_iota(jnp.int32, total.shape, 1)
    pair_ref[...] = total[:1, :16]
    rest = jnp.where(jnp.logical_and(lane < 16, lane != me), total, 0.0)
    mean_ref[...] = (jnp.sum(rest, axis=1, keepdims=True) / 15)[:1]


def call(kernel, ins, outs, *args, scratch=(), mebibytes=20):
    return pl.pallas_call(
        kernel,
        in_specs=ins,
        out_specs=tuple(VMEM for _ in outs) if len(outs) > 1 else VMEM,
        out_shape=outs if len(outs) > 1 else outs[0],
        scratch_shapes=list(scratch),
        compiler_params=params(mebibytes),
    )(*args)


def shift(size, by):
    return [((i + by) % size, i) for i in range(size)]


def windows():
    groups = []
    for z in range(8):
        for core in range(2):
            for run in range(2):
                start = 4 * run + 2 * core + z % 2
                ys = sorted(((start + i) % 8 for i in range(4)), key=lambda y: y % 4)
                groups.append(
                    [(((y // 4 * 8 + z) * 2 + core) * 4 + x) * 4 + y % 4 for x in range(4) for y in ys]
                )
    return groups


def spread(chunks):
    axes = ("yh", "z", "core", "x", "y")
    return lax.all_to_all(chunks, axes, split_axis=0, concat_axis=0, tiled=True, axis_index_groups=windows())


def shards(layer_input, token_ids, lengths, idf_table, query_weight, key_weight, value_weight, output_weight):
    _, length, width = layer_input.shape
    depth = query_weight.shape[0]
    half = width // 2
    bf16, f32 = jnp.bfloat16, jnp.float32
    chunks, extended = call(
        prepare_kernel,
        [SMEM] + [pl.BlockSpec(memory_space=pltpu.HBM)] * 5,
        (
            jax.ShapeDtypeStruct((16, depth, 3 * LANES + half), bf16),
            jax.ShapeDtypeStruct((length + PAD, width), bf16),
        ),
        lengths, layer_input, query_weight, key_weight, value_weight, output_weight,
        scratch=[pltpu.VMEM((depth, width), bf16)] * 4 + [pltpu.SemaphoreType.DMA((5,))],
        mebibytes=63,
    )
    weights = spread(chunks)
    others = [lax.ppermute(extended, "x", shift(4, k)) for k in (1, 2, 3)]
    positions = jnp.arange(length, dtype=jnp.int32)
    valid = positions[None, :] < lengths[:, None]
    token_weight = (jnp.take(idf_table, token_ids, axis=0) * valid.astype(f32)).astype(bf16)
    weights, others, token_weight = lax.optimization_barrier((weights, others, token_weight))
    near_half = weights.reshape(width, 3 * LANES + half)
    far_half = lax.ppermute(near_half, "core", [(0, 1), (1, 0)])
    contexts = call(
        attend_kernel,
        [VMEM] * 7,
        (jax.ShapeDtypeStruct((4, 4 * length + PAD, 4 * HEAD), bf16),),
        extended, *others, near_half, far_half, token_weight,
    )
    contexts = lax.all_to_all(contexts, "x", split_axis=0, concat_axis=0, tiled=True)
    embedded, own, row, weights = call(
        embed_kernel,
        [VMEM] * 7,
        (
            jax.ShapeDtypeStruct((1, length, width), bf16),
            jax.ShapeDtypeStruct((length + PAD, width), bf16),
            jax.ShapeDtypeStruct((4 * length, width), bf16),
            jax.ShapeDtypeStruct((4 * PAD, LANES), f32),
        ),
        contexts, extended, *others, near_half, far_half,
        scratch=(pltpu.VMEM((4 * length, width), bf16), pltpu.VMEM((4 * length, width), f32)),
    )
    near = lax.ppermute(own, "y", shift(4, 1))
    far = lax.ppermute(own, "y", [(2, 0), (1, 3)])
    known = call(
        pairs_kernel, [VMEM] * 4, (jax.ShapeDtypeStruct((16, 8, LANES), f32),), row, weights, near, far
    )
    known = lax.all_to_all(known, ("x", "y"), split_axis=0, concat_axis=0, tiled=True)
    pair, mean = call(
        finish_kernel,
        [VMEM],
        (jax.ShapeDtypeStruct((1, 16), f32), jax.ShapeDtypeStruct((1, 1), f32)),
        known,
    )
    return embedded, pair, mean.reshape(1)


def solution(mesh):
    fine = Mesh(np.asarray(mesh.devices).reshape(2, 8, 2, 4, 4), ("yh", "z", "core", "x", "y"))
    src = ("yh", "z", "core")
    cand = ("x", "y")
    in_specs = (
        P(src + cand, None, None),
        P(src + cand, None),
        P(src + cand),
        P(src),
        P(cand, None),
        P(cand, None),
        P(cand, None),
        P(cand, None),
    )
    out_specs = (P(src + cand, None, None), P(src + cand, None), P(src + cand))
    return jax.shard_map(shards, mesh=fine, in_specs=in_specs, out_specs=out_specs, check_vma=False)
```

time: 110 us -> 109 us (level)
  blocking collectives: 12.6 us -> 31.6 us
  starting transfers between devices: 41.8 us -> 29.2 us
  waiting for transfers between devices: 43.7 us -> 35.9 us
    ppermute x3, waiting for transfers between devices: 0.01 us -> 21.5 us  [shards(): others = [lax.ppermute(extended, 'x', shift(4, k)) for k in (1, 2, 3)]]
    all_to_all x0 -> x1, blocking collectives: none -> 18.4 us  [shards(): lax.all_to_all(contexts, 'x', split_axis=0, concat_axis=0, tiled=True)]
    all_to_all x3 -> x1, waiting for transfers between devices: 14.2 us -> 0.01 us  [spread(): lax.all_to_all(chunks, axes, split_axis=0, concat_axis=0, tiled=True, axi...]
    ppermute x3 -> x0, waiting for transfers between devices: 13.5 us -> none  [shards(): lax.ppermute(output_weight, ('yh', 'y'), shift(8, k))]
    ppermute x3 -> x0, starting transfers between devices: 9.42 us -> none  [shards(): lax.ppermute(output_weight, ('yh', 'y'), shift(8, k))]
    all_to_all x3 -> x1, starting transfers between devices: 15.5 us -> 9.02 us  [spread(): lax.all_to_all(chunks, axes, split_axis=0, concat_axis=0, tiled=True, axi...]
    ppermute x1, waiting for transfers between devices: 9.52 us -> 6.21 us  [shards(): far = lax.ppermute(own, 'y', [(2, 0), (1, 3)])]
    ppermute x1, starting transfers between devices: 1.94 us -> 5.24 us  [shards(): near = lax.ppermute(own, 'y', shift(4, 1))]
  transfers between devices with their start and end apart: 12 -> 7, of which waited for: 6 -> 5; matrix products, arithmetic and copies ran while one was open for 1% -> 1% of each run, Pallas kernels for 0% -> 0%
where the time goes in v3:
time: 109 us; the launch traced here: 108 us
  waiting for transfers between devices  35.9 us (33%)
  blocking collectives  31.6 us (29%)
  starting transfers between devices  29.2 us (27%)
  Pallas kernels  8.69 us (8%)
  between operations  1.48 us (1%)
  local copies, waits for them, and re-layouts  1.17 us (1%)
    ppermute x3, waiting for transfers between devices, shards(): others = [lax.ppermute(extended, 'x', shift(4, k)) for k in (1, 2, 3)]  21.5 us
    all_to_all x1, blocking collectives, shards(): lax.all_to_all(contexts, 'x', split_axis=0, concat_axis=0, tiled=True)  18.4 us
    all_to_all x1, blocking collectives, shards(): lax.all_to_all(known, ('x', 'y'), split_axis=0, concat_axis=0, tiled=True)  13.2 us
    ppermute x3, starting transfers between devices, shards(): others = [lax.ppermute(extended, 'x', shift(4, k)) for k in (1, 2, 3)]  11.8 us
    all_to_all x1, starting transfers between devices, spread(): lax.all_to_all(chunks, axes, split_axis=0, concat_axis=0, tiled=True, axi...  9.02 us
    pallas_call x5, Pallas kernels, call(): pl.pallas_call(kernel, in_specs=ins, out_specs=tuple((VMEM for _ in outs)...  8.69 us
    ppermute x1, waiting for transfers between devices, shards(): far = lax.ppermute(own, 'y', [(2, 0), (1, 3)])  6.21 us
    ppermute x1, starting transfers between devices, shards(): near = lax.ppermute(own, 'y', shift(4, 1))  5.24 us
  transfers between devices with their start and end apart: 7, of which 5 were waited for; matrix products, arithmetic and copies ran while one was open for 1% of the time, Pallas kernels for 0%

profile of v3, /device:TPU:448, one launch (start us, length us, event | category | flops | bytes accessed | tf_op | source)
XLA Modules:
  0.0 108.1 jit_solution(13472682841138226363)
XLA Ops:
  0.6 0.0 copy-start
  1.3 2.6 %shard_map.103 = (bf16[16,64,896]{2,1,0:T(8,128)(2,1)}, bf16[144,1024]{1,0:T(8,128)(2,1)}) custom-call(s32[1]{0:T(128)} %copy.11.lengths_ref, bf16[1,128,1024]{2,1,0:T(8,128)(2,1)} %x_hbm.1, bf16[64,1024]{1,0:T(8,128)(2,1)} %q_hbm.1, bf16[64,1024]{1,0:T(8,128)(2,1)} %k_hbm.1, bf16[64,1024]{1,0:T(8,128)(2,1)} %v_hbm.1, bf16[64,1024]{1,0:T(8,128)(2,1)} %o_hbm.1), custom_call_target="tpu_custom_call" | custom-call | tf_op jit(solution)/shard_map/pallas_call | solution.py:164
  4.0 0.0 copy-start.2
  4.0 9.0 %all-to-all-start = ((bf16[16,64,896]{2,1,0:T(8,128)(2,1)}), bf16[16,64,896]{2,1,0:T(8,128)(2,1)S(1)}, u32[]{:S(2)}, u32[]{:S(2)}) async-start(bf16[16,64,896]{2,1,0:T(8,128)(2,1)} %get-tuple-element.17), calls=%async_computation | async-start | bytes 3670016 | tf_op jit(solution)/shard_map/all_to_all | solution.py:193
  13.0 3.8 %collective-permute-start.2 = (bf16[144,1024]{1,0:T(8,128)(2,1)S(1)}, bf16[144,1024]{1,0:T(8,128)(2,1)S(1)}, u32[]{:S(2)}, u32[]{:S(2)}) collective-permute-start(bf16[144,1024]{1,0:T(8,128)(2,1)S(1)} %copy-done.1), channel_id=1, source_target_pairs={{12,0},{0,4},{4,8},{8,12},{13,1},{1,5},{5,9},{9,13},{14,2},{2,6},{... | collective-permute-start | bytes 884744 | tf_op jit(solution)/shard_map/ppermute | solution.py:213
  16.9 4.6 %collective-permute-start.1 = (bf16[144,1024]{1,0:T(8,128)(2,1)S(1)}, bf16[144,1024]{1,0:T(8,128)(2,1)S(1)}, u32[]{:S(2)}, u32[]{:S(2)}) collective-permute-start(bf16[144,1024]{1,0:T(8,128)(2,1)S(1)} %copy-done.1), channel_id=1, source_target_pairs={{8,0},{12,4},{0,8},{4,12},{9,1},{13,5},{1,9},{5,13},{10,2},{14,6},... | collective-permute-start | bytes 884744 | tf_op jit(solution)/shard_map/ppermute | solution.py:213
  21.5 3.4 %collective-permute-start = (bf16[144,1024]{1,0:T(8,128)(2,1)S(1)}, bf16[144,1024]{1,0:T(8,128)(2,1)S(1)}, u32[]{:S(2)}, u32[]{:S(2)}) collective-permute-start(bf16[144,1024]{1,0:T(8,128)(2,1)S(1)} %copy-done.1), channel_id=1, source_target_pairs={{4,0},{8,4},{12,8},{0,12},{5,1},{9,5},{13,9},{1,13},{6,2},{10,6},{... | collective-permute-start | bytes 884744 | tf_op jit(solution)/shard_map/ppermute | solution.py:213
  24.9 1.1 %gather_fusion = bf16[128]{0:T(256)(128)(2,1)S(1)} fusion(f32[50265]{0:T(1024)S(1)} %copy-done, s32[1024]{0:T(1024)S(1)} %pad_clamp_fusion), kind=kCustom, calls=%fused_computation | custom fusion | bytes 1024 | tf_op jit(solution)/shard_map/jit(_take)/gather | solution.py:216
  26.1 15.8 %collective-permute-done.2.x3 = bf16[144,1024]{1,0:T(8,128)(2,1)S(1)} collective-permute-done((bf16[144,1024]{1,0:T(8,128)(2,1)S(1)}, bf16[144,1024]{1,0:T(8,128)(2,1)S(1)}, u32[]{:S(2)}, u32[]{:S(2)}) %collective-permute-start.2) | collective-permute-done | bytes 294944 | tf_op jit(solution)/shard_map/ppermute | solution.py:213
  41.9 5.6 %collective-permute-done.1.x2 = bf16[144,1024]{1,0:T(8,128)(2,1)S(1)} collective-permute-done((bf16[144,1024]{1,0:T(8,128)(2,1)S(1)}, bf16[144,1024]{1,0:T(8,128)(2,1)S(1)}, u32[]{:S(2)}, u32[]{:S(2)}) %collective-permute-start.1) | collective-permute-done | bytes 294944 | tf_op jit(solution)/shard_map/ppermute | solution.py:213
  47.5 0.0 collective-permute-done.x1
  47.6 0.0 all-to-all-done
  47.6 1.9 %collective-permute-start.3 = (bf16[1024,896]{1,0:T(8,128)(2,1)S(1)}, bf16[1024,896]{1,0:T(8,128)(2,1)S(1)}, u32[]{:S(2)}, u32[]{:S(2)}) collective-permute-start(bf16[1024,896]{1,0:T(8,128)(2,1)S(1)} %bitcast.8), channel_id=1, source_target_pairs={{0,16},{16,0},{1,17},{17,1},{2,18},{18,2},{3,19},{19,3},{4,20},{20... | collective-permute-start | bytes 5505032 | tf_op jit(solution)/shard_map/ppermute | solution.py:219
  49.5 3.8 %collective-permute-done.3.wb_ref = bf16[1024,896]{1,0:T(8,128)(2,1)S(1)} collective-permute-done((bf16[1024,896]{1,0:T(8,128)(2,1)S(1)}, bf16[1024,896]{1,0:T(8,128)(2,1)S(1)}, u32[]{:S(2)}, u32[]{:S(2)}) %collective-permute-start.3) | collective-permute-done | bytes 1835040 | tf_op jit(solution)/shard_map/ppermute | solution.py:219
  53.2 1.9 %shard_map.104 = bf16[4,528,256]{2,1,0:T(8,128)(2,1)S(1)} custom-call(bf16[144,1024]{1,0:T(8,128)(2,1)S(1)} %copy-done.1, bf16[144,1024]{1,0:T(8,128)(2,1)S(1)} %collective-permute-done.x1, bf16[144,1024]{1,0:T(8,128)(2,1)S(1)} %collective-permute-done.1.x2, bf16[144,1024]{1,0:T(8,128)(2,1)S(1)} %collective-permute-done.2.x3, bf16[1024,896]{1,0:T(8,128)(2,1)S(1)} %bitcast.9, ...), custom_call_target="tpu_custom_call" | custom-call | tf_op jit(solution)/shard_map/pallas_call | solution.py:164
  55.2 18.4 %all_to_all.15.ctxs_ref = bf16[4,528,256]{2,1,0:T(8,128)(2,1)S(1)} all-to-all(bf16[4,528,256]{2,1,0:T(8,128)(2,1)S(1)} %shard_map.104), channel_id=1, replica_groups=mesh['yh'=2,'z'=8,'core'=2,'x'=4,'y'=4] {'x'}, dimensions={0} | all-to-all | bytes 2162688 | tf_op jit(solution)/shard_map/all_to_all | solution.py:226
  73.6 2.6 %shard_map.105 = (bf16[1,128,1024]{2,1,0:T(8,128)(2,1)}, bf16[144,1024]{1,0:T(8,128)(2,1)S(1)}, bf16[512,1024]{1,0:T(8,128)(2,1)S(1)}, f32[64,128]{1,0:T(8,128)S(1)}) custom-call(bf16[4,528,256]{2,1,0:T(8,128)(2,1)S(1)} %all_to_all.15.ctxs_ref, bf16[144,1024]{1,0:T(8,128)(2,1)S(1)} %copy-done.1, bf16[144,1024]{1,0:T(8,128)(2,1)S(1)} %collective-permute-done.x1, ...), custom_call_target="tpu_custom_call" | custom-call | tf_op jit(solution)/shard_map/pallas_call | solution.py:164
  76.2 1.3 %collective-permute-start.5 = (bf16[144,1024]{1,0:T(8,128)(2,1)S(1)}, bf16[144,1024]{1,0:T(8,128)(2,1)S(1)}, u32[]{:S(2)}, u32[]{:S(2)}) collective-permute-start(bf16[144,1024]{1,0:T(8,128)(2,1)S(1)} %get-tuple-element.26), channel_id=1, source_target_pairs={{2,0},{1,3},{6,4},{5,7},{10,8},{9,11},{14,12},{13,15},{18,16},{17,... | collective-permute-start | bytes 884744 | tf_op jit(solution)/shard_map/ppermute | solution.py:240
  77.4 5.2 %collective-permute-start.4 = (bf16[144,1024]{1,0:T(8,128)(2,1)S(1)}, bf16[144,1024]{1,0:T(8,128)(2,1)S(1)}, u32[]{:S(2)}, u32[]{:S(2)}) collective-permute-start(bf16[144,1024]{1,0:T(8,128)(2,1)S(1)} %get-tuple-element.26), channel_id=1, source_target_pairs={{1,0},{2,1},{3,2},{0,3},{5,4},{6,5},{7,6},{4,7},{9,8},{10,9},{11,1... | collective-permute-start | bytes 884744 | tf_op jit(solution)/shard_map/ppermute | solution.py:239
  82.7 6.2 %collective-permute-done.5.far_ref = bf16[144,1024]{1,0:T(8,128)(2,1)S(1)} collective-permute-done((bf16[144,1024]{1,0:T(8,128)(2,1)S(1)}, bf16[144,1024]{1,0:T(8,128)(2,1)S(1)}, u32[]{:S(2)}, u32[]{:S(2)}) %collective-permute-start.5) | collective-permute-done | bytes 294944 | tf_op jit(solution)/shard_map/ppermute | solution.py:240
  88.9 4.4 %collective-permute-done.4.near_ref = bf16[144,1024]{1,0:T(8,128)(2,1)S(1)} collective-permute-done((bf16[144,1024]{1,0:T(8,128)(2,1)S(1)}, bf16[144,1024]{1,0:T(8,128)(2,1)S(1)}, u32[]{:S(2)}, u32[]{:S(2)}) %collective-permute-start.4) | collective-permute-done | bytes 294944 | tf_op jit(solution)/shard_map/ppermute | solution.py:239
  93.3 0.9 shard_map.106
  94.3 13.2 %all_to_all.16.got_ref = f32[16,8,128]{2,1,0:T(8,128)S(1)} all-to-all(f32[16,8,128]{2,1,0:T(8,128)S(1)} %shard_map.106), channel_id=1, replica_groups=mesh['yh'=2,'z'=8,'core'=2,'x'=4,'y'=4] {'x','y'}, dimensions={0} | all-to-all | bytes 131072 | tf_op jit(solution)/shard_map/all_to_all | solution.py:244
  107.5 0.6 shard_map.107
  (7 shorter events, 0.0 us)
Async XLA Ops:
  0.6 24.3 %copy-start = (f32[50265]{0:T(1024)S(1)}, f32[50265]{0:T(1024)}, u32[]{:S(2)}) copy-start(f32[50265]{0:T(1024)} %param.11) | copy-start | bytes 603184
  4.0 9.1 %copy-start.1 = (bf16[144,1024]{1,0:T(8,128)(2,1)S(1)}, bf16[144,1024]{1,0:T(8,128)(2,1)}, u32[]{:S(2)}) copy-start(bf16[144,1024]{1,0:T(8,128)(2,1)} %get-tuple-element.16.x0) | copy-start | bytes 884740
  4.0 20.9 %copy-start.2 = (s32[1,128]{1,0:T(1,128)S(1)}, s32[1,128]{1,0:T(1,128)}, u32[]{:S(2)}) copy-start(s32[1,128]{1,0:T(1,128)} %param.9) | copy-start | bytes 1540
  4.0 43.5 %all-to-all-start = ((bf16[16,64,896]{2,1,0:T(8,128)(2,1)}), bf16[16,64,896]{2,1,0:T(8,128)(2,1)S(1)}, u32[]{:S(2)}, u32[]{:S(2)}) async-start(bf16[16,64,896]{2,1,0:T(8,128)(2,1)} %get-tuple-element.17), calls=%async_computation | async-start | bytes 3670016 | tf_op jit(solution)/shard_map/all_to_all | solution.py:193
  13.0 28.9 %collective-permute-start.2 = (bf16[144,1024]{1,0:T(8,128)(2,1)S(1)}, bf16[144,1024]{1,0:T(8,128)(2,1)S(1)}, u32[]{:S(2)}, u32[]{:S(2)}) collective-permute-start(bf16[144,1024]{1,0:T(8,128)(2,1)S(1)} %copy-done.1), channel_id=1, source_target_pairs={{12,0},{0,4},{4,8},{8,12},{13,1},{1,5},{5,9},{9,13},{14,2},{2,6},{... | collective-permute-start | bytes 884744 | tf_op jit(solution)/shard_map/ppermute | solution.py:213
  16.9 30.7 %collective-permute-start.1 = (bf16[144,1024]{1,0:T(8,128)(2,1)S(1)}, bf16[144,1024]{1,0:T(8,128)(2,1)S(1)}, u32[]{:S(2)}, u32[]{:S(2)}) collective-permute-start(bf16[144,1024]{1,0:T(8,128)(2,1)S(1)} %copy-done.1), channel_id=1, source_target_pairs={{8,0},{12,4},{0,8},{4,12},{9,1},{13,5},{1,9},{5,13},{10,2},{14,6},... | collective-permute-start | bytes 884744 | tf_op jit(solution)/shard_map/ppermute | solution.py:213
  21.5 26.1 %collective-permute-start = (bf16[144,1024]{1,0:T(8,128)(2,1)S(1)}, bf16[144,1024]{1,0:T(8,128)(2,1)S(1)}, u32[]{:S(2)}, u32[]{:S(2)}) collective-permute-start(bf16[144,1024]{1,0:T(8,128)(2,1)S(1)} %copy-done.1), channel_id=1, source_target_pairs={{4,0},{8,4},{12,8},{0,12},{5,1},{9,5},{13,9},{1,13},{6,2},{10,6},{... | collective-permute-start | bytes 884744 | tf_op jit(solution)/shard_map/ppermute | solution.py:213
  47.6 5.7 %collective-permute-start.3 = (bf16[1024,896]{1,0:T(8,128)(2,1)S(1)}, bf16[1024,896]{1,0:T(8,128)(2,1)S(1)}, u32[]{:S(2)}, u32[]{:S(2)}) collective-permute-start(bf16[1024,896]{1,0:T(8,128)(2,1)S(1)} %bitcast.8), channel_id=1, source_target_pairs={{0,16},{16,0},{1,17},{17,1},{2,18},{18,2},{3,19},{19,3},{4,20},{20... | collective-permute-start | bytes 5505032 | tf_op jit(solution)/shard_map/ppermute | solution.py:219
  76.2 12.7 %collective-permute-start.5 = (bf16[144,1024]{1,0:T(8,128)(2,1)S(1)}, bf16[144,1024]{1,0:T(8,128)(2,1)S(1)}, u32[]{:S(2)}, u32[]{:S(2)}) collective-permute-start(bf16[144,1024]{1,0:T(8,128)(2,1)S(1)} %get-tuple-element.26), channel_id=1, source_target_pairs={{2,0},{1,3},{6,4},{5,7},{10,8},{9,11},{14,12},{13,15},{18,16},{17,... | collective-permute-start | bytes 884744 | tf_op jit(solution)/shard_map/ppermute | solution.py:240
  77.4 15.9 %collective-permute-start.4 = (bf16[144,1024]{1,0:T(8,128)(2,1)S(1)}, bf16[144,1024]{1,0:T(8,128)(2,1)S(1)}, u32[]{:S(2)}, u32[]{:S(2)}) collective-permute-start(bf16[144,1024]{1,0:T(8,128)(2,1)S(1)} %get-tuple-element.26), channel_id=1, source_target_pairs={{1,0},{2,1},{3,2},{0,3},{5,4},{6,5},{7,6},{4,7},{9,8},{10,9},{11,1... | collective-permute-start | bytes 884744 | tf_op jit(solution)/shard_map/ppermute | solution.py:239

commit v4 on v1

--- a/solution.py
+++ b/solution.py
@@ -15,62 +15,96 @@
 SMEM = pl.BlockSpec(memory_space=pltpu.SMEM)
 
 
-def params():
-    return pltpu.CompilerParams(vmem_limit_bytes=40 * 1024 * 1024)
-
-
-def prepare_kernel(lengths_ref, x_ref, q_ref, k_ref, v_ref, chunk_ref, ext_ref):
+def params(mebibytes):
+    return pltpu.CompilerParams(vmem_limit_bytes=mebibytes * 1024 * 1024)
+
+
+def chunks_kernel(q_hbm, k_hbm, v_hbm, chunk_hbm, q_ref, k_ref, v_ref, piece_ref, sems, out_sems):
     core = lax.axis_index("core")
-    rows = x_ref.shape[1]
+    copies = []
+    for n, (far, near) in enumerate(((q_hbm, q_ref), (k_hbm, k_ref), (v_hbm, v_ref))):
+        copies.append(pltpu.make_async_copy(far, near, sems.at[n]))
+    for copy in copies:
+        copy.start()
+    for copy in copies:
+        copy.wait()
+    sends = []
     for block in range(4):
         at = pl.multiple_of(block * 2 * LANES + core * LANES, LANES)
         for n, ref in enumerate((q_ref, k_ref, v_ref)):
-            piece = ref[:, pl.ds(at, LANES)]
-            for y in range(4):
-                chunk_ref[block * 4 + y, :, n * LANES : (n + 1) * LANES] = piece
+            piece_ref[block, :, n * LANES : (n + 1) * LANES] = ref[:, pl.ds(at, LANES)]
+        for y in range(4):
+            p = block * 4 + y
+            send = pltpu.make_async_copy(piece_ref.at[block], chunk_hbm.at[p], out_sems.at[p])
+            send.start()
+            sends.append(send)
+    for send in sends:
+        send.wait()
+
+
+def extend_kernel(x_ref, used_ref, o_ref, ext_ref, half_ref):
+    half = half_ref.shape[0]
+    half_ref[...] = o_ref[pl.ds(pl.multiple_of(lax.axis_index("core") * half, half), half), :]
+    rows = x_ref.shape[1]
     ext_ref[:rows, :] = x_ref[0]
-    length = lengths_ref[0].astype(jnp.float32)
-    ext_ref[rows:, :] = jnp.full((PAD, ext_ref.shape[1]), length, jnp.float32).astype(jnp.bfloat16)
-
-
-def attend_kernel(x0, x1, x2, x3, wa_ref, wb_ref, o0, o1, o2, o3, part_ref, wo_ref):
+    used = jnp.concatenate([used_ref[...]] * (ext_ref.shape[1] // LANES), axis=1)
+    ext_ref[rows:, :] = jnp.broadcast_to(used, (PAD, ext_ref.shape[1])).astype(jnp.bfloat16)
+
+
+def heads(tokens, used, w_ref):
+    length = LANES
+    first = lax.broadcasted_iota(jnp.int32, (length, LANES), 1) < HEAD
+    position = lax.broadcasted_iota(jnp.int32, (2 * length, length), 1).astype(jnp.float32)
+    qkv = jnp.dot(tokens, w_ref[...], preferred_element_type=jnp.float32).astype(jnp.bfloat16)
+    out = []
+    for c in range(4):
+        rows = slice(c * length, (c + 1) * length)
+        q = qkv[rows, :LANES]
+        key = qkv[rows, LANES : 2 * LANES]
+        v = qkv[rows, 2 * LANES :]
+        zero = jnp.zeros_like(q)
+        both = jnp.concatenate([jnp.where(first, q, zero), jnp.where(first, zero, q)], axis=0)
+        scores = lax.dot_general(
+            both, key, (((1,), (1,)), ((), ())), preferred_element_type=jnp.float32
+        ) * (HEAD ** -0.5)
+        scores = jnp.where(position < used[c], scores, -1e9)
+        expo = jnp.exp(scores - jnp.max(scores, axis=1, keepdims=True))
+        probs = (expo / jnp.sum(expo, axis=1, keepdims=True)).astype(jnp.bfloat16)
+        ctx = jnp.dot(probs, v, preferred_element_type=jnp.float32)
+        out.append(jnp.where(first, ctx[:length], ctx[length:]).astype(jnp.bfloat16))
+    return out
+
+
+def row_of(refs):
+    length = LANES
+    tokens = jnp.concatenate([r[:length, :] for r in refs], axis=0)
+    return tokens, [r[length : length + 1, :length].astype(jnp.float32) for r in refs]
+
+
+def near_kernel(x0, x1, x2, x3, w_ref, out_ref):
+    tokens, used = row_of((x0, x1, x2, x3))
+    for c, context in enumerate(heads(tokens, used, w_ref)):
+        out_ref[c * LANES : (c + 1) * LANES, :] = context
+
+
+def far_kernel(x0, x1, x2, x3, w_ref, near_ref, own_ref, mine_ref, mate_ref, part_ref, wo_ref):
     core = lax.axis_index("core")
     x = lax.axis_index("x")
     y = lax.axis_index("y")
     length = LANES
-    for k, ref in enumerate((o0, o1, o2, o3)):
-        at = pl.multiple_of(lax.rem(y + k, 4) * HEAD, HEAD)
-        wo_ref[pl.ds(at, HEAD), :] = ref[...]
-    xs = (x0, x1, x2, x3)
-    tokens = jnp.concatenate([r[:length, :] for r in xs], axis=0)
-    lane = lax.broadcasted_iota(jnp.int32, (length, LANES), 1)
-    first = lane < HEAD
-    lane2 = lax.broadcasted_iota(jnp.int32, (2 * length, length), 1).astype(jnp.float32)
-    contexts = []
-    for w_ref in (wa_ref, wb_ref):
-        qkv = jnp.dot(tokens, w_ref[...], preferred_element_type=jnp.float32).astype(jnp.bfloat16)
-        own = []
-        for c in range(4):
-            rows = slice(c * length, (c + 1) * length)
-            q = qkv[rows, :LANES]
-            key = qkv[rows, LANES : 2 * LANES]
-            v = qkv[rows, 2 * LANES :]
-            zero = jnp.zeros_like(q)
-            both = jnp.concatenate([jnp.where(first, q, zero), jnp.where(first, zero, q)], axis=0)
-            scores = lax.dot_general(
-                both, key, (((1,), (1,)), ((), ())), preferred_element_type=jnp.float32
-            ) * (HEAD ** -0.5)
-            used = xs[c][length : length + 1, :length].astype(jnp.float32)
-            scores = jnp.where(lane2 < used, scores, -1e9)
-            expo = jnp.exp(scores - jnp.max(scores, axis=1, keepdims=True))
-            probs = (expo / jnp.sum(expo, axis=1, keepdims=True)).astype(jnp.bfloat16)
-            ctx = jnp.dot(probs, v, preferred_element_type=jnp.float32)
-            own.append(jnp.where(first, ctx[:length], ctx[length:]).astype(jnp.bfloat16))
-        contexts.append(jnp.concatenate(own, axis=0))
+    half = HEAD // 2
+    wo_ref[pl.ds(pl.multiple_of(y * HEAD, HEAD), HEAD), :] = own_ref[...]
+    for side, ref in ((core, mine_ref), (1 - core, mate_ref)):
+        at = pl.multiple_of(lax.rem(y + 1 + 2 * side, 4) * HEAD, HEAD)
+        wo_ref[pl.ds(at, HEAD), :] = ref[:HEAD, :]
+        at = pl.multiple_of(lax.rem(y + 2, 4) * HEAD + side * half, half)
+        wo_ref[pl.ds(at, half), :] = ref[HEAD:, :]
+    tokens, used = row_of((x0, x1, x2, x3))
+    far = jnp.concatenate(heads(tokens, used, w_ref), axis=0)
     wo_a = wo_ref[pl.ds(pl.multiple_of(core * LANES, LANES), LANES), :]
     wo_b = wo_ref[pl.ds(pl.multiple_of((1 - core) * LANES, LANES), LANES), :]
-    part = jnp.dot(contexts[0], wo_a, preferred_element_type=jnp.float32)
-    part = part + jnp.dot(contexts[1], wo_b, preferred_element_type=jnp.float32)
+    part = jnp.dot(near_ref[...], wo_a, preferred_element_type=jnp.float32)
+    part = part + jnp.dot(far, wo_b, preferred_element_type=jnp.float32)
     for c in range(4):
         part_ref[lax.rem(x + c, 4)] = part[c * length : (c + 1) * length].astype(jnp.bfloat16)
 
@@ -146,51 +180,96 @@
     mean_ref[...] = (jnp.sum(rest, axis=1, keepdims=True) / 15)[:1]
 
 
-def call(kernel, ins, outs, *args, scratch=()):
+def call(kernel, ins, outs, *args, scratch=(), mebibytes=20):
     return pl.pallas_call(
         kernel,
         in_specs=ins,
         out_specs=tuple(VMEM for _ in outs) if len(outs) > 1 else VMEM,
         out_shape=outs if len(outs) > 1 else outs[0],
         scratch_shapes=list(scratch),
-        compiler_params=params(),
+        compiler_params=params(mebibytes),
     )(*args)
 
 
 def shift(size, by):
     return [((i + by) % size, i) for i in range(size)]
+
+
+def sideways():
+    pairs = []
+    for y in range(8):
+        for core in range(2):
+            source = (y + (1 if core == 0 else 7)) % 8
+            pairs.append(((source // 4 * 2 + core) * 4 + source % 4, (y // 4 * 2 + core) * 4 + y % 4))
+    return pairs
+
+
+def windows():
+    groups = []
+    for z in range(8):
+        for core in range(2):
+            for run in range(2):
+                start = 4 * run + 2 * core + z % 2
+                ys = sorted(((start + i) % 8 for i in range(4)), key=lambda y: y % 4)
+                groups.append(
+                    [(((y // 4 * 8 + z) * 2 + core) * 4 + x) * 4 + y % 4 for x in range(4) for y in ys]
+                )
+    return groups
+
+
+def spread(chunks):
+    axes = ("yh", "z", "core", "x", "y")
+    return lax.all_to_all(chunks, axes, split_axis=0, concat_axis=0, tiled=True, axis_index_groups=windows())
 
 
 def shards(layer_input, token_ids, lengths, idf_table, query_weight, key_weight, value_weight, output_weight):
     _, length, width = layer_input.shape
     depth = query_weight.shape[0]
     bf16, f32 = jnp.bfloat16, jnp.float32
-    chunks, extended = call(
-        prepare_kernel,
-        [SMEM] + [VMEM] * 4,
-        (
-            jax.ShapeDtypeStruct((16, depth, 3 * LANES), bf16),
-            jax.ShapeDtypeStruct((length + PAD, width), bf16),
-        ),
-        lengths, layer_input, query_weight, key_weight, value_weight,
-    )
-    near_half = lax.all_to_all(chunks, ("x", "y"), split_axis=0, concat_axis=0, tiled=True)
+    hbm = pl.BlockSpec(memory_space=pltpu.HBM)
+    chunks = pl.pallas_call(
+        chunks_kernel,
+        in_specs=[hbm] * 3,
+        out_specs=hbm,
+        out_shape=jax.ShapeDtypeStruct((16, depth, 3 * LANES), bf16),
+        scratch_shapes=[pltpu.VMEM((depth, width), bf16)] * 3
+        + [
+            pltpu.VMEM((4, depth, 3 * LANES), bf16),
+            pltpu.SemaphoreType.DMA((3,)),
+            pltpu.SemaphoreType.DMA((16,)),
+        ],
+        compiler_params=params(63),
+    )(query_weight, key_weight, value_weight)
+    used = jnp.broadcast_to(lengths.astype(f32)[:, None], (1, LANES))
+    extended, half = call(
+        extend_kernel,
+        [VMEM] * 3,
+        (jax.ShapeDtypeStruct((length + PAD, width), bf16), jax.ShapeDtypeStruct((depth // 2, width), bf16)),
+        layer_input, used, output_weight,
+    )
+    beside = lax.ppermute(output_weight, ("yh", "core", "y"), sideways())
+    across = lax.ppermute(half, ("yh", "y"), shift(8, 2))
+    weights = spread(chunks)
     others = [lax.ppermute(extended, "x", shift(4, k)) for k in (1, 2, 3)]
-    blocks = [lax.ppermute(output_weight, ("yh", "y"), shift(8, k)) for k in (1, 2, 7)]
-    far_half = lax.ppermute(near_half, "core", [(0, 1), (1, 0)])
-    parts = call(
-        attend_kernel,
-        [VMEM] * 10,
-        (jax.ShapeDtypeStruct((4, length, width), bf16),),
-        extended, *others,
-        near_half.reshape(width, 3 * LANES), far_half.reshape(width, 3 * LANES),
-        output_weight, *blocks,
-        scratch=(pltpu.VMEM((4 * HEAD, width), bf16),),
-    )
-    parts = lax.all_to_all(parts, "x", split_axis=0, concat_axis=0, tiled=True)
+    mine = jnp.concatenate([beside, across], axis=0)
     positions = jnp.arange(length, dtype=jnp.int32)
     valid = positions[None, :] < lengths[:, None]
     token_weight = (jnp.take(idf_table, token_ids, axis=0) * valid.astype(f32)).astype(bf16)
+    weights, others, token_weight, mine = lax.optimization_barrier((weights, others, token_weight, mine))
+    near_half = weights.reshape(width, 3 * LANES)
+    far_half = lax.ppermute(near_half, "core", [(0, 1), (1, 0)])
+    mate = lax.ppermute(mine, "core", [(0, 1), (1, 0)])
+    context = call(
+        near_kernel, [VMEM] * 5, (jax.ShapeDtypeStruct((4 * length, 2 * HEAD), bf16),), extended, *others, near_half
+    )
+    parts = call(
+        far_kernel,
+        [VMEM] * 9,
+        (jax.ShapeDtypeStruct((4, length, width), bf16),),
+        extended, *others, far_half, context, output_weight, mine, mate,
+        scratch=(pltpu.VMEM((4 * HEAD, width), bf16),),
+    )
+    parts = lax.all_to_all(parts, "x", split_axis=0, concat_axis=0, tiled=True)
     embedded, own, row = call(
         embed_kernel,
         [VMEM] * 3,

time: 119 us -> 102 us (0.86)
  waiting for transfers between devices: 30 us -> 12.3 us
  starting transfers between devices: 32.7 us -> 43.9 us
  blocking collectives: 42.7 us -> 34 us
  local copies, waits for them, and re-layouts: 4.83 us -> 1.18 us
  Pallas kernels: 6.69 us -> 8.3 us
    all_to_all x1, waiting for transfers between devices: 11.7 us -> 0.01 us  [spread(): lax.all_to_all(chunks, axes, split_axis=0, concat_axis=0, tiled=True, axi...]
    all_to_all x1, blocking collectives: 29.4 us -> 18.8 us  [shards(): parts = lax.all_to_all(parts, 'x', split_axis=0, concat_axis=0, tiled=True)]
    ppermute x3, waiting for transfers between devices: 8.79 us -> 1.67 us  [the longest x1 1.67 us: shards(): across = lax.ppermute(half, ('yh', 'y'), shift(8, 2))]
    all_to_all x1, starting transfers between devices: 3.65 us -> 8.89 us  [spread(): lax.all_to_all(chunks, axes, split_axis=0, concat_axis=0, tiled=True, axi...]
    unnamed x16 -> x8, local copies, waits for them, and re-layouts: 3.68 us -> 0.02 us
    ppermute x3, starting transfers between devices: 9.3 us -> 11.7 us  [the longest x1 5.04 us: shards(): beside = lax.ppermute(output_weight, ('yh', 'core', 'y'), sideways())]
    pallas_call x0 -> x1, Pallas kernels: none -> 2.16 us  [shards(): pl.pallas_call(chunks_kernel, in_specs=[hbm] * 3, out_specs=hbm, out_shap...]
    all_to_all x1, blocking collectives: 13.4 us -> 15.3 us  [shards(): lax.all_to_all(known, ('x', 'y'), split_axis=0, concat_axis=0, tiled=True)]
  transfers between devices with their start and end apart: 11 -> 11, of which waited for: 5 -> 4; matrix products, arithmetic and copies ran while one was open for 1% -> 1% of each run, Pallas kernels for 0% -> 1%
where the time goes in v4:
time: 102 us; the launch traced here: 101 us
  starting transfers between devices  43.9 us (43%)
  blocking collectives  34 us (33%)
  waiting for transfers between devices  12.3 us (12%)
  Pallas kernels  8.3 us (8%)
  between operations  1.52 us (1%)
  local copies, waits for them, and re-layouts  1.18 us (1%)
    all_to_all x1, blocking collectives, shards(): parts = lax.all_to_all(parts, 'x', split_axis=0, concat_axis=0, tiled=True)  18.8 us
    all_to_all x1, blocking collectives, shards(): lax.all_to_all(known, ('x', 'y'), split_axis=0, concat_axis=0, tiled=True)  15.3 us
    ppermute x3, starting transfers between devices, shards(): others = [lax.ppermute(extended, 'x', shift(4, k)) for k in (1, 2, 3)]  11.3 us
    all_to_all x1, starting transfers between devices, spread(): lax.all_to_all(chunks, axes, split_axis=0, concat_axis=0, tiled=True, axi...  8.89 us
    pallas_call x6, Pallas kernels, call(): pl.pallas_call(kernel, in_specs=ins, out_specs=tuple((VMEM for _ in outs)...  6.14 us
    ppermute x1, waiting for transfers between devices, shards(): far = lax.ppermute(own, 'y', [(2, 0), (1, 3)])  6.13 us
    ppermute x1, starting transfers between devices, shards(): near = lax.ppermute(own, 'y', shift(4, 1))  5.21 us
    ppermute x1, starting transfers between devices, shards(): beside = lax.ppermute(output_weight, ('yh', 'core', 'y'), sideways())  5.04 us
  transfers between devices with their start and end apart: 11, of which 4 were waited for; matrix products, arithmetic and copies ran while one was open for 1% of the time, Pallas kernels for 1%

profile of v4, /device:TPU:448, one launch (start us, length us, event | category | flops | bytes accessed | tf_op | source)
XLA Modules:
  0.0 101.2 jit_solution(8760424791996423004)
XLA Ops:
  0.7 2.2 %shard_map.103 = bf16[16,64,384]{2,1,0:T(8,128)(2,1)} custom-call(bf16[64,1024]{1,0:T(8,128)(2,1)} %q_hbm.1, bf16[64,1024]{1,0:T(8,128)(2,1)} %k_hbm.1, bf16[64,1024]{1,0:T(8,128)(2,1)} %v_hbm.1), custom_call_target="tpu_custom_call" | custom-call | tf_op jit(solution)/shard_map/pallas_call | solution.py:230
  2.8 8.9 %all-to-all-start = ((bf16[16,64,384]{2,1,0:T(8,128)(2,1)}), bf16[16,64,384]{2,1,0:T(8,128)(2,1)S(1)}, u32[]{:S(2)}, u32[]{:S(2)}) async-start(bf16[16,64,384]{2,1,0:T(8,128)(2,1)} %shard_map.103), calls=%async_computation | async-start | bytes 1572864 | tf_op jit(solution)/shard_map/all_to_all | solution.py:222
  11.8 5.0 %collective-permute-start.3 = (bf16[64,1024]{1,0:T(8,128)(2,1)S(1)}, bf16[64,1024]{1,0:T(8,128)(2,1)S(1)}, u32[]{:S(2)}, u32[]{:S(2)}) collective-permute-start(bf16[64,1024]{1,0:T(8,128)(2,1)S(1)} %copy-done.2), channel_id=1, source_target_pairs={{1,0},{275,16},{2,1},{16,17},{3,2},{17,18},{256,3},{18,19},{257,25... | collective-permute-start | bytes 393224 | tf_op jit(solution)/shard_map/ppermute | solution.py:250
  17.5 3.4 %collective-permute-start.2 = (bf16[144,1024]{1,0:T(8,128)(2,1)S(1)}, bf16[144,1024]{1,0:T(8,128)(2,1)S(1)}, u32[]{:S(2)}, u32[]{:S(2)}) collective-permute-start(bf16[144,1024]{1,0:T(8,128)(2,1)S(1)} %get-tuple-element.16.x0), channel_id=1, source_target_pairs={{12,0},{0,4},{4,8},{8,12},{13,1},{1,5},{5,9},{9,13},{14,2},{2,6},{... | collective-permute-start | bytes 884744 | tf_op jit(solution)/shard_map/ppermute | solution.py:253
  20.9 4.6 %collective-permute-start.1 = (bf16[144,1024]{1,0:T(8,128)(2,1)S(1)}, bf16[144,1024]{1,0:T(8,128)(2,1)S(1)}, u32[]{:S(2)}, u32[]{:S(2)}) collective-permute-start(bf16[144,1024]{1,0:T(8,128)(2,1)S(1)} %get-tuple-element.16.x0), channel_id=1, source_target_pairs={{8,0},{12,4},{0,8},{4,12},{9,1},{13,5},{1,9},{5,13},{10,2},{14,6},... | collective-permute-start | bytes 884744 | tf_op jit(solution)/shard_map/ppermute | solution.py:253
  25.5 3.4 %collective-permute-start = (bf16[144,1024]{1,0:T(8,128)(2,1)S(1)}, bf16[144,1024]{1,0:T(8,128)(2,1)S(1)}, u32[]{:S(2)}, u32[]{:S(2)}) collective-permute-start(bf16[144,1024]{1,0:T(8,128)(2,1)S(1)} %get-tuple-element.16.x0), channel_id=1, source_target_pairs={{4,0},{8,4},{12,8},{0,12},{5,1},{9,5},{13,9},{1,13},{6,2},{10,6},{... | collective-permute-start | bytes 884744 | tf_op jit(solution)/shard_map/ppermute | solution.py:253
  28.9 4.3 %collective-permute-start.4 = (bf16[32,1024]{1,0:T(8,128)(2,1)S(1)}, bf16[32,1024]{1,0:T(8,128)(2,1)S(1)}, u32[]{:S(2)}, u32[]{:S(2)}) collective-permute-start(bf16[32,1024]{1,0:T(8,128)(2,1)S(1)} %get-tuple-element.17), channel_id=1, source_target_pairs={{2,0},{3,1},{256,2},{257,3},{258,256},{259,257},{0,258},{1,259},{6... | collective-permute-start | bytes 196616 | tf_op jit(solution)/shard_map/ppermute | solution.py:251
  33.2 1.1 %gather_fusion = bf16[128]{0:T(256)(128)(2,1)S(1)} fusion(f32[50265]{0:T(1024)S(1)} %copy-done, s32[1024]{0:T(1024)S(1)} %pad_clamp_fusion), kind=kCustom, calls=%fused_computation | custom fusion | bytes 1024 | tf_op jit(solution)/shard_map/jit(_take)/gather | solution.py:257
  34.4 1.7 %collective-permute-done.4 = bf16[32,1024]{1,0:T(8,128)(2,1)S(1)} collective-permute-done((bf16[32,1024]{1,0:T(8,128)(2,1)S(1)}, bf16[32,1024]{1,0:T(8,128)(2,1)S(1)}, u32[]{:S(2)}, u32[]{:S(2)}) %collective-permute-start.4) | collective-permute-done | bytes 65568 | tf_op jit(solution)/shard_map/ppermute | solution.py:251
  36.1 0.4 collective-permute-done.1.x2
  36.4 1.9 %collective-permute-start.5 = (bf16[1024,384]{1,0:T(8,128)(2,1)S(1)}, bf16[1024,384]{1,0:T(8,128)(2,1)S(1)}, u32[]{:S(2)}, u32[]{:S(2)}) collective-permute-start(bf16[1024,384]{1,0:T(8,128)(2,1)S(1)} %bitcast.9), channel_id=1, source_target_pairs={{0,16},{16,0},{1,17},{17,1},{2,18},{18,2},{3,19},{19,3},{4,20},{20... | collective-permute-start | bytes 2359304 | tf_op jit(solution)/shard_map/ppermute | solution.py:260
  38.3 2.4 %collective-permute-start.6 = (bf16[96,1024]{1,0:T(8,128)(2,1)S(1)}, bf16[96,1024]{1,0:T(8,128)(2,1)S(1)}, u32[]{:S(2)}, u32[]{:S(2)}) collective-permute-start(bf16[96,1024]{1,0:T(8,128)(2,1)S(1)} %pad_maximum_fusion.mine_ref), channel_id=1, source_target_pairs={{0,16},{16,0},{1,17},{17,1},{2,18},{18,2},{3,19},{19,3},{4,20},{20... | collective-permute-start | bytes 589832 | tf_op jit(solution)/shard_map/ppermute | solution.py:261
  40.7 1.2 %shard_map.105.near_ref = bf16[512,128]{1,0:T(8,128)(2,1)S(1)} custom-call(bf16[144,1024]{1,0:T(8,128)(2,1)S(1)} %get-tuple-element.16.x0, bf16[144,1024]{1,0:T(8,128)(2,1)S(1)} %collective-permute-done.x1, bf16[144,1024]{1,0:T(8,128)(2,1)S(1)} %collective-permute-done.1.x2, bf16[144,1024]{1,0:T(8,128)(2,1)S(1)} %collective-permute-done.2.x3, ...), custom_call_target="tpu_custom_call" | custom-call | tf_op jit(solution)/shard_map/pallas_call | solution.py:184
  42.0 1.8 %shard_map.106 = bf16[4,128,1024]{2,1,0:T(8,128)(2,1)S(1)} custom-call(bf16[144,1024]{1,0:T(8,128)(2,1)S(1)} %get-tuple-element.16.x0, bf16[144,1024]{1,0:T(8,128)(2,1)S(1)} %collective-permute-done.x1, bf16[144,1024]{1,0:T(8,128)(2,1)S(1)} %collective-permute-done.1.x2, bf16[144,1024]{1,0:T(8,128)(2,1)S(1)} %collective-permute-done.2.x3, ...), custom_call_target="tpu_custom_call" | custom-call | tf_op jit(solution)/shard_map/pallas_call | solution.py:184
  43.8 18.8 %all_to_all.20.parts_ref = bf16[4,128,1024]{2,1,0:T(8,128)(2,1)S(1)} all-to-all(bf16[4,128,1024]{2,1,0:T(8,128)(2,1)S(1)} %shard_map.106), channel_id=1, replica_groups=mesh['yh'=2,'z'=8,'core'=2,'x'=4,'y'=4] {'x'}, dimensions={0} | all-to-all | bytes 2097152 | tf_op jit(solution)/shard_map/all_to_all | solution.py:272
  62.6 1.5 %shard_map.107 = (bf16[1,128,1024]{2,1,0:T(8,128)(2,1)}, bf16[144,1024]{1,0:T(8,128)(2,1)S(1)}, bf16[4,144,1024]{2,1,0:T(8,128)(2,1)}) custom-call(bf16[1,128]{1,0:T(2,128)(2,1)S(1)} %fusion.weight_ref, bf16[4,128,1024]{2,1,0:T(8,128)(2,1)S(1)} %all_to_all.20.parts_ref, bf16[1,128,1024]{2,1,0:T(8,128)(2,1)S(1)} %copy-done.1), custom_call_target="tpu_custom_call" | custom-call | tf_op jit(solution)/shard_map/pallas_call | solution.py:184
  64.1 3.5 %all-to-all-start.2 = ((bf16[4,144,1024]{2,1,0:T(8,128)(2,1)}), bf16[4,144,1024]{2,1,0:T(8,128)(2,1)S(1)}, u32[]{:S(2)}, u32[]{:S(2)}) async-start(bf16[4,144,1024]{2,1,0:T(8,128)(2,1)} %get-tuple-element.25), calls=%async_computation.2 | async-start | bytes 2359296 | tf_op jit(solution)/shard_map/all_to_all | solution.py:285
  67.6 1.3 %collective-permute-start.8 = (bf16[144,1024]{1,0:T(8,128)(2,1)S(1)}, bf16[144,1024]{1,0:T(8,128)(2,1)S(1)}, u32[]{:S(2)}, u32[]{:S(2)}) collective-permute-start(bf16[144,1024]{1,0:T(8,128)(2,1)S(1)} %get-tuple-element.26.own_ref), channel_id=1, source_target_pairs={{2,0},{1,3},{6,4},{5,7},{10,8},{9,11},{14,12},{13,15},{18,16},{17,... | collective-permute-start | bytes 884744 | tf_op jit(solution)/shard_map/ppermute | solution.py:284
  68.9 5.2 %collective-permute-start.7 = (bf16[144,1024]{1,0:T(8,128)(2,1)S(1)}, bf16[144,1024]{1,0:T(8,128)(2,1)S(1)}, u32[]{:S(2)}, u32[]{:S(2)}) collective-permute-start(bf16[144,1024]{1,0:T(8,128)(2,1)S(1)} %get-tuple-element.26.own_ref), channel_id=1, source_target_pairs={{1,0},{2,1},{3,2},{0,3},{5,4},{6,5},{7,6},{4,7},{9,8},{10,9},{11,1... | collective-permute-start | bytes 884744 | tf_op jit(solution)/shard_map/ppermute | solution.py:283
  74.2 6.1 %collective-permute-done.8.far_ref = bf16[144,1024]{1,0:T(8,128)(2,1)S(1)} collective-permute-done((bf16[144,1024]{1,0:T(8,128)(2,1)S(1)}, bf16[144,1024]{1,0:T(8,128)(2,1)S(1)}, u32[]{:S(2)}, u32[]{:S(2)}) %collective-permute-start.8) | collective-permute-done | bytes 294944 | tf_op jit(solution)/shard_map/ppermute | solution.py:284
  80.3 4.1 %collective-permute-done.7.near_ref = bf16[144,1024]{1,0:T(8,128)(2,1)S(1)} collective-permute-done((bf16[144,1024]{1,0:T(8,128)(2,1)S(1)}, bf16[144,1024]{1,0:T(8,128)(2,1)S(1)}, u32[]{:S(2)}, u32[]{:S(2)}) %collective-permute-start.7) | collective-permute-done | bytes 294944 | tf_op jit(solution)/shard_map/ppermute | solution.py:283
  84.4 0.9 shard_map.108
  85.4 15.3 %all_to_all.21.got_ref = f32[16,8,128]{2,1,0:T(8,128)S(1)} all-to-all(f32[16,8,128]{2,1,0:T(8,128)S(1)} %shard_map.108), channel_id=1, replica_groups=mesh['yh'=2,'z'=8,'core'=2,'x'=4,'y'=4] {'x','y'}, dimensions={0} | all-to-all | bytes 131072 | tf_op jit(solution)/shard_map/all_to_all | solution.py:289
  100.6 0.6 shard_map.109
  (21 shorter events, 0.1 us)
Async XLA Ops:
  0.6 32.5 %copy-start = (f32[50265]{0:T(1024)S(1)}, f32[50265]{0:T(1024)}, u32[]{:S(2)}) copy-start(f32[50265]{0:T(1024)} %param.11) | copy-start | bytes 603184
  0.6 11.1 %copy-start.2 = (bf16[64,1024]{1,0:T(8,128)(2,1)S(1)}, bf16[64,1024]{1,0:T(8,128)(2,1)}, u32[]{:S(2)}) copy-start(bf16[64,1024]{1,0:T(8,128)(2,1)} %own_ref.1) | copy-start | bytes 393220
  0.7 16.8 %copy-start.1 = (bf16[1,128,1024]{2,1,0:T(8,128)(2,1)S(1)}, bf16[1,128,1024]{2,1,0:T(8,128)(2,1)}, u32[]{:S(2)}) copy-start(bf16[1,128,1024]{2,1,0:T(8,128)(2,1)} %x_ref.3) | copy-start | bytes 786436
  2.8 30.3 %copy-start.3 = (s32[1,128]{1,0:T(1,128)S(1)}, s32[1,128]{1,0:T(1,128)}, u32[]{:S(2)}) copy-start(s32[1,128]{1,0:T(1,128)} %param.9) | copy-start | bytes 1540
  2.8 33.6 %all-to-all-start = ((bf16[16,64,384]{2,1,0:T(8,128)(2,1)}), bf16[16,64,384]{2,1,0:T(8,128)(2,1)S(1)}, u32[]{:S(2)}, u32[]{:S(2)}) async-start(bf16[16,64,384]{2,1,0:T(8,128)(2,1)} %shard_map.103), calls=%async_computation | async-start | bytes 1572864 | tf_op jit(solution)/shard_map/all_to_all | solution.py:222
  11.8 24.3 %collective-permute-start.3 = (bf16[64,1024]{1,0:T(8,128)(2,1)S(1)}, bf16[64,1024]{1,0:T(8,128)(2,1)S(1)}, u32[]{:S(2)}, u32[]{:S(2)}) collective-permute-start(bf16[64,1024]{1,0:T(8,128)(2,1)S(1)} %copy-done.2), channel_id=1, source_target_pairs={{1,0},{275,16},{2,1},{16,17},{3,2},{17,18},{256,3},{18,19},{257,25... | collective-permute-start | bytes 393224 | tf_op jit(solution)/shard_map/ppermute | solution.py:250
  17.5 18.5 %collective-permute-start.2 = (bf16[144,1024]{1,0:T(8,128)(2,1)S(1)}, bf16[144,1024]{1,0:T(8,128)(2,1)S(1)}, u32[]{:S(2)}, u32[]{:S(2)}) collective-permute-start(bf16[144,1024]{1,0:T(8,128)(2,1)S(1)} %get-tuple-element.16.x0), channel_id=1, source_target_pairs={{12,0},{0,4},{4,8},{8,12},{13,1},{1,5},{5,9},{9,13},{14,2},{2,6},{... | collective-permute-start | bytes 884744 | tf_op jit(solution)/shard_map/ppermute | solution.py:253
  20.9 15.5 %collective-permute-start.1 = (bf16[144,1024]{1,0:T(8,128)(2,1)S(1)}, bf16[144,1024]{1,0:T(8,128)(2,1)S(1)}, u32[]{:S(2)}, u32[]{:S(2)}) collective-permute-start(bf16[144,1024]{1,0:T(8,128)(2,1)S(1)} %get-tuple-element.16.x0), channel_id=1, source_target_pairs={{8,0},{12,4},{0,8},{4,12},{9,1},{13,5},{1,9},{5,13},{10,2},{14,6},... | collective-permute-start | bytes 884744 | tf_op jit(solution)/shard_map/ppermute | solution.py:253
  25.5 10.9 %collective-permute-start = (bf16[144,1024]{1,0:T(8,128)(2,1)S(1)}, bf16[144,1024]{1,0:T(8,128)(2,1)S(1)}, u32[]{:S(2)}, u32[]{:S(2)}) collective-permute-start(bf16[144,1024]{1,0:T(8,128)(2,1)S(1)} %get-tuple-element.16.x0), channel_id=1, source_target_pairs={{4,0},{8,4},{12,8},{0,12},{5,1},{9,5},{13,9},{1,13},{6,2},{10,6},{... | collective-permute-start | bytes 884744 | tf_op jit(solution)/shard_map/ppermute | solution.py:253
  28.9 7.2 %collective-permute-start.4 = (bf16[32,1024]{1,0:T(8,128)(2,1)S(1)}, bf16[32,1024]{1,0:T(8,128)(2,1)S(1)}, u32[]{:S(2)}, u32[]{:S(2)}) collective-permute-start(bf16[32,1024]{1,0:T(8,128)(2,1)S(1)} %get-tuple-element.17), channel_id=1, source_target_pairs={{2,0},{3,1},{256,2},{257,3},{258,256},{259,257},{0,258},{1,259},{6... | collective-permute-start | bytes 196616 | tf_op jit(solution)/shard_map/ppermute | solution.py:251
  36.4 5.6 %collective-permute-start.5 = (bf16[1024,384]{1,0:T(8,128)(2,1)S(1)}, bf16[1024,384]{1,0:T(8,128)(2,1)S(1)}, u32[]{:S(2)}, u32[]{:S(2)}) collective-permute-start(bf16[1024,384]{1,0:T(8,128)(2,1)S(1)} %bitcast.9), channel_id=1, source_target_pairs={{0,16},{16,0},{1,17},{17,1},{2,18},{18,2},{3,19},{19,3},{4,20},{20... | collective-permute-start | bytes 2359304 | tf_op jit(solution)/shard_map/ppermute | solution.py:260
  38.3 3.6 %collective-permute-start.6 = (bf16[96,1024]{1,0:T(8,128)(2,1)S(1)}, bf16[96,1024]{1,0:T(8,128)(2,1)S(1)}, u32[]{:S(2)}, u32[]{:S(2)}) collective-permute-start(bf16[96,1024]{1,0:T(8,128)(2,1)S(1)} %pad_maximum_fusion.mine_ref), channel_id=1, source_target_pairs={{0,16},{16,0},{1,17},{17,1},{2,18},{18,2},{3,19},{19,3},{4,20},{20... | collective-permute-start | bytes 589832 | tf_op jit(solution)/shard_map/ppermute | solution.py:261
  64.1 20.3 %all-to-all-start.2 = ((bf16[4,144,1024]{2,1,0:T(8,128)(2,1)}), bf16[4,144,1024]{2,1,0:T(8,128)(2,1)S(1)}, u32[]{:S(2)}, u32[]{:S(2)}) async-start(bf16[4,144,1024]{2,1,0:T(8,128)(2,1)} %get-tuple-element.25), calls=%async_computation.2 | async-start | bytes 2359296 | tf_op jit(solution)/shard_map/all_to_all | solution.py:285
  67.6 12.6 %collective-permute-start.8 = (bf16[144,1024]{1,0:T(8,128)(2,1)S(1)}, bf16[144,1024]{1,0:T(8,128)(2,1)S(1)}, u32[]{:S(2)}, u32[]{:S(2)}) collective-permute-start(bf16[144,1024]{1,0:T(8,128)(2,1)S(1)} %get-tuple-element.26.own_ref), channel_id=1, source_target_pairs={{2,0},{1,3},{6,4},{5,7},{10,8},{9,11},{14,12},{13,15},{18,16},{17,... | collective-permute-start | bytes 884744 | tf_op jit(solution)/shard_map/ppermute | solution.py:284
  68.9 15.5 %collective-permute-start.7 = (bf16[144,1024]{1,0:T(8,128)(2,1)S(1)}, bf16[144,1024]{1,0:T(8,128)(2,1)S(1)}, u32[]{:S(2)}, u32[]{:S(2)}) collective-permute-start(bf16[144,1024]{1,0:T(8,128)(2,1)S(1)} %get-tuple-element.26.own_ref), channel_id=1, source_target_pairs={{1,0},{2,1},{3,2},{0,3},{5,4},{6,5},{7,6},{4,7},{9,8},{10,9},{11,1... | collective-permute-start | bytes 884744 | tf_op jit(solution)/shard_map/ppermute | solution.py:283

commit v5 on v4

--- a/solution.py
+++ b/solution.py
@@ -42,8 +42,9 @@
         send.wait()
 
 
-def extend_kernel(x_ref, used_ref, o_ref, ext_ref, half_ref):
+def extend_kernel(x_ref, used_ref, o_ref, ext_ref, half_ref, block_ref):
     half = half_ref.shape[0]
+    block_ref[...] = o_ref[...]
     half_ref[...] = o_ref[pl.ds(pl.multiple_of(lax.axis_index("core") * half, half), half), :]
     rows = x_ref.shape[1]
     ext_ref[:rows, :] = x_ref[0]
@@ -241,13 +242,17 @@
         compiler_params=params(63),
     )(query_weight, key_weight, value_weight)
     used = jnp.broadcast_to(lengths.astype(f32)[:, None], (1, LANES))
-    extended, half = call(
+    extended, half, block = call(
         extend_kernel,
         [VMEM] * 3,
-        (jax.ShapeDtypeStruct((length + PAD, width), bf16), jax.ShapeDtypeStruct((depth // 2, width), bf16)),
+        (
+            jax.ShapeDtypeStruct((length + PAD, width), bf16),
+            jax.ShapeDtypeStruct((depth // 2, width), bf16),
+            jax.ShapeDtypeStruct((depth, width), bf16),
+        ),
         layer_input, used, output_weight,
     )
-    beside = lax.ppermute(output_weight, ("yh", "core", "y"), sideways())
+    beside = lax.ppermute(block, ("yh", "core", "y"), sideways())
     across = lax.ppermute(half, ("yh", "y"), shift(8, 2))
     weights = spread(chunks)
     others = [lax.ppermute(extended, "x", shift(4, k)) for k in (1, 2, 3)]

time: 102 us -> 100 us (0.980)
  blocking collectives: 34 us -> 31.7 us
  waiting for transfers between devices: 12.3 us -> 14.2 us
  starting transfers between devices: 43.9 us -> 42.8 us
    ppermute x1, waiting for transfers between devices: 0.01 us -> 2.26 us  [shards(): beside = lax.ppermute(block, ('yh', 'core', 'y'), sideways())]
    all_to_all x1, blocking collectives: 15.3 us -> 13.6 us  [shards(): lax.all_to_all(known, ('x', 'y'), split_axis=0, concat_axis=0, tiled=True)]
    ppermute x1, starting transfers between devices: 5.04 us -> 3.37 us  [shards(): beside = lax.ppermute(block, ('yh', 'core', 'y'), sideways())]
    ppermute x1, waiting for transfers between devices: 1.67 us -> 0.01 us  [shards(): across = lax.ppermute(half, ('yh', 'y'), shift(8, 2))]
    ppermute x1, starting transfers between devices: 4.27 us -> 5.48 us  [shards(): across = lax.ppermute(half, ('yh', 'y'), shift(8, 2))]
    ppermute x1, waiting for transfers between devices: 6.13 us -> 7.33 us  [shards(): far = lax.ppermute(own, 'y', [(2, 0), (1, 3)])]
    ppermute x1, starting transfers between devices: 5.21 us -> 4.14 us  [shards(): near = lax.ppermute(own, 'y', shift(4, 1))]
  transfers between devices with their start and end apart: 11 -> 11, of which waited for: 4 -> 3; matrix products, arithmetic and copies ran while one was open for 1% -> 1% of each run, Pallas kernels for 1% -> 1%
where the time goes in v5:
time: 100 us; the launch traced here: 99.8 us
  starting transfers between devices  42.8 us (43%)
  blocking collectives  31.7 us (32%)
  waiting for transfers between devices  14.2 us (14%)
  Pallas kernels  8.31 us (8%)
  between operations  1.55 us (2%)
  local copies, waits for them, and re-layouts  1.18 us (1%)
    all_to_all x1, blocking collectives, shards(): parts = lax.all_to_all(parts, 'x', split_axis=0, concat_axis=0, tiled=True)  18.1 us
    all_to_all x1, blocking collectives, shards(): lax.all_to_all(known, ('x', 'y'), split_axis=0, concat_axis=0, tiled=True)  13.6 us
    ppermute x3, starting transfers between devices, shards(): others = [lax.ppermute(extended, 'x', shift(4, k)) for k in (1, 2, 3)]  11.8 us
    all_to_all x1, starting transfers between devices, spread(): lax.all_to_all(chunks, axes, split_axis=0, concat_axis=0, tiled=True, axi...  8.89 us
    ppermute x1, waiting for transfers between devices, shards(): far = lax.ppermute(own, 'y', [(2, 0), (1, 3)])  7.33 us
    pallas_call x6, Pallas kernels, call(): pl.pallas_call(kernel, in_specs=ins, out_specs=tuple((VMEM for _ in outs)...  6.15 us
    ppermute x1, starting transfers between devices, shards(): across = lax.ppermute(half, ('yh', 'y'), shift(8, 2))  5.48 us
    ppermute x1, waiting for transfers between devices, shards(): near = lax.ppermute(own, 'y', shift(4, 1))  4.6 us
  transfers between devices with their start and end apart: 11, of which 3 were waited for; matrix products, arithmetic and copies ran while one was open for 1% of the time, Pallas kernels for 1%

profile of v5, /device:TPU:448, one launch (start us, length us, event | category | flops | bytes accessed | tf_op | source)
XLA Modules:
  0.0 99.8 jit_solution(6414259176946525537)
XLA Ops:
  0.6 0.0 copy-start
  0.7 2.2 %shard_map.103 = bf16[16,64,384]{2,1,0:T(8,128)(2,1)} custom-call(bf16[64,1024]{1,0:T(8,128)(2,1)} %q_hbm.1, bf16[64,1024]{1,0:T(8,128)(2,1)} %k_hbm.1, bf16[64,1024]{1,0:T(8,128)(2,1)} %v_hbm.1), custom_call_target="tpu_custom_call" | custom-call | tf_op jit(solution)/shard_map/pallas_call | solution.py:231
  2.8 8.9 %all-to-all-start = ((bf16[16,64,384]{2,1,0:T(8,128)(2,1)}), bf16[16,64,384]{2,1,0:T(8,128)(2,1)S(1)}, u32[]{:S(2)}, u32[]{:S(2)}) async-start(bf16[16,64,384]{2,1,0:T(8,128)(2,1)} %shard_map.103), calls=%async_computation | async-start | bytes 1572864 | tf_op jit(solution)/shard_map/all_to_all | solution.py:223
  12.5 3.8 %collective-permute-start.2 = (bf16[144,1024]{1,0:T(8,128)(2,1)S(1)}, bf16[144,1024]{1,0:T(8,128)(2,1)S(1)}, u32[]{:S(2)}, u32[]{:S(2)}) collective-permute-start(bf16[144,1024]{1,0:T(8,128)(2,1)S(1)} %get-tuple-element.17.x0), channel_id=1, source_target_pairs={{12,0},{0,4},{4,8},{8,12},{13,1},{1,5},{5,9},{9,13},{14,2},{2,6},{... | collective-permute-start | bytes 884744 | tf_op jit(solution)/shard_map/ppermute | solution.py:258
  16.3 4.6 %collective-permute-start.1 = (bf16[144,1024]{1,0:T(8,128)(2,1)S(1)}, bf16[144,1024]{1,0:T(8,128)(2,1)S(1)}, u32[]{:S(2)}, u32[]{:S(2)}) collective-permute-start(bf16[144,1024]{1,0:T(8,128)(2,1)S(1)} %get-tuple-element.17.x0), channel_id=1, source_target_pairs={{8,0},{12,4},{0,8},{4,12},{9,1},{13,5},{1,9},{5,13},{10,2},{14,6},... | collective-permute-start | bytes 884744 | tf_op jit(solution)/shard_map/ppermute | solution.py:258
  20.9 3.4 %collective-permute-start = (bf16[144,1024]{1,0:T(8,128)(2,1)S(1)}, bf16[144,1024]{1,0:T(8,128)(2,1)S(1)}, u32[]{:S(2)}, u32[]{:S(2)}) collective-permute-start(bf16[144,1024]{1,0:T(8,128)(2,1)S(1)} %get-tuple-element.17.x0), channel_id=1, source_target_pairs={{4,0},{8,4},{12,8},{0,12},{5,1},{9,5},{13,9},{1,13},{6,2},{10,6},{... | collective-permute-start | bytes 884744 | tf_op jit(solution)/shard_map/ppermute | solution.py:258
  24.3 5.5 %collective-permute-start.4 = (bf16[32,1024]{1,0:T(8,128)(2,1)S(1)}, bf16[32,1024]{1,0:T(8,128)(2,1)S(1)}, u32[]{:S(2)}, u32[]{:S(2)}) collective-permute-start(bf16[32,1024]{1,0:T(8,128)(2,1)S(1)} %get-tuple-element.19), channel_id=1, source_target_pairs={{2,0},{3,1},{256,2},{257,3},{258,256},{259,257},{0,258},{1,259},{6... | collective-permute-start | bytes 196616 | tf_op jit(solution)/shard_map/ppermute | solution.py:256
  29.8 3.4 %collective-permute-start.3 = (bf16[64,1024]{1,0:T(8,128)(2,1)S(1)}, bf16[64,1024]{1,0:T(8,128)(2,1)S(1)}, u32[]{:S(2)}, u32[]{:S(2)}) collective-permute-start(bf16[64,1024]{1,0:T(8,128)(2,1)S(1)} %get-tuple-element.18), channel_id=1, source_target_pairs={{1,0},{275,16},{2,1},{16,17},{3,2},{17,18},{256,3},{18,19},{257,25... | collective-permute-start | bytes 393224 | tf_op jit(solution)/shard_map/ppermute | solution.py:255
  33.2 1.1 %gather_fusion = bf16[128]{0:T(256)(128)(2,1)S(1)} fusion(f32[50265]{0:T(1024)S(1)} %copy-done, s32[1024]{0:T(1024)S(1)} %pad_clamp_fusion), kind=kCustom, calls=%fused_computation | custom fusion | bytes 1024 | tf_op jit(solution)/shard_map/jit(_take)/gather | solution.py:262
  34.4 2.3 %collective-permute-done.3 = bf16[64,1024]{1,0:T(8,128)(2,1)S(1)} collective-permute-done((bf16[64,1024]{1,0:T(8,128)(2,1)S(1)}, bf16[64,1024]{1,0:T(8,128)(2,1)S(1)}, u32[]{:S(2)}, u32[]{:S(2)}) %collective-permute-start.3) | collective-permute-done | bytes 131104 | tf_op jit(solution)/shard_map/ppermute | solution.py:255
  36.7 1.9 %collective-permute-start.5 = (bf16[1024,384]{1,0:T(8,128)(2,1)S(1)}, bf16[1024,384]{1,0:T(8,128)(2,1)S(1)}, u32[]{:S(2)}, u32[]{:S(2)}) collective-permute-start(bf16[1024,384]{1,0:T(8,128)(2,1)S(1)} %bitcast.9), channel_id=1, source_target_pairs={{0,16},{16,0},{1,17},{17,1},{2,18},{18,2},{3,19},{19,3},{4,20},{20... | collective-permute-start | bytes 2359304 | tf_op jit(solution)/shard_map/ppermute | solution.py:265
  38.6 2.4 %collective-permute-start.6 = (bf16[96,1024]{1,0:T(8,128)(2,1)S(1)}, bf16[96,1024]{1,0:T(8,128)(2,1)S(1)}, u32[]{:S(2)}, u32[]{:S(2)}) collective-permute-start(bf16[96,1024]{1,0:T(8,128)(2,1)S(1)} %pad_maximum_fusion.mine_ref), channel_id=1, source_target_pairs={{0,16},{16,0},{1,17},{17,1},{2,18},{18,2},{3,19},{19,3},{4,20},{20... | collective-permute-start | bytes 589832 | tf_op jit(solution)/shard_map/ppermute | solution.py:266
  41.0 1.2 %shard_map.105.near_ref = bf16[512,128]{1,0:T(8,128)(2,1)S(1)} custom-call(bf16[144,1024]{1,0:T(8,128)(2,1)S(1)} %get-tuple-element.17.x0, bf16[144,1024]{1,0:T(8,128)(2,1)S(1)} %collective-permute-done.x1, bf16[144,1024]{1,0:T(8,128)(2,1)S(1)} %collective-permute-done.1.x2, bf16[144,1024]{1,0:T(8,128)(2,1)S(1)} %collective-permute-done.2.x3, ...), custom_call_target="tpu_custom_call" | custom-call | tf_op jit(solution)/shard_map/pallas_call | solution.py:185
  42.3 1.8 %shard_map.106 = bf16[4,128,1024]{2,1,0:T(8,128)(2,1)S(1)} custom-call(bf16[144,1024]{1,0:T(8,128)(2,1)S(1)} %get-tuple-element.17.x0, bf16[144,1024]{1,0:T(8,128)(2,1)S(1)} %collective-permute-done.x1, bf16[144,1024]{1,0:T(8,128)(2,1)S(1)} %collective-permute-done.1.x2, bf16[144,1024]{1,0:T(8,128)(2,1)S(1)} %collective-permute-done.2.x3, ...), custom_call_target="tpu_custom_call" | custom-call | tf_op jit(solution)/shard_map/pallas_call | solution.py:185
  44.1 18.1 %all_to_all.20.parts_ref = bf16[4,128,1024]{2,1,0:T(8,128)(2,1)S(1)} all-to-all(bf16[4,128,1024]{2,1,0:T(8,128)(2,1)S(1)} %shard_map.106), channel_id=1, replica_groups=mesh['yh'=2,'z'=8,'core'=2,'x'=4,'y'=4] {'x'}, dimensions={0} | all-to-all | bytes 2097152 | tf_op jit(solution)/shard_map/all_to_all | solution.py:277
  62.2 1.5 %shard_map.107 = (bf16[1,128,1024]{2,1,0:T(8,128)(2,1)}, bf16[144,1024]{1,0:T(8,128)(2,1)S(1)}, bf16[4,144,1024]{2,1,0:T(8,128)(2,1)}) custom-call(bf16[1,128]{1,0:T(2,128)(2,1)S(1)} %fusion.weight_ref, bf16[4,128,1024]{2,1,0:T(8,128)(2,1)S(1)} %all_to_all.20.parts_ref, bf16[1,128,1024]{2,1,0:T(8,128)(2,1)S(1)} %copy-done.1), custom_call_target="tpu_custom_call" | custom-call | tf_op jit(solution)/shard_map/pallas_call | solution.py:185
  63.8 3.5 %all-to-all-start.2 = ((bf16[4,144,1024]{2,1,0:T(8,128)(2,1)}), bf16[4,144,1024]{2,1,0:T(8,128)(2,1)S(1)}, u32[]{:S(2)}, u32[]{:S(2)}) async-start(bf16[4,144,1024]{2,1,0:T(8,128)(2,1)} %get-tuple-element.27), calls=%async_computation.2 | async-start | bytes 2359296 | tf_op jit(solution)/shard_map/all_to_all | solution.py:290
  67.3 1.3 %collective-permute-start.8 = (bf16[144,1024]{1,0:T(8,128)(2,1)S(1)}, bf16[144,1024]{1,0:T(8,128)(2,1)S(1)}, u32[]{:S(2)}, u32[]{:S(2)}) collective-permute-start(bf16[144,1024]{1,0:T(8,128)(2,1)S(1)} %get-tuple-element.28.own_ref), channel_id=1, source_target_pairs={{2,0},{1,3},{6,4},{5,7},{10,8},{9,11},{14,12},{13,15},{18,16},{17,... | collective-permute-start | bytes 884744 | tf_op jit(solution)/shard_map/ppermute | solution.py:289
  68.6 4.1 %collective-permute-start.7 = (bf16[144,1024]{1,0:T(8,128)(2,1)S(1)}, bf16[144,1024]{1,0:T(8,128)(2,1)S(1)}, u32[]{:S(2)}, u32[]{:S(2)}) collective-permute-start(bf16[144,1024]{1,0:T(8,128)(2,1)S(1)} %get-tuple-element.28.own_ref), channel_id=1, source_target_pairs={{1,0},{2,1},{3,2},{0,3},{5,4},{6,5},{7,6},{4,7},{9,8},{10,9},{11,1... | collective-permute-start | bytes 884744 | tf_op jit(solution)/shard_map/ppermute | solution.py:288
  72.7 7.3 %collective-permute-done.8.far_ref = bf16[144,1024]{1,0:T(8,128)(2,1)S(1)} collective-permute-done((bf16[144,1024]{1,0:T(8,128)(2,1)S(1)}, bf16[144,1024]{1,0:T(8,128)(2,1)S(1)}, u32[]{:S(2)}, u32[]{:S(2)}) %collective-permute-start.8) | collective-permute-done | bytes 294944 | tf_op jit(solution)/shard_map/ppermute | solution.py:289
  80.1 4.6 %collective-permute-done.7.near_ref = bf16[144,1024]{1,0:T(8,128)(2,1)S(1)} collective-permute-done((bf16[144,1024]{1,0:T(8,128)(2,1)S(1)}, bf16[144,1024]{1,0:T(8,128)(2,1)S(1)}, u32[]{:S(2)}, u32[]{:S(2)}) %collective-permute-start.7) | collective-permute-done | bytes 294944 | tf_op jit(solution)/shard_map/ppermute | solution.py:288
  84.7 0.9 shard_map.108
  85.6 13.6 %all_to_all.21.got_ref = f32[16,8,128]{2,1,0:T(8,128)S(1)} all-to-all(f32[16,8,128]{2,1,0:T(8,128)S(1)} %shard_map.108), channel_id=1, replica_groups=mesh['yh'=2,'z'=8,'core'=2,'x'=4,'y'=4] {'x','y'}, dimensions={0} | all-to-all | bytes 131072 | tf_op jit(solution)/shard_map/all_to_all | solution.py:294
  99.2 0.6 shard_map.109
  (21 shorter events, 0.1 us)
Async XLA Ops:
  0.6 32.6 %copy-start = (f32[50265]{0:T(1024)S(1)}, f32[50265]{0:T(1024)}, u32[]{:S(2)}) copy-start(f32[50265]{0:T(1024)} %param.11) | copy-start | bytes 603184
  0.6 11.8 %copy-start.2 = (bf16[64,1024]{1,0:T(8,128)(2,1)S(1)}, bf16[64,1024]{1,0:T(8,128)(2,1)}, u32[]{:S(2)}) copy-start(bf16[64,1024]{1,0:T(8,128)(2,1)} %own_ref.1) | copy-start | bytes 393220
  0.7 11.8 %copy-start.1 = (bf16[1,128,1024]{2,1,0:T(8,128)(2,1)S(1)}, bf16[1,128,1024]{2,1,0:T(8,128)(2,1)}, u32[]{:S(2)}) copy-start(bf16[1,128,1024]{2,1,0:T(8,128)(2,1)} %x_ref.3) | copy-start | bytes 786436
  2.8 30.3 %copy-start.3 = (s32[1,128]{1,0:T(1,128)S(1)}, s32[1,128]{1,0:T(1,128)}, u32[]{:S(2)}) copy-start(s32[1,128]{1,0:T(1,128)} %param.9) | copy-start | bytes 1540
  2.8 33.8 %all-to-all-start = ((bf16[16,64,384]{2,1,0:T(8,128)(2,1)}), bf16[16,64,384]{2,1,0:T(8,128)(2,1)S(1)}, u32[]{:S(2)}, u32[]{:S(2)}) async-start(bf16[16,64,384]{2,1,0:T(8,128)(2,1)} %shard_map.103), calls=%async_computation | async-start | bytes 1572864 | tf_op jit(solution)/shard_map/all_to_all | solution.py:223
  12.5 24.2 %collective-permute-start.2 = (bf16[144,1024]{1,0:T(8,128)(2,1)S(1)}, bf16[144,1024]{1,0:T(8,128)(2,1)S(1)}, u32[]{:S(2)}, u32[]{:S(2)}) collective-permute-start(bf16[144,1024]{1,0:T(8,128)(2,1)S(1)} %get-tuple-element.17.x0), channel_id=1, source_target_pairs={{12,0},{0,4},{4,8},{8,12},{13,1},{1,5},{5,9},{9,13},{14,2},{2,6},{... | collective-permute-start | bytes 884744 | tf_op jit(solution)/shard_map/ppermute | solution.py:258
  16.3 20.4 %collective-permute-start.1 = (bf16[144,1024]{1,0:T(8,128)(2,1)S(1)}, bf16[144,1024]{1,0:T(8,128)(2,1)S(1)}, u32[]{:S(2)}, u32[]{:S(2)}) collective-permute-start(bf16[144,1024]{1,0:T(8,128)(2,1)S(1)} %get-tuple-element.17.x0), channel_id=1, source_target_pairs={{8,0},{12,4},{0,8},{4,12},{9,1},{13,5},{1,9},{5,13},{10,2},{14,6},... | collective-permute-start | bytes 884744 | tf_op jit(solution)/shard_map/ppermute | solution.py:258
  20.9 15.8 %collective-permute-start = (bf16[144,1024]{1,0:T(8,128)(2,1)S(1)}, bf16[144,1024]{1,0:T(8,128)(2,1)S(1)}, u32[]{:S(2)}, u32[]{:S(2)}) collective-permute-start(bf16[144,1024]{1,0:T(8,128)(2,1)S(1)} %get-tuple-element.17.x0), channel_id=1, source_target_pairs={{4,0},{8,4},{12,8},{0,12},{5,1},{9,5},{13,9},{1,13},{6,2},{10,6},{... | collective-permute-start | bytes 884744 | tf_op jit(solution)/shard_map/ppermute | solution.py:258
  24.3 10.1 %collective-permute-start.4 = (bf16[32,1024]{1,0:T(8,128)(2,1)S(1)}, bf16[32,1024]{1,0:T(8,128)(2,1)S(1)}, u32[]{:S(2)}, u32[]{:S(2)}) collective-permute-start(bf16[32,1024]{1,0:T(8,128)(2,1)S(1)} %get-tuple-element.19), channel_id=1, source_target_pairs={{2,0},{3,1},{256,2},{257,3},{258,256},{259,257},{0,258},{1,259},{6... | collective-permute-start | bytes 196616 | tf_op jit(solution)/shard_map/ppermute | solution.py:256
  29.8 6.9 %collective-permute-start.3 = (bf16[64,1024]{1,0:T(8,128)(2,1)S(1)}, bf16[64,1024]{1,0:T(8,128)(2,1)S(1)}, u32[]{:S(2)}, u32[]{:S(2)}) collective-permute-start(bf16[64,1024]{1,0:T(8,128)(2,1)S(1)} %get-tuple-element.18), channel_id=1, source_target_pairs={{1,0},{275,16},{2,1},{16,17},{3,2},{17,18},{256,3},{18,19},{257,25... | collective-permute-start | bytes 393224 | tf_op jit(solution)/shard_map/ppermute | solution.py:255
  36.7 5.6 %collective-permute-start.5 = (bf16[1024,384]{1,0:T(8,128)(2,1)S(1)}, bf16[1024,384]{1,0:T(8,128)(2,1)S(1)}, u32[]{:S(2)}, u32[]{:S(2)}) collective-permute-start(bf16[1024,384]{1,0:T(8,128)(2,1)S(1)} %bitcast.9), channel_id=1, source_target_pairs={{0,16},{16,0},{1,17},{17,1},{2,18},{18,2},{3,19},{19,3},{4,20},{20... | collective-permute-start | bytes 2359304 | tf_op jit(solution)/shard_map/ppermute | solution.py:265
  38.6 3.6 %collective-permute-start.6 = (bf16[96,1024]{1,0:T(8,128)(2,1)S(1)}, bf16[96,1024]{1,0:T(8,128)(2,1)S(1)}, u32[]{:S(2)}, u32[]{:S(2)}) collective-permute-start(bf16[96,1024]{1,0:T(8,128)(2,1)S(1)} %pad_maximum_fusion.mine_ref), channel_id=1, source_target_pairs={{0,16},{16,0},{1,17},{17,1},{2,18},{18,2},{3,19},{19,3},{4,20},{20... | collective-permute-start | bytes 589832 | tf_op jit(solution)/shard_map/ppermute | solution.py:266
  63.8 20.9 %all-to-all-start.2 = ((bf16[4,144,1024]{2,1,0:T(8,128)(2,1)}), bf16[4,144,1024]{2,1,0:T(8,128)(2,1)S(1)}, u32[]{:S(2)}, u32[]{:S(2)}) async-start(bf16[4,144,1024]{2,1,0:T(8,128)(2,1)} %get-tuple-element.27), calls=%async_computation.2 | async-start | bytes 2359296 | tf_op jit(solution)/shard_map/all_to_all | solution.py:290
  67.3 12.8 %collective-permute-start.8 = (bf16[144,1024]{1,0:T(8,128)(2,1)S(1)}, bf16[144,1024]{1,0:T(8,128)(2,1)S(1)}, u32[]{:S(2)}, u32[]{:S(2)}) collective-permute-start(bf16[144,1024]{1,0:T(8,128)(2,1)S(1)} %get-tuple-element.28.own_ref), channel_id=1, source_target_pairs={{2,0},{1,3},{6,4},{5,7},{10,8},{9,11},{14,12},{13,15},{18,16},{17,... | collective-permute-start | bytes 884744 | tf_op jit(solution)/shard_map/ppermute | solution.py:289
  68.6 16.1 %collective-permute-start.7 = (bf16[144,1024]{1,0:T(8,128)(2,1)S(1)}, bf16[144,1024]{1,0:T(8,128)(2,1)S(1)}, u32[]{:S(2)}, u32[]{:S(2)}) collective-permute-start(bf16[144,1024]{1,0:T(8,128)(2,1)S(1)} %get-tuple-element.28.own_ref), channel_id=1, source_target_pairs={{1,0},{2,1},{3,2},{0,3},{5,4},{6,5},{7,6},{4,7},{9,8},{10,9},{11,1... | collective-permute-start | bytes 884744 | tf_op jit(solution)/shard_map/ppermute | solution.py:288

commit v6 on v5

--- a/solution.py
+++ b/solution.py
@@ -19,20 +19,20 @@
     return pltpu.CompilerParams(vmem_limit_bytes=mebibytes * 1024 * 1024)
 
 
-def chunks_kernel(q_hbm, k_hbm, v_hbm, chunk_hbm, q_ref, k_ref, v_ref, piece_ref, sems, out_sems):
+def chunks_kernel(q_hbm, k_hbm, v_hbm, chunk_hbm, piece_ref, sems, out_sems):
     core = lax.axis_index("core")
     copies = []
-    for n, (far, near) in enumerate(((q_hbm, q_ref), (k_hbm, k_ref), (v_hbm, v_ref))):
-        copies.append(pltpu.make_async_copy(far, near, sems.at[n]))
+    for block in range(4):
+        at = pl.multiple_of(block * 2 * LANES + core * LANES, LANES)
+        for n, ref in enumerate((q_hbm, k_hbm, v_hbm)):
+            to = piece_ref.at[block, :, pl.ds(n * LANES, LANES)]
+            copies.append(pltpu.make_async_copy(ref.at[:, pl.ds(at, LANES)], to, sems.at[block * 3 + n]))
     for copy in copies:
         copy.start()
-    for copy in copies:
-        copy.wait()
     sends = []
     for block in range(4):
-        at = pl.multiple_of(block * 2 * LANES + core * LANES, LANES)
-        for n, ref in enumerate((q_ref, k_ref, v_ref)):
-            piece_ref[block, :, n * LANES : (n + 1) * LANES] = ref[:, pl.ds(at, LANES)]
+        for n in range(3):
+            copies[block * 3 + n].wait()
         for y in range(4):
             p = block * 4 + y
             send = pltpu.make_async_copy(piece_ref.at[block], chunk_hbm.at[p], out_sems.at[p])
@@ -233,10 +233,9 @@
         in_specs=[hbm] * 3,
         out_specs=hbm,
         out_shape=jax.ShapeDtypeStruct((16, depth, 3 * LANES), bf16),
-        scratch_shapes=[pltpu.VMEM((depth, width), bf16)] * 3
-        + [
+        scratch_shapes=[
             pltpu.VMEM((4, depth, 3 * LANES), bf16),
-            pltpu.SemaphoreType.DMA((3,)),
+            pltpu.SemaphoreType.DMA((12,)),
             pltpu.SemaphoreType.DMA((16,)),
         ],
         compiler_params=params(63),

time: 100 us -> 100 us (level)
  no operation moved by 1% of the time
where the time goes in v6:
time: 100 us; the launch traced here: 99.6 us
  starting transfers between devices  42.8 us (43%)
  blocking collectives  31.7 us (32%)
  waiting for transfers between devices  14.2 us (14%)
  Pallas kernels  8.11 us (8%)
  between operations  1.55 us (2%)
  local copies, waits for them, and re-layouts  1.18 us (1%)
    all_to_all x1, blocking collectives, shards(): parts = lax.all_to_all(parts, 'x', split_axis=0, concat_axis=0, tiled=True)  18.1 us
    all_to_all x1, blocking collectives, shards(): lax.all_to_all(known, ('x', 'y'), split_axis=0, concat_axis=0, tiled=True)  13.6 us
    ppermute x3, starting transfers between devices, shards(): others = [lax.ppermute(extended, 'x', shift(4, k)) for k in (1, 2, 3)]  11.8 us
    all_to_all x1, starting transfers between devices, spread(): lax.all_to_all(chunks, axes, split_axis=0, concat_axis=0, tiled=True, axi...  8.89 us
    ppermute x1, waiting for transfers between devices, shards(): far = lax.ppermute(own, 'y', [(2, 0), (1, 3)])  7.33 us
    pallas_call x6, Pallas kernels, call(): pl.pallas_call(kernel, in_specs=ins, out_specs=tuple((VMEM for _ in outs)...  6.15 us
    ppermute x1, starting transfers between devices, shards(): across = lax.ppermute(half, ('yh', 'y'), shift(8, 2))  5.48 us
    ppermute x1, waiting for transfers between devices, shards(): near = lax.ppermute(own, 'y', shift(4, 1))  4.6 us
  transfers between devices with their start and end apart: 11, of which 3 were waited for; matrix products, arithmetic and copies ran while one was open for 1% of the time, Pallas kernels for 1%

profile of v6, /device:TPU:448, one launch (start us, length us, event | category | flops | bytes accessed | tf_op | source)
XLA Modules:
  0.0 99.6 jit_solution(12628155025267550260)
XLA Ops:
  0.6 0.0 copy-start
  0.7 2.0 %shard_map.103 = bf16[16,64,384]{2,1,0:T(8,128)(2,1)} custom-call(bf16[64,1024]{1,0:T(8,128)(2,1)} %q_hbm.1, bf16[64,1024]{1,0:T(8,128)(2,1)} %k_hbm.1, bf16[64,1024]{1,0:T(8,128)(2,1)} %v_hbm.1), custom_call_target="tpu_custom_call" | custom-call | tf_op jit(solution)/shard_map/pallas_call | solution.py:231
  2.6 8.9 %all-to-all-start = ((bf16[16,64,384]{2,1,0:T(8,128)(2,1)}), bf16[16,64,384]{2,1,0:T(8,128)(2,1)S(1)}, u32[]{:S(2)}, u32[]{:S(2)}) async-start(bf16[16,64,384]{2,1,0:T(8,128)(2,1)} %shard_map.103), calls=%async_computation | async-start | bytes 1572864 | tf_op jit(solution)/shard_map/all_to_all | solution.py:223
  12.3 3.8 %collective-permute-start.2 = (bf16[144,1024]{1,0:T(8,128)(2,1)S(1)}, bf16[144,1024]{1,0:T(8,128)(2,1)S(1)}, u32[]{:S(2)}, u32[]{:S(2)}) collective-permute-start(bf16[144,1024]{1,0:T(8,128)(2,1)S(1)} %get-tuple-element.17.x0), channel_id=1, source_target_pairs={{12,0},{0,4},{4,8},{8,12},{13,1},{1,5},{5,9},{9,13},{14,2},{2,6},{... | collective-permute-start | bytes 884744 | tf_op jit(solution)/shard_map/ppermute | solution.py:257
  16.1 4.6 %collective-permute-start.1 = (bf16[144,1024]{1,0:T(8,128)(2,1)S(1)}, bf16[144,1024]{1,0:T(8,128)(2,1)S(1)}, u32[]{:S(2)}, u32[]{:S(2)}) collective-permute-start(bf16[144,1024]{1,0:T(8,128)(2,1)S(1)} %get-tuple-element.17.x0), channel_id=1, source_target_pairs={{8,0},{12,4},{0,8},{4,12},{9,1},{13,5},{1,9},{5,13},{10,2},{14,6},... | collective-permute-start | bytes 884744 | tf_op jit(solution)/shard_map/ppermute | solution.py:257
  20.7 3.4 %collective-permute-start = (bf16[144,1024]{1,0:T(8,128)(2,1)S(1)}, bf16[144,1024]{1,0:T(8,128)(2,1)S(1)}, u32[]{:S(2)}, u32[]{:S(2)}) collective-permute-start(bf16[144,1024]{1,0:T(8,128)(2,1)S(1)} %get-tuple-element.17.x0), channel_id=1, source_target_pairs={{4,0},{8,4},{12,8},{0,12},{5,1},{9,5},{13,9},{1,13},{6,2},{10,6},{... | collective-permute-start | bytes 884744 | tf_op jit(solution)/shard_map/ppermute | solution.py:257
  24.1 5.5 %collective-permute-start.4 = (bf16[32,1024]{1,0:T(8,128)(2,1)S(1)}, bf16[32,1024]{1,0:T(8,128)(2,1)S(1)}, u32[]{:S(2)}, u32[]{:S(2)}) collective-permute-start(bf16[32,1024]{1,0:T(8,128)(2,1)S(1)} %get-tuple-element.19), channel_id=1, source_target_pairs={{2,0},{3,1},{256,2},{257,3},{258,256},{259,257},{0,258},{1,259},{6... | collective-permute-start | bytes 196616 | tf_op jit(solution)/shard_map/ppermute | solution.py:255
  29.6 3.4 %collective-permute-start.3 = (bf16[64,1024]{1,0:T(8,128)(2,1)S(1)}, bf16[64,1024]{1,0:T(8,128)(2,1)S(1)}, u32[]{:S(2)}, u32[]{:S(2)}) collective-permute-start(bf16[64,1024]{1,0:T(8,128)(2,1)S(1)} %get-tuple-element.18), channel_id=1, source_target_pairs={{1,0},{275,16},{2,1},{16,17},{3,2},{17,18},{256,3},{18,19},{257,25... | collective-permute-start | bytes 393224 | tf_op jit(solution)/shard_map/ppermute | solution.py:254
  33.0 1.1 %gather_fusion = bf16[128]{0:T(256)(128)(2,1)S(1)} fusion(f32[50265]{0:T(1024)S(1)} %copy-done, s32[1024]{0:T(1024)S(1)} %pad_clamp_fusion), kind=kCustom, calls=%fused_computation | custom fusion | bytes 1024 | tf_op jit(solution)/shard_map/jit(_take)/gather | solution.py:261
  34.2 2.3 %collective-permute-done.3 = bf16[64,1024]{1,0:T(8,128)(2,1)S(1)} collective-permute-done((bf16[64,1024]{1,0:T(8,128)(2,1)S(1)}, bf16[64,1024]{1,0:T(8,128)(2,1)S(1)}, u32[]{:S(2)}, u32[]{:S(2)}) %collective-permute-start.3) | collective-permute-done | bytes 131104 | tf_op jit(solution)/shard_map/ppermute | solution.py:254
  36.5 1.9 %collective-permute-start.5 = (bf16[1024,384]{1,0:T(8,128)(2,1)S(1)}, bf16[1024,384]{1,0:T(8,128)(2,1)S(1)}, u32[]{:S(2)}, u32[]{:S(2)}) collective-permute-start(bf16[1024,384]{1,0:T(8,128)(2,1)S(1)} %bitcast.9), channel_id=1, source_target_pairs={{0,16},{16,0},{1,17},{17,1},{2,18},{18,2},{3,19},{19,3},{4,20},{20... | collective-permute-start | bytes 2359304 | tf_op jit(solution)/shard_map/ppermute | solution.py:264
  38.4 2.4 %collective-permute-start.6 = (bf16[96,1024]{1,0:T(8,128)(2,1)S(1)}, bf16[96,1024]{1,0:T(8,128)(2,1)S(1)}, u32[]{:S(2)}, u32[]{:S(2)}) collective-permute-start(bf16[96,1024]{1,0:T(8,128)(2,1)S(1)} %pad_maximum_fusion.mine_ref), channel_id=1, source_target_pairs={{0,16},{16,0},{1,17},{17,1},{2,18},{18,2},{3,19},{19,3},{4,20},{20... | collective-permute-start | bytes 589832 | tf_op jit(solution)/shard_map/ppermute | solution.py:265
  40.8 1.2 %shard_map.105.near_ref = bf16[512,128]{1,0:T(8,128)(2,1)S(1)} custom-call(bf16[144,1024]{1,0:T(8,128)(2,1)S(1)} %get-tuple-element.17.x0, bf16[144,1024]{1,0:T(8,128)(2,1)S(1)} %collective-permute-done.x1, bf16[144,1024]{1,0:T(8,128)(2,1)S(1)} %collective-permute-done.1.x2, bf16[144,1024]{1,0:T(8,128)(2,1)S(1)} %collective-permute-done.2.x3, ...), custom_call_target="tpu_custom_call" | custom-call | tf_op jit(solution)/shard_map/pallas_call | solution.py:185
  42.1 1.8 %shard_map.106 = bf16[4,128,1024]{2,1,0:T(8,128)(2,1)S(1)} custom-call(bf16[144,1024]{1,0:T(8,128)(2,1)S(1)} %get-tuple-element.17.x0, bf16[144,1024]{1,0:T(8,128)(2,1)S(1)} %collective-permute-done.x1, bf16[144,1024]{1,0:T(8,128)(2,1)S(1)} %collective-permute-done.1.x2, bf16[144,1024]{1,0:T(8,128)(2,1)S(1)} %collective-permute-done.2.x3, ...), custom_call_target="tpu_custom_call" | custom-call | tf_op jit(solution)/shard_map/pallas_call | solution.py:185
  43.9 18.1 %all_to_all.20.parts_ref = bf16[4,128,1024]{2,1,0:T(8,128)(2,1)S(1)} all-to-all(bf16[4,128,1024]{2,1,0:T(8,128)(2,1)S(1)} %shard_map.106), channel_id=1, replica_groups=mesh['yh'=2,'z'=8,'core'=2,'x'=4,'y'=4] {'x'}, dimensions={0} | all-to-all | bytes 2097152 | tf_op jit(solution)/shard_map/all_to_all | solution.py:276
  62.0 1.5 %shard_map.107 = (bf16[1,128,1024]{2,1,0:T(8,128)(2,1)}, bf16[144,1024]{1,0:T(8,128)(2,1)S(1)}, bf16[4,144,1024]{2,1,0:T(8,128)(2,1)}) custom-call(bf16[1,128]{1,0:T(2,128)(2,1)S(1)} %fusion.weight_ref, bf16[4,128,1024]{2,1,0:T(8,128)(2,1)S(1)} %all_to_all.20.parts_ref, bf16[1,128,1024]{2,1,0:T(8,128)(2,1)S(1)} %copy-done.1), custom_call_target="tpu_custom_call" | custom-call | tf_op jit(solution)/shard_map/pallas_call | solution.py:185
  63.6 3.5 %all-to-all-start.2 = ((bf16[4,144,1024]{2,1,0:T(8,128)(2,1)}), bf16[4,144,1024]{2,1,0:T(8,128)(2,1)S(1)}, u32[]{:S(2)}, u32[]{:S(2)}) async-start(bf16[4,144,1024]{2,1,0:T(8,128)(2,1)} %get-tuple-element.27), calls=%async_computation.2 | async-start | bytes 2359296 | tf_op jit(solution)/shard_map/all_to_all | solution.py:289
  67.1 1.3 %collective-permute-start.8 = (bf16[144,1024]{1,0:T(8,128)(2,1)S(1)}, bf16[144,1024]{1,0:T(8,128)(2,1)S(1)}, u32[]{:S(2)}, u32[]{:S(2)}) collective-permute-start(bf16[144,1024]{1,0:T(8,128)(2,1)S(1)} %get-tuple-element.28.own_ref), channel_id=1, source_target_pairs={{2,0},{1,3},{6,4},{5,7},{10,8},{9,11},{14,12},{13,15},{18,16},{17,... | collective-permute-start | bytes 884744 | tf_op jit(solution)/shard_map/ppermute | solution.py:288
  68.4 4.1 %collective-permute-start.7 = (bf16[144,1024]{1,0:T(8,128)(2,1)S(1)}, bf16[144,1024]{1,0:T(8,128)(2,1)S(1)}, u32[]{:S(2)}, u32[]{:S(2)}) collective-permute-start(bf16[144,1024]{1,0:T(8,128)(2,1)S(1)} %get-tuple-element.28.own_ref), channel_id=1, source_target_pairs={{1,0},{2,1},{3,2},{0,3},{5,4},{6,5},{7,6},{4,7},{9,8},{10,9},{11,1... | collective-permute-start | bytes 884744 | tf_op jit(solution)/shard_map/ppermute | solution.py:287
  72.5 7.3 %collective-permute-done.8.far_ref = bf16[144,1024]{1,0:T(8,128)(2,1)S(1)} collective-permute-done((bf16[144,1024]{1,0:T(8,128)(2,1)S(1)}, bf16[144,1024]{1,0:T(8,128)(2,1)S(1)}, u32[]{:S(2)}, u32[]{:S(2)}) %collective-permute-start.8) | collective-permute-done | bytes 294944 | tf_op jit(solution)/shard_map/ppermute | solution.py:288
  79.9 4.6 %collective-permute-done.7.near_ref = bf16[144,1024]{1,0:T(8,128)(2,1)S(1)} collective-permute-done((bf16[144,1024]{1,0:T(8,128)(2,1)S(1)}, bf16[144,1024]{1,0:T(8,128)(2,1)S(1)}, u32[]{:S(2)}, u32[]{:S(2)}) %collective-permute-start.7) | collective-permute-done | bytes 294944 | tf_op jit(solution)/shard_map/ppermute | solution.py:287
  84.5 1.0 shard_map.108
  85.4 13.6 %all_to_all.21.got_ref = f32[16,8,128]{2,1,0:T(8,128)S(1)} all-to-all(f32[16,8,128]{2,1,0:T(8,128)S(1)} %shard_map.108), channel_id=1, replica_groups=mesh['yh'=2,'z'=8,'core'=2,'x'=4,'y'=4] {'x','y'}, dimensions={0} | all-to-all | bytes 131072 | tf_op jit(solution)/shard_map/all_to_all | solution.py:293
  99.0 0.6 shard_map.109
  (21 shorter events, 0.1 us)
Async XLA Ops:
  0.6 32.4 %copy-start = (f32[50265]{0:T(1024)S(1)}, f32[50265]{0:T(1024)}, u32[]{:S(2)}) copy-start(f32[50265]{0:T(1024)} %param.11) | copy-start | bytes 603184
  0.6 11.6 %copy-start.2 = (bf16[64,1024]{1,0:T(8,128)(2,1)S(1)}, bf16[64,1024]{1,0:T(8,128)(2,1)}, u32[]{:S(2)}) copy-start(bf16[64,1024]{1,0:T(8,128)(2,1)} %own_ref.1) | copy-start | bytes 393220
  0.7 11.6 %copy-start.1 = (bf16[1,128,1024]{2,1,0:T(8,128)(2,1)S(1)}, bf16[1,128,1024]{2,1,0:T(8,128)(2,1)}, u32[]{:S(2)}) copy-start(bf16[1,128,1024]{2,1,0:T(8,128)(2,1)} %x_ref.3) | copy-start | bytes 786436
  2.6 30.3 %copy-start.3 = (s32[1,128]{1,0:T(1,128)S(1)}, s32[1,128]{1,0:T(1,128)}, u32[]{:S(2)}) copy-start(s32[1,128]{1,0:T(1,128)} %param.9) | copy-start | bytes 1540
  2.6 33.8 %all-to-all-start = ((bf16[16,64,384]{2,1,0:T(8,128)(2,1)}), bf16[16,64,384]{2,1,0:T(8,128)(2,1)S(1)}, u32[]{:S(2)}, u32[]{:S(2)}) async-start(bf16[16,64,384]{2,1,0:T(8,128)(2,1)} %shard_map.103), calls=%async_computation | async-start | bytes 1572864 | tf_op jit(solution)/shard_map/all_to_all | solution.py:223
  12.3 24.2 %collective-permute-start.2 = (bf16[144,1024]{1,0:T(8,128)(2,1)S(1)}, bf16[144,1024]{1,0:T(8,128)(2,1)S(1)}, u32[]{:S(2)}, u32[]{:S(2)}) collective-permute-start(bf16[144,1024]{1,0:T(8,128)(2,1)S(1)} %get-tuple-element.17.x0), channel_id=1, source_target_pairs={{12,0},{0,4},{4,8},{8,12},{13,1},{1,5},{5,9},{9,13},{14,2},{2,6},{... | collective-permute-start | bytes 884744 | tf_op jit(solution)/shard_map/ppermute | solution.py:257
  16.1 20.4 %collective-permute-start.1 = (bf16[144,1024]{1,0:T(8,128)(2,1)S(1)}, bf16[144,1024]{1,0:T(8,128)(2,1)S(1)}, u32[]{:S(2)}, u32[]{:S(2)}) collective-permute-start(bf16[144,1024]{1,0:T(8,128)(2,1)S(1)} %get-tuple-element.17.x0), channel_id=1, source_target_pairs={{8,0},{12,4},{0,8},{4,12},{9,1},{13,5},{1,9},{5,13},{10,2},{14,6},... | collective-permute-start | bytes 884744 | tf_op jit(solution)/shard_map/ppermute | solution.py:257
  20.7 15.8 %collective-permute-start = (bf16[144,1024]{1,0:T(8,128)(2,1)S(1)}, bf16[144,1024]{1,0:T(8,128)(2,1)S(1)}, u32[]{:S(2)}, u32[]{:S(2)}) collective-permute-start(bf16[144,1024]{1,0:T(8,128)(2,1)S(1)} %get-tuple-element.17.x0), channel_id=1, source_target_pairs={{4,0},{8,4},{12,8},{0,12},{5,1},{9,5},{13,9},{1,13},{6,2},{10,6},{... | collective-permute-start | bytes 884744 | tf_op jit(solution)/shard_map/ppermute | solution.py:257
  24.1 10.1 %collective-permute-start.4 = (bf16[32,1024]{1,0:T(8,128)(2,1)S(1)}, bf16[32,1024]{1,0:T(8,128)(2,1)S(1)}, u32[]{:S(2)}, u32[]{:S(2)}) collective-permute-start(bf16[32,1024]{1,0:T(8,128)(2,1)S(1)} %get-tuple-element.19), channel_id=1, source_target_pairs={{2,0},{3,1},{256,2},{257,3},{258,256},{259,257},{0,258},{1,259},{6... | collective-permute-start | bytes 196616 | tf_op jit(solution)/shard_map/ppermute | solution.py:255
  29.6 6.9 %collective-permute-start.3 = (bf16[64,1024]{1,0:T(8,128)(2,1)S(1)}, bf16[64,1024]{1,0:T(8,128)(2,1)S(1)}, u32[]{:S(2)}, u32[]{:S(2)}) collective-permute-start(bf16[64,1024]{1,0:T(8,128)(2,1)S(1)} %get-tuple-element.18), channel_id=1, source_target_pairs={{1,0},{275,16},{2,1},{16,17},{3,2},{17,18},{256,3},{18,19},{257,25... | collective-permute-start | bytes 393224 | tf_op jit(solution)/shard_map/ppermute | solution.py:254
  36.5 5.6 %collective-permute-start.5 = (bf16[1024,384]{1,0:T(8,128)(2,1)S(1)}, bf16[1024,384]{1,0:T(8,128)(2,1)S(1)}, u32[]{:S(2)}, u32[]{:S(2)}) collective-permute-start(bf16[1024,384]{1,0:T(8,128)(2,1)S(1)} %bitcast.9), channel_id=1, source_target_pairs={{0,16},{16,0},{1,17},{17,1},{2,18},{18,2},{3,19},{19,3},{4,20},{20... | collective-permute-start | bytes 2359304 | tf_op jit(solution)/shard_map/ppermute | solution.py:264
  38.4 3.6 %collective-permute-start.6 = (bf16[96,1024]{1,0:T(8,128)(2,1)S(1)}, bf16[96,1024]{1,0:T(8,128)(2,1)S(1)}, u32[]{:S(2)}, u32[]{:S(2)}) collective-permute-start(bf16[96,1024]{1,0:T(8,128)(2,1)S(1)} %pad_maximum_fusion.mine_ref), channel_id=1, source_target_pairs={{0,16},{16,0},{1,17},{17,1},{2,18},{18,2},{3,19},{19,3},{4,20},{20... | collective-permute-start | bytes 589832 | tf_op jit(solution)/shard_map/ppermute | solution.py:265
  63.6 20.9 %all-to-all-start.2 = ((bf16[4,144,1024]{2,1,0:T(8,128)(2,1)}), bf16[4,144,1024]{2,1,0:T(8,128)(2,1)S(1)}, u32[]{:S(2)}, u32[]{:S(2)}) async-start(bf16[4,144,1024]{2,1,0:T(8,128)(2,1)} %get-tuple-element.27), calls=%async_computation.2 | async-start | bytes 2359296 | tf_op jit(solution)/shard_map/all_to_all | solution.py:289
  67.1 12.8 %collective-permute-start.8 = (bf16[144,1024]{1,0:T(8,128)(2,1)S(1)}, bf16[144,1024]{1,0:T(8,128)(2,1)S(1)}, u32[]{:S(2)}, u32[]{:S(2)}) collective-permute-start(bf16[144,1024]{1,0:T(8,128)(2,1)S(1)} %get-tuple-element.28.own_ref), channel_id=1, source_target_pairs={{2,0},{1,3},{6,4},{5,7},{10,8},{9,11},{14,12},{13,15},{18,16},{17,... | collective-permute-start | bytes 884744 | tf_op jit(solution)/shard_map/ppermute | solution.py:288
  68.4 16.1 %collective-permute-start.7 = (bf16[144,1024]{1,0:T(8,128)(2,1)S(1)}, bf16[144,1024]{1,0:T(8,128)(2,1)S(1)}, u32[]{:S(2)}, u32[]{:S(2)}) collective-permute-start(bf16[144,1024]{1,0:T(8,128)(2,1)S(1)} %get-tuple-element.28.own_ref), channel_id=1, source_target_pairs={{1,0},{2,1},{3,2},{0,3},{5,4},{6,5},{7,6},{4,7},{9,8},{10,9},{11,1... | collective-permute-start | bytes 884744 | tf_op jit(solution)/shard_map/ppermute | solution.py:287

commit v7 on v6

--- a/solution.py
+++ b/solution.py
@@ -167,7 +167,7 @@
                 here = jnp.logical_and(here, has_far)
             total = total + jnp.where(here, jnp.broadcast_to(utility, total.shape), 0.0)
     for p in range(16):
-        out_ref[p] = jnp.broadcast_to(total[p : p + 1], (8, LANES))
+        out_ref[p] = total[p : p + 1]
 
 
 def finish_kernel(got_ref, pair_ref, mean_ref):
@@ -288,7 +288,7 @@
     far = lax.ppermute(own, "y", [(2, 0), (1, 3)])
     row = lax.all_to_all(row, "x", split_axis=0, concat_axis=0, tiled=True)
     known = call(
-        pairs_kernel, [VMEM] * 4, (jax.ShapeDtypeStruct((16, 8, LANES), f32),), row, near, far, own
+        pairs_kernel, [VMEM] * 4, (jax.ShapeDtypeStruct((16, 1, LANES), f32),), row, near, far, own
     )
     known = lax.all_to_all(known, ("x", "y"), split_axis=0, concat_axis=0, tiled=True)
     pair, mean = call(

time: 100 us -> 99.9 us (level)
  no operation moved by 1% of the time
where the time goes in v7:
time: 99.9 us; the launch traced here: 99.4 us
  starting transfers between devices  42.8 us (43%)
  blocking collectives  31.5 us (32%)
  waiting for transfers between devices  14.2 us (14%)
  Pallas kernels  8.1 us (8%)
  between operations  1.55 us (2%)
  local copies, waits for them, and re-layouts  1.18 us (1%)
    all_to_all x1, blocking collectives, shards(): parts = lax.all_to_all(parts, 'x', split_axis=0, concat_axis=0, tiled=True)  18.1 us
    all_to_all x1, blocking collectives, shards(): lax.all_to_all(known, ('x', 'y'), split_axis=0, concat_axis=0, tiled=True)  13.3 us
    ppermute x3, starting transfers between devices, shards(): others = [lax.ppermute(extended, 'x', shift(4, k)) for k in (1, 2, 3)]  11.8 us
    all_to_all x1, starting transfers between devices, spread(): lax.all_to_all(chunks, axes, split_axis=0, concat_axis=0, tiled=True, axi...  8.89 us
    ppermute x1, waiting for transfers between devices, shards(): far = lax.ppermute(own, 'y', [(2, 0), (1, 3)])  7.33 us
    pallas_call x6, Pallas kernels, call(): pl.pallas_call(kernel, in_specs=ins, out_specs=tuple((VMEM for _ in outs)...  6.15 us
    ppermute x1, starting transfers between devices, shards(): across = lax.ppermute(half, ('yh', 'y'), shift(8, 2))  5.48 us
    ppermute x1, waiting for transfers between devices, shards(): near = lax.ppermute(own, 'y', shift(4, 1))  4.6 us
  transfers between devices with their start and end apart: 11, of which 3 were waited for; matrix products, arithmetic and copies ran while one was open for 1% of the time, Pallas kernels for 1%

profile of v7, /device:TPU:448, one launch (start us, length us, event | category | flops | bytes accessed | tf_op | source)
XLA Modules:
  0.0 99.4 jit_solution(12860695559380564675)
XLA Ops:
  0.6 0.0 copy-start
  0.7 2.0 %shard_map.103 = bf16[16,64,384]{2,1,0:T(8,128)(2,1)} custom-call(bf16[64,1024]{1,0:T(8,128)(2,1)} %q_hbm.1, bf16[64,1024]{1,0:T(8,128)(2,1)} %k_hbm.1, bf16[64,1024]{1,0:T(8,128)(2,1)} %v_hbm.1), custom_call_target="tpu_custom_call" | custom-call | tf_op jit(solution)/shard_map/pallas_call | solution.py:231
  2.6 8.9 %all-to-all-start = ((bf16[16,64,384]{2,1,0:T(8,128)(2,1)}), bf16[16,64,384]{2,1,0:T(8,128)(2,1)S(1)}, u32[]{:S(2)}, u32[]{:S(2)}) async-start(bf16[16,64,384]{2,1,0:T(8,128)(2,1)} %shard_map.103), calls=%async_computation | async-start | bytes 1572864 | tf_op jit(solution)/shard_map/all_to_all | solution.py:223
  12.3 3.8 %collective-permute-start.2 = (bf16[144,1024]{1,0:T(8,128)(2,1)S(1)}, bf16[144,1024]{1,0:T(8,128)(2,1)S(1)}, u32[]{:S(2)}, u32[]{:S(2)}) collective-permute-start(bf16[144,1024]{1,0:T(8,128)(2,1)S(1)} %get-tuple-element.17.x0), channel_id=1, source_target_pairs={{12,0},{0,4},{4,8},{8,12},{13,1},{1,5},{5,9},{9,13},{14,2},{2,6},{... | collective-permute-start | bytes 884744 | tf_op jit(solution)/shard_map/ppermute | solution.py:257
  16.1 4.6 %collective-permute-start.1 = (bf16[144,1024]{1,0:T(8,128)(2,1)S(1)}, bf16[144,1024]{1,0:T(8,128)(2,1)S(1)}, u32[]{:S(2)}, u32[]{:S(2)}) collective-permute-start(bf16[144,1024]{1,0:T(8,128)(2,1)S(1)} %get-tuple-element.17.x0), channel_id=1, source_target_pairs={{8,0},{12,4},{0,8},{4,12},{9,1},{13,5},{1,9},{5,13},{10,2},{14,6},... | collective-permute-start | bytes 884744 | tf_op jit(solution)/shard_map/ppermute | solution.py:257
  20.7 3.4 %collective-permute-start = (bf16[144,1024]{1,0:T(8,128)(2,1)S(1)}, bf16[144,1024]{1,0:T(8,128)(2,1)S(1)}, u32[]{:S(2)}, u32[]{:S(2)}) collective-permute-start(bf16[144,1024]{1,0:T(8,128)(2,1)S(1)} %get-tuple-element.17.x0), channel_id=1, source_target_pairs={{4,0},{8,4},{12,8},{0,12},{5,1},{9,5},{13,9},{1,13},{6,2},{10,6},{... | collective-permute-start | bytes 884744 | tf_op jit(solution)/shard_map/ppermute | solution.py:257
  24.1 5.5 %collective-permute-start.4 = (bf16[32,1024]{1,0:T(8,128)(2,1)S(1)}, bf16[32,1024]{1,0:T(8,128)(2,1)S(1)}, u32[]{:S(2)}, u32[]{:S(2)}) collective-permute-start(bf16[32,1024]{1,0:T(8,128)(2,1)S(1)} %get-tuple-element.19), channel_id=1, source_target_pairs={{2,0},{3,1},{256,2},{257,3},{258,256},{259,257},{0,258},{1,259},{6... | collective-permute-start | bytes 196616 | tf_op jit(solution)/shard_map/ppermute | solution.py:255
  29.6 3.4 %collective-permute-start.3 = (bf16[64,1024]{1,0:T(8,128)(2,1)S(1)}, bf16[64,1024]{1,0:T(8,128)(2,1)S(1)}, u32[]{:S(2)}, u32[]{:S(2)}) collective-permute-start(bf16[64,1024]{1,0:T(8,128)(2,1)S(1)} %get-tuple-element.18), channel_id=1, source_target_pairs={{1,0},{275,16},{2,1},{16,17},{3,2},{17,18},{256,3},{18,19},{257,25... | collective-permute-start | bytes 393224 | tf_op jit(solution)/shard_map/ppermute | solution.py:254
  33.0 1.1 %gather_fusion = bf16[128]{0:T(256)(128)(2,1)S(1)} fusion(f32[50265]{0:T(1024)S(1)} %copy-done, s32[1024]{0:T(1024)S(1)} %pad_clamp_fusion), kind=kCustom, calls=%fused_computation | custom fusion | bytes 1024 | tf_op jit(solution)/shard_map/jit(_take)/gather | solution.py:261
  34.2 2.3 %collective-permute-done.3 = bf16[64,1024]{1,0:T(8,128)(2,1)S(1)} collective-permute-done((bf16[64,1024]{1,0:T(8,128)(2,1)S(1)}, bf16[64,1024]{1,0:T(8,128)(2,1)S(1)}, u32[]{:S(2)}, u32[]{:S(2)}) %collective-permute-start.3) | collective-permute-done | bytes 131104 | tf_op jit(solution)/shard_map/ppermute | solution.py:254
  36.5 1.9 %collective-permute-start.5 = (bf16[1024,384]{1,0:T(8,128)(2,1)S(1)}, bf16[1024,384]{1,0:T(8,128)(2,1)S(1)}, u32[]{:S(2)}, u32[]{:S(2)}) collective-permute-start(bf16[1024,384]{1,0:T(8,128)(2,1)S(1)} %bitcast.9), channel_id=1, source_target_pairs={{0,16},{16,0},{1,17},{17,1},{2,18},{18,2},{3,19},{19,3},{4,20},{20... | collective-permute-start | bytes 2359304 | tf_op jit(solution)/shard_map/ppermute | solution.py:264
  38.4 2.4 %collective-permute-start.6 = (bf16[96,1024]{1,0:T(8,128)(2,1)S(1)}, bf16[96,1024]{1,0:T(8,128)(2,1)S(1)}, u32[]{:S(2)}, u32[]{:S(2)}) collective-permute-start(bf16[96,1024]{1,0:T(8,128)(2,1)S(1)} %pad_maximum_fusion.mine_ref), channel_id=1, source_target_pairs={{0,16},{16,0},{1,17},{17,1},{2,18},{18,2},{3,19},{19,3},{4,20},{20... | collective-permute-start | bytes 589832 | tf_op jit(solution)/shard_map/ppermute | solution.py:265
  40.8 1.2 %shard_map.105.near_ref = bf16[512,128]{1,0:T(8,128)(2,1)S(1)} custom-call(bf16[144,1024]{1,0:T(8,128)(2,1)S(1)} %get-tuple-element.17.x0, bf16[144,1024]{1,0:T(8,128)(2,1)S(1)} %collective-permute-done.x1, bf16[144,1024]{1,0:T(8,128)(2,1)S(1)} %collective-permute-done.1.x2, bf16[144,1024]{1,0:T(8,128)(2,1)S(1)} %collective-permute-done.2.x3, ...), custom_call_target="tpu_custom_call" | custom-call | tf_op jit(solution)/shard_map/pallas_call | solution.py:185
  42.1 1.8 %shard_map.106 = bf16[4,128,1024]{2,1,0:T(8,128)(2,1)S(1)} custom-call(bf16[144,1024]{1,0:T(8,128)(2,1)S(1)} %get-tuple-element.17.x0, bf16[144,1024]{1,0:T(8,128)(2,1)S(1)} %collective-permute-done.x1, bf16[144,1024]{1,0:T(8,128)(2,1)S(1)} %collective-permute-done.1.x2, bf16[144,1024]{1,0:T(8,128)(2,1)S(1)} %collective-permute-done.2.x3, ...), custom_call_target="tpu_custom_call" | custom-call | tf_op jit(solution)/shard_map/pallas_call | solution.py:185
  43.9 18.1 %all_to_all.20.parts_ref = bf16[4,128,1024]{2,1,0:T(8,128)(2,1)S(1)} all-to-all(bf16[4,128,1024]{2,1,0:T(8,128)(2,1)S(1)} %shard_map.106), channel_id=1, replica_groups=mesh['yh'=2,'z'=8,'core'=2,'x'=4,'y'=4] {'x'}, dimensions={0} | all-to-all | bytes 2097152 | tf_op jit(solution)/shard_map/all_to_all | solution.py:276
  62.0 1.5 %shard_map.107 = (bf16[1,128,1024]{2,1,0:T(8,128)(2,1)}, bf16[144,1024]{1,0:T(8,128)(2,1)S(1)}, bf16[4,144,1024]{2,1,0:T(8,128)(2,1)}) custom-call(bf16[1,128]{1,0:T(2,128)(2,1)S(1)} %fusion.weight_ref, bf16[4,128,1024]{2,1,0:T(8,128)(2,1)S(1)} %all_to_all.20.parts_ref, bf16[1,128,1024]{2,1,0:T(8,128)(2,1)S(1)} %copy-done.1), custom_call_target="tpu_custom_call" | custom-call | tf_op jit(solution)/shard_map/pallas_call | solution.py:185
  63.6 3.5 %all-to-all-start.2 = ((bf16[4,144,1024]{2,1,0:T(8,128)(2,1)}), bf16[4,144,1024]{2,1,0:T(8,128)(2,1)S(1)}, u32[]{:S(2)}, u32[]{:S(2)}) async-start(bf16[4,144,1024]{2,1,0:T(8,128)(2,1)} %get-tuple-element.27), calls=%async_computation.2 | async-start | bytes 2359296 | tf_op jit(solution)/shard_map/all_to_all | solution.py:289
  67.1 1.3 %collective-permute-start.8 = (bf16[144,1024]{1,0:T(8,128)(2,1)S(1)}, bf16[144,1024]{1,0:T(8,128)(2,1)S(1)}, u32[]{:S(2)}, u32[]{:S(2)}) collective-permute-start(bf16[144,1024]{1,0:T(8,128)(2,1)S(1)} %get-tuple-element.28.own_ref), channel_id=1, source_target_pairs={{2,0},{1,3},{6,4},{5,7},{10,8},{9,11},{14,12},{13,15},{18,16},{17,... | collective-permute-start | bytes 884744 | tf_op jit(solution)/shard_map/ppermute | solution.py:288
  68.4 4.1 %collective-permute-start.7 = (bf16[144,1024]{1,0:T(8,128)(2,1)S(1)}, bf16[144,1024]{1,0:T(8,128)(2,1)S(1)}, u32[]{:S(2)}, u32[]{:S(2)}) collective-permute-start(bf16[144,1024]{1,0:T(8,128)(2,1)S(1)} %get-tuple-element.28.own_ref), channel_id=1, source_target_pairs={{1,0},{2,1},{3,2},{0,3},{5,4},{6,5},{7,6},{4,7},{9,8},{10,9},{11,1... | collective-permute-start | bytes 884744 | tf_op jit(solution)/shard_map/ppermute | solution.py:287
  72.5 7.3 %collective-permute-done.8.far_ref = bf16[144,1024]{1,0:T(8,128)(2,1)S(1)} collective-permute-done((bf16[144,1024]{1,0:T(8,128)(2,1)S(1)}, bf16[144,1024]{1,0:T(8,128)(2,1)S(1)}, u32[]{:S(2)}, u32[]{:S(2)}) %collective-permute-start.8) | collective-permute-done | bytes 294944 | tf_op jit(solution)/shard_map/ppermute | solution.py:288
  79.9 4.6 %collective-permute-done.7.near_ref = bf16[144,1024]{1,0:T(8,128)(2,1)S(1)} collective-permute-done((bf16[144,1024]{1,0:T(8,128)(2,1)S(1)}, bf16[144,1024]{1,0:T(8,128)(2,1)S(1)}, u32[]{:S(2)}, u32[]{:S(2)}) %collective-permute-start.7) | collective-permute-done | bytes 294944 | tf_op jit(solution)/shard_map/ppermute | solution.py:287
  84.5 0.9 shard_map.108
  85.4 13.3 %all_to_all.21.got_ref = f32[16,1,128]{2,1,0:T(1,128)S(1)} all-to-all(f32[16,1,128]{2,1,0:T(1,128)S(1)} %shard_map.108), channel_id=1, replica_groups=mesh['yh'=2,'z'=8,'core'=2,'x'=4,'y'=4] {'x','y'}, dimensions={0} | all-to-all | bytes 16384 | tf_op jit(solution)/shard_map/all_to_all | solution.py:293
  98.7 0.6 shard_map.109
  (21 shorter events, 0.1 us)
Async XLA Ops:
  0.6 32.4 %copy-start = (f32[50265]{0:T(1024)S(1)}, f32[50265]{0:T(1024)}, u32[]{:S(2)}) copy-start(f32[50265]{0:T(1024)} %param.11) | copy-start | bytes 603184
  0.6 11.6 %copy-start.2 = (bf16[64,1024]{1,0:T(8,128)(2,1)S(1)}, bf16[64,1024]{1,0:T(8,128)(2,1)}, u32[]{:S(2)}) copy-start(bf16[64,1024]{1,0:T(8,128)(2,1)} %own_ref.1) | copy-start | bytes 393220
  0.7 11.6 %copy-start.1 = (bf16[1,128,1024]{2,1,0:T(8,128)(2,1)S(1)}, bf16[1,128,1024]{2,1,0:T(8,128)(2,1)}, u32[]{:S(2)}) copy-start(bf16[1,128,1024]{2,1,0:T(8,128)(2,1)} %x_ref.3) | copy-start | bytes 786436
  2.6 30.3 %copy-start.3 = (s32[1,128]{1,0:T(1,128)S(1)}, s32[1,128]{1,0:T(1,128)}, u32[]{:S(2)}) copy-start(s32[1,128]{1,0:T(1,128)} %param.9) | copy-start | bytes 1540
  2.6 33.8 %all-to-all-start = ((bf16[16,64,384]{2,1,0:T(8,128)(2,1)}), bf16[16,64,384]{2,1,0:T(8,128)(2,1)S(1)}, u32[]{:S(2)}, u32[]{:S(2)}) async-start(bf16[16,64,384]{2,1,0:T(8,128)(2,1)} %shard_map.103), calls=%async_computation | async-start | bytes 1572864 | tf_op jit(solution)/shard_map/all_to_all | solution.py:223
  12.3 24.2 %collective-permute-start.2 = (bf16[144,1024]{1,0:T(8,128)(2,1)S(1)}, bf16[144,1024]{1,0:T(8,128)(2,1)S(1)}, u32[]{:S(2)}, u32[]{:S(2)}) collective-permute-start(bf16[144,1024]{1,0:T(8,128)(2,1)S(1)} %get-tuple-element.17.x0), channel_id=1, source_target_pairs={{12,0},{0,4},{4,8},{8,12},{13,1},{1,5},{5,9},{9,13},{14,2},{2,6},{... | collective-permute-start | bytes 884744 | tf_op jit(solution)/shard_map/ppermute | solution.py:257
  16.1 20.4 %collective-permute-start.1 = (bf16[144,1024]{1,0:T(8,128)(2,1)S(1)}, bf16[144,1024]{1,0:T(8,128)(2,1)S(1)}, u32[]{:S(2)}, u32[]{:S(2)}) collective-permute-start(bf16[144,1024]{1,0:T(8,128)(2,1)S(1)} %get-tuple-element.17.x0), channel_id=1, source_target_pairs={{8,0},{12,4},{0,8},{4,12},{9,1},{13,5},{1,9},{5,13},{10,2},{14,6},... | collective-permute-start | bytes 884744 | tf_op jit(solution)/shard_map/ppermute | solution.py:257
  20.7 15.8 %collective-permute-start = (bf16[144,1024]{1,0:T(8,128)(2,1)S(1)}, bf16[144,1024]{1,0:T(8,128)(2,1)S(1)}, u32[]{:S(2)}, u32[]{:S(2)}) collective-permute-start(bf16[144,1024]{1,0:T(8,128)(2,1)S(1)} %get-tuple-element.17.x0), channel_id=1, source_target_pairs={{4,0},{8,4},{12,8},{0,12},{5,1},{9,5},{13,9},{1,13},{6,2},{10,6},{... | collective-permute-start | bytes 884744 | tf_op jit(solution)/shard_map/ppermute | solution.py:257
  24.1 10.1 %collective-permute-start.4 = (bf16[32,1024]{1,0:T(8,128)(2,1)S(1)}, bf16[32,1024]{1,0:T(8,128)(2,1)S(1)}, u32[]{:S(2)}, u32[]{:S(2)}) collective-permute-start(bf16[32,1024]{1,0:T(8,128)(2,1)S(1)} %get-tuple-element.19), channel_id=1, source_target_pairs={{2,0},{3,1},{256,2},{257,3},{258,256},{259,257},{0,258},{1,259},{6... | collective-permute-start | bytes 196616 | tf_op jit(solution)/shard_map/ppermute | solution.py:255
  29.6 6.9 %collective-permute-start.3 = (bf16[64,1024]{1,0:T(8,128)(2,1)S(1)}, bf16[64,1024]{1,0:T(8,128)(2,1)S(1)}, u32[]{:S(2)}, u32[]{:S(2)}) collective-permute-start(bf16[64,1024]{1,0:T(8,128)(2,1)S(1)} %get-tuple-element.18), channel_id=1, source_target_pairs={{1,0},{275,16},{2,1},{16,17},{3,2},{17,18},{256,3},{18,19},{257,25... | collective-permute-start | bytes 393224 | tf_op jit(solution)/shard_map/ppermute | solution.py:254
  36.5 5.6 %collective-permute-start.5 = (bf16[1024,384]{1,0:T(8,128)(2,1)S(1)}, bf16[1024,384]{1,0:T(8,128)(2,1)S(1)}, u32[]{:S(2)}, u32[]{:S(2)}) collective-permute-start(bf16[1024,384]{1,0:T(8,128)(2,1)S(1)} %bitcast.9), channel_id=1, source_target_pairs={{0,16},{16,0},{1,17},{17,1},{2,18},{18,2},{3,19},{19,3},{4,20},{20... | collective-permute-start | bytes 2359304 | tf_op jit(solution)/shard_map/ppermute | solution.py:264
  38.4 3.6 %collective-permute-start.6 = (bf16[96,1024]{1,0:T(8,128)(2,1)S(1)}, bf16[96,1024]{1,0:T(8,128)(2,1)S(1)}, u32[]{:S(2)}, u32[]{:S(2)}) collective-permute-start(bf16[96,1024]{1,0:T(8,128)(2,1)S(1)} %pad_maximum_fusion.mine_ref), channel_id=1, source_target_pairs={{0,16},{16,0},{1,17},{17,1},{2,18},{18,2},{3,19},{19,3},{4,20},{20... | collective-permute-start | bytes 589832 | tf_op jit(solution)/shard_map/ppermute | solution.py:265
  63.6 20.9 %all-to-all-start.2 = ((bf16[4,144,1024]{2,1,0:T(8,128)(2,1)}), bf16[4,144,1024]{2,1,0:T(8,128)(2,1)S(1)}, u32[]{:S(2)}, u32[]{:S(2)}) async-start(bf16[4,144,1024]{2,1,0:T(8,128)(2,1)} %get-tuple-element.27), calls=%async_computation.2 | async-start | bytes 2359296 | tf_op jit(solution)/shard_map/all_to_all | solution.py:289
  67.1 12.8 %collective-permute-start.8 = (bf16[144,1024]{1,0:T(8,128)(2,1)S(1)}, bf16[144,1024]{1,0:T(8,128)(2,1)S(1)}, u32[]{:S(2)}, u32[]{:S(2)}) collective-permute-start(bf16[144,1024]{1,0:T(8,128)(2,1)S(1)} %get-tuple-element.28.own_ref), channel_id=1, source_target_pairs={{2,0},{1,3},{6,4},{5,7},{10,8},{9,11},{14,12},{13,15},{18,16},{17,... | collective-permute-start | bytes 884744 | tf_op jit(solution)/shard_map/ppermute | solution.py:288
  68.4 16.1 %collective-permute-start.7 = (bf16[144,1024]{1,0:T(8,128)(2,1)S(1)}, bf16[144,1024]{1,0:T(8,128)(2,1)S(1)}, u32[]{:S(2)}, u32[]{:S(2)}) collective-permute-start(bf16[144,1024]{1,0:T(8,128)(2,1)S(1)} %get-tuple-element.28.own_ref), channel_id=1, source_target_pairs={{1,0},{2,1},{3,2},{0,3},{5,4},{6,5},{7,6},{4,7},{9,8},{10,9},{11,1... | collective-permute-start | bytes 884744 | tf_op jit(solution)/shard_map/ppermute | solution.py:287
